TPU v7x, 32 devices: a whole 2x2x4 slice. The times are simulated.
32 devices in a mesh: fsdp: 8 (over y, x, core), tensor: 4 (over z).
Axes of the slice: x: 2, y: 2, z: 4, core: 2. Of those that a mesh axis runs over, the one named last changes fastest.
Arguments:
- pixels: bfloat16 [32768, 768], P(('fsdp', 'tensor')), may hold values from -6 to 6
- segment: int32 [32768], P('fsdp'), may hold values from -1 to 4, as said below
- band_group: int32 [32768], P(('fsdp', 'tensor')), may hold values from 0 to 3, as said below
- scaled_position: int32 [32768], P(('fsdp', 'tensor')), may hold values from 0 to 390, as said below
- patch_weight: bfloat16 [4, 768, 1024], P(None, None, ('fsdp', 'tensor')), may hold values from -0.21875 to 0.21875
- patch_bias: bfloat16 [4, 1024], P(None, ('fsdp', 'tensor')), may hold values from -3 to 3
- norm_gains: bfloat16 [2, 1024], P(None, ('fsdp', 'tensor')), may hold values from 0.5 to 1.5
- vector_biases: bfloat16 [4, 1024], P(None, ('fsdp', 'tensor')), may hold values from -2 to 2
- attention_weight: bfloat16 [3, 1024, 1024], P(None, 'fsdp', 'tensor'), may hold values from -0.1875 to 0.1875
- query_value_bias: bfloat16 [2, 1024], P(None, ('tensor', 'fsdp')), may hold values from -2 to 2
- merge_weight: bfloat16 [1024, 1024], P('tensor', 'fsdp'), may hold values from -0.5 to 0.5
- expand_weight: bfloat16 [1024, 4096], P('fsdp', 'tensor'), may hold values from -0.1875 to 0.1875
- expand_bias: bfloat16 [4096], P(('tensor', 'fsdp')), may hold values from -3 to 3
- contract_weight: bfloat16 [4096, 1024], P('tensor', 'fsdp'), may hold values from -0.09375 to 0.09375
- cotangent: bfloat16 [32768, 1024], P(('fsdp', 'tensor')), may hold values from -6 to 6
Outputs:
- block_output: float32 [32768, 1024], P(('fsdp', 'tensor'))
- pixel_grad: float32 [32768, 768], P(('fsdp', 'tensor'))
- patch_weight_grad: float32 [4, 768, 1024], P(None, None, ('fsdp', 'tensor'))
- patch_bias_grad: float32 [4, 1024], P(None, ('fsdp', 'tensor'))
- norm_gains_grad: float32 [2, 1024], P(None, ('fsdp', 'tensor'))
- vector_biases_grad: float32 [4, 1024], P(None, ('fsdp', 'tensor'))
- attention_weight_grad: float32 [3, 1024, 1024], P(None, 'fsdp', 'tensor')
- query_value_bias_grad: float32 [2, 1024], P(None, ('tensor', 'fsdp'))
- merge_weight_grad: float32 [1024, 1024], P('tensor', 'fsdp')
- expand_weight_grad: float32 [1024, 4096], P('fsdp', 'tensor')
- expand_bias_grad: float32 [4096], P(('tensor', 'fsdp'))
- contract_weight_grad: float32 [4096, 1024], P('tensor', 'fsdp')
Inputs may be any that keep to these rules, and one draw needn't show every extreme that they name: `segment`: rows of 1024 consecutive slots each hold whole items numbered 0, 1, ... from the row's start: a 13-band item fills 3 * 196 slots, an RGB item 196; -1 marks the padding after the row's last item. `band_group`: 0 on RGB items and padding; a 13-band item's three runs of 196 slots carry the groups 1, 2 and 3, one each, in some order. `scaled_position`: within each aligned block of 196 slots of an item, the slot's place in the run times a scale of 1 or 2 that is fixed for the item; 0 on padding.
All inputs are finite; a program needn't handle non-finite values.
Results may differ from a plain program's by a relative error of at most 0.019.
Values may be sent and summed in bfloat16 or wider, within the bound.
No kernel may reach another device: no remote copies, remote signals or barrier semaphores. Data moves between devices by JAX's collectives and lax.ppermute only.
A program may use at most 512 MiB of HBM per device.

v0:
```python
from functools import partial
import math

import jax
import jax.numpy as jnp
from jax import lax
from jax.sharding import PartitionSpec as P

D = 1024
HEAD_DIM = 64
GROUPS = 4
SLOTS = 1024


HIGHEST_PRECISION = lax.Precision.HIGHEST
EPSILON = 1e-06


def positions(index, model_width):
    half_width = model_width // 2
    rates = jnp.exp(jnp.arange(half_width).astype(jnp.float32) * (-math.log(10000.0) / half_width))
    angles = index.astype(jnp.float32)[:, None] * rates[None, :]
    return jnp.concatenate([jnp.sin(angles), jnp.cos(angles)], axis=1)


def product(left, right):
    return jnp.dot(left, right, preferred_element_type=jnp.float32)


def contract_rows(left, right):
    return lax.dot_general(
        left, right, (((0,), (0,)), ((), ())), preferred_element_type=jnp.float32
    )


def contract_cols(left, right):
    return lax.dot_general(
        left, right, (((1,), (1,)), ((), ())), preferred_element_type=jnp.float32
    )


def normalize(values):
    row_mean = jnp.mean(values, axis=-1, keepdims=True)
    centred = values - row_mean
    inv_scale = lax.rsqrt(jnp.mean(centred * centred, axis=-1, keepdims=True) + EPSILON)
    return (centred * inv_scale, inv_scale)


def normalize_back(grad_normed, normed, inv_scale):
    return inv_scale * (
        grad_normed
        - jnp.mean(grad_normed, axis=-1, keepdims=True)
        - normed * jnp.mean(grad_normed * normed, axis=-1, keepdims=True)
    )


def group_count(table):
    head_count = table.shape[1] // HEAD_DIM
    return head_count // math.gcd(head_count, 4)


def to_groups(table, groups):
    slot_count, width = table.shape
    return table.reshape(slot_count, groups, width // groups).transpose(1, 0, 2)


def from_groups(table):
    groups, slot_count, width = table.shape
    return table.transpose(1, 0, 2).reshape(slot_count, groups * width)


def masked_scores(query_rows, key_rows, segment):
    slot_count = query_rows.shape[0]
    head_count = query_rows.shape[1] // HEAD_DIM
    query_heads = query_rows.reshape(slot_count, head_count, HEAD_DIM)
    key_heads = key_rows.reshape(slot_count, head_count, HEAD_DIM)
    scores = jnp.einsum(
        "qhe,khe->hqk", query_heads, key_heads, preferred_element_type=jnp.float32
    ) * HEAD_DIM ** (-0.5)
    same_item = segment[:, None] == segment[None, :]
    return (jnp.where(same_item[None], scores, -1e30), query_heads, key_heads)


def attend(inputs):
    query_all, key_all, value_all, segment = inputs
    groups = group_count(query_all)

    def one_group(parts):
        query_rows, key_rows, value_rows = parts
        scores, query_heads, key_heads = masked_scores(query_rows, key_rows, segment)
        value_heads = value_rows.reshape(query_heads.shape)
        row_max = jnp.max(scores, axis=-1, keepdims=True)
        shifted = jnp.exp(scores - row_max)
        row_total = jnp.sum(shifted, axis=-1, keepdims=True)
        probabilities = (shifted / row_total).astype(jnp.bfloat16)
        attended = jnp.einsum(
            "hqk,khe->qhe", probabilities, value_heads, preferred_element_type=jnp.float32
        )
        return (
            attended.reshape(query_rows.shape).astype(jnp.bfloat16),
            (row_max + jnp.log(row_total))[:, :, 0],
        )

    attended, log_total = lax.map(
        one_group,
        (to_groups(query_all, groups), to_groups(key_all, groups), to_groups(value_all, groups)),
    )
    return (from_groups(attended), log_total.reshape(-1, log_total.shape[2]))


def attend_back(inputs):
    query_all, key_all, value_all, segment, log_all, grad_all = inputs
    groups = group_count(query_all)

    def one_group(parts):
        query_rows, key_rows, value_rows, log_total, grad_attended = parts
        scores, query_heads, key_heads = masked_scores(query_rows, key_rows, segment)
        value_heads = value_rows.reshape(query_heads.shape)
        weights_full = jnp.exp(scores - log_total[:, :, None])
        grad_heads = grad_attended.reshape(query_heads.shape)
        grad_value = jnp.einsum(
            "hqk,qhe->khe",
            weights_full.astype(jnp.bfloat16),
            grad_heads,
            preferred_element_type=jnp.float32,
        )
        grad_weights = jnp.einsum(
            "qhe,khe->hqk", grad_heads, value_heads, preferred_element_type=jnp.float32
        )
        grad_scores = (
            weights_full
            * (grad_weights - jnp.sum(weights_full * grad_weights, axis=-1, keepdims=True))
        ).astype(jnp.bfloat16)
        grad_query = jnp.einsum(
            "hqk,khe->qhe", grad_scores, key_heads, preferred_element_type=jnp.float32
        ) * HEAD_DIM ** (-0.5)
        grad_key = jnp.einsum(
            "hqk,qhe->khe", grad_scores, query_heads, preferred_element_type=jnp.float32
        ) * HEAD_DIM ** (-0.5)
        row_shape = query_rows.shape
        return (
            grad_query.reshape(row_shape).astype(jnp.bfloat16),
            grad_key.reshape(row_shape).astype(jnp.bfloat16),
            grad_value.reshape(row_shape).astype(jnp.bfloat16),
        )

    log_groups = log_all.reshape(groups, log_all.shape[0] // groups, log_all.shape[1])
    grad_query, grad_key, grad_value = lax.map(
        one_group,
        (
            to_groups(query_all, groups),
            to_groups(key_all, groups),
            to_groups(value_all, groups),
            log_groups,
            to_groups(grad_all, groups),
        ),
    )
    return (from_groups(grad_query), from_groups(grad_key), from_groups(grad_value))


def load_weights(
    attention_weight, query_value_bias, merge_weight, expand_weight, expand_bias, contract_weight
):
    shards = (
        lax.all_gather(attention_weight, "fsdp", axis=1, tiled=True),
        lax.all_gather(query_value_bias, "fsdp", axis=1, tiled=True),
        lax.all_gather(merge_weight, "fsdp", axis=1, tiled=True),
        lax.all_gather(expand_weight, "fsdp", axis=0, tiled=True),
        lax.all_gather(expand_bias, "fsdp", axis=0, tiled=True),
        lax.all_gather(contract_weight, "fsdp", axis=1, tiled=True),
    )
    return shards


def body(
    pixels,
    segment,
    band_group,
    scaled_position,
    patch_weight,
    patch_bias,
    norm_gains,
    vector_biases,
    attention_weight,
    query_value_bias,
    merge_weight,
    expand_weight,
    expand_bias,
    contract_weight,
    cotangent,
):
    local_rows = pixels.shape[0]
    patch_full, patch_bias_full, gains_full, biases_full = (
        lax.all_gather(patch_weight, ("fsdp", "tensor"), axis=2, tiled=True),
        lax.all_gather(patch_bias, ("fsdp", "tensor"), axis=1, tiled=True),
        lax.all_gather(norm_gains, ("fsdp", "tensor"), axis=1, tiled=True),
        lax.all_gather(vector_biases, ("fsdp", "tensor"), axis=1, tiled=True),
    )
    gain_rows = gains_full.astype(jnp.float32)
    bias_rows = biases_full.astype(jnp.float32)
    attention_full, query_value_full, merge_full, expand_full, expand_bias_full, contract_full = (
        load_weights(
            attention_weight,
            query_value_bias,
            merge_weight,
            expand_weight,
            expand_bias,
            contract_weight,
        )
    )
    query_value_float = query_value_full.astype(jnp.float32)
    expand_bias_float = expand_bias_full.astype(jnp.float32)
    onehot = (band_group[:, None] == jnp.arange(GROUPS)[None, :]).astype(jnp.float32)
    embedded = onehot[:, 0:1] * product(pixels, patch_full[0])
    for group_id in range(1, GROUPS):
        embedded = embedded + onehot[:, group_id : group_id + 1] * product(
            pixels, patch_full[group_id]
        )
    stream_zero = (
        embedded
        + jnp.dot(onehot, patch_bias_full.astype(jnp.float32), precision=HIGHEST_PRECISION)
        + positions(scaled_position, D)
    )
    normed_one, scale_one = normalize(stream_zero)
    input_one = (normed_one * gain_rows[0] + bias_rows[0]).astype(jnp.bfloat16)
    rows_one = lax.all_gather(input_one, "tensor", axis=0, tiled=True)
    query_rows = (product(rows_one, attention_full[0]) + query_value_float[0]).astype(jnp.bfloat16)
    key_rows = product(rows_one, attention_full[1]).astype(jnp.bfloat16)
    value_rows = (product(rows_one, attention_full[2]) + query_value_float[1]).astype(jnp.bfloat16)
    row_count = rows_one.shape[0] // SLOTS

    def by_row(table):
        return table.reshape((row_count, SLOTS) + table.shape[1:])

    attended, log_total = lax.map(
        attend, (by_row(query_rows), by_row(key_rows), by_row(value_rows), by_row(segment))
    )
    attended = attended.reshape(rows_one.shape[0], -1)
    branch_one = lax.psum_scatter(
        product(attended, merge_full).astype(jnp.bfloat16),
        "tensor",
        scatter_dimension=0,
        tiled=True,
    ).astype(jnp.float32)
    stream_one = stream_zero + branch_one + bias_rows[1]
    normed_two, scale_two = normalize(stream_one)
    input_two = (normed_two * gain_rows[1] + bias_rows[2]).astype(jnp.bfloat16)
    rows_two = lax.all_gather(input_two, "tensor", axis=0, tiled=True)
    hidden_pre = product(rows_two, expand_full) + expand_bias_float
    gelu_value, gelu_pull = jax.vjp(partial(jax.nn.gelu, approximate=False), hidden_pre)
    activated = gelu_value.astype(jnp.bfloat16)
    branch_two = lax.psum_scatter(
        product(
            lax.slice_in_dim(activated, 0, local_rows * lax.axis_size("tensor"), axis=0),
            contract_full,
        ).astype(jnp.bfloat16),
        "tensor",
        scatter_dimension=0,
        tiled=True,
    ).astype(jnp.float32)
    block_output = stream_one + branch_two + bias_rows[3]
    attention_full, query_value_full, merge_full, expand_full, expand_bias_full, contract_full = (
        load_weights(
            attention_weight,
            query_value_bias,
            merge_weight,
            expand_weight,
            expand_bias,
            contract_weight,
        )
    )
    grad_top = cotangent.astype(jnp.float32)
    grad_bias_last = jnp.sum(grad_top, axis=0)
    rows_grad = lax.all_gather(cotangent, "tensor", axis=0, tiled=True)
    grad_contract = contract_rows(activated, rows_grad)
    grad_active = contract_cols(rows_grad, contract_full)
    grad_hidden = gelu_pull(grad_active)[0].astype(jnp.bfloat16)
    grad_expand_bias = jnp.sum(grad_hidden, axis=0, dtype=jnp.float32)
    grad_expand = contract_rows(rows_two, grad_hidden)
    grad_two = lax.psum_scatter(
        contract_cols(grad_hidden, expand_full).astype(jnp.bfloat16),
        "tensor",
        scatter_dimension=0,
        tiled=True,
    ).astype(jnp.float32)
    grad_gain_two = jnp.sum(grad_two * normed_two, axis=0)
    grad_bias_two = jnp.sum(grad_two, axis=0)
    grad_stream_one = grad_top + normalize_back(grad_two * gain_rows[1], normed_two, scale_two)
    grad_bias_one = jnp.sum(grad_stream_one, axis=0)
    grad_branch = grad_stream_one.astype(jnp.bfloat16)
    rows_branch = lax.all_gather(grad_branch, "tensor", axis=0, tiled=True)
    grad_merge = contract_rows(attended, rows_branch)
    grad_attended = contract_cols(rows_branch, merge_full).astype(jnp.bfloat16)
    grad_query, grad_key, grad_value = lax.map(
        attend_back,
        (
            by_row(query_rows),
            by_row(key_rows),
            by_row(value_rows),
            by_row(segment),
            log_total,
            by_row(grad_attended),
        ),
    )
    grad_query = grad_query.reshape(rows_one.shape[0], -1)
    grad_key = grad_key.reshape(rows_one.shape[0], -1)
    grad_value = grad_value.reshape(rows_one.shape[0], -1)
    grad_attention = jnp.stack(
        [
            contract_rows(rows_one, grad_query),
            contract_rows(rows_one, grad_key),
            contract_rows(rows_one, grad_value),
        ]
    )
    grad_query_value = jnp.stack(
        [
            jnp.sum(grad_query, axis=0, dtype=jnp.float32),
            jnp.sum(grad_value, axis=0, dtype=jnp.float32),
        ]
    )
    total = contract_cols(grad_query, attention_full[0])
    total = total + contract_cols(grad_key, attention_full[1])
    grad_one = lax.psum_scatter(
        (total + contract_cols(grad_value, attention_full[2])).astype(jnp.bfloat16),
        "tensor",
        scatter_dimension=0,
        tiled=True,
    ).astype(jnp.float32)
    grad_gain_one = jnp.sum(grad_one * normed_one, axis=0)
    grad_bias_zero = jnp.sum(grad_one, axis=0)
    grad_stream_zero = grad_stream_one + normalize_back(
        grad_one * gain_rows[0], normed_one, scale_one
    )
    grad_patch_bias = jnp.dot(onehot.T, grad_stream_zero, precision=HIGHEST_PRECISION)
    grad_embed = grad_stream_zero.astype(jnp.bfloat16)
    grad_patch = jnp.stack(
        [
            contract_rows(
                pixels * onehot[:, group_id : group_id + 1].astype(jnp.bfloat16), grad_embed
            )
            for group_id in range(GROUPS)
        ]
    )
    pixel_grad = onehot[:, 0:1] * contract_cols(grad_embed, patch_full[0])
    for group_id in range(1, GROUPS):
        pixel_grad = pixel_grad + onehot[:, group_id : group_id + 1] * contract_cols(
            grad_embed, patch_full[group_id]
        )
    grad_gains = jnp.stack([grad_gain_one, grad_gain_two])
    grad_biases = jnp.stack([grad_bias_zero, grad_bias_one, grad_bias_two, grad_bias_last])
    summed = (
        lax.psum_scatter(
            grad_attention.astype(jnp.bfloat16), "fsdp", scatter_dimension=1, tiled=True
        ).astype(jnp.float32),
        lax.psum_scatter(
            grad_query_value.astype(jnp.bfloat16), "fsdp", scatter_dimension=1, tiled=True
        ).astype(jnp.float32),
        lax.psum_scatter(
            grad_merge.astype(jnp.bfloat16), "fsdp", scatter_dimension=1, tiled=True
        ).astype(jnp.float32),
        lax.psum_scatter(
            grad_expand.astype(jnp.bfloat16), "fsdp", scatter_dimension=0, tiled=True
        ).astype(jnp.float32),
        lax.psum_scatter(
            grad_expand_bias.astype(jnp.bfloat16), "fsdp", scatter_dimension=0, tiled=True
        ).astype(jnp.float32),
        lax.psum_scatter(
            grad_contract.astype(jnp.bfloat16), "fsdp", scatter_dimension=1, tiled=True
        ).astype(jnp.float32),
    )
    small_sums = (
        lax.psum_scatter(grad_patch, ("fsdp", "tensor"), scatter_dimension=2, tiled=True),
        lax.psum_scatter(grad_patch_bias, ("fsdp", "tensor"), scatter_dimension=1, tiled=True),
        lax.psum_scatter(grad_gains, ("fsdp", "tensor"), scatter_dimension=1, tiled=True),
        lax.psum_scatter(grad_biases, ("fsdp", "tensor"), scatter_dimension=1, tiled=True),
    )
    return (
        block_output,
        pixel_grad,
        small_sums[0],
        small_sums[1],
        small_sums[2],
        small_sums[3],
        summed[0],
        summed[1],
        summed[2],
        summed[3],
        summed[4],
        summed[5],
    )


def solution(mesh):
    placed = (
        P(("fsdp", "tensor"), None),
        P("fsdp"),
        P(("fsdp", "tensor")),
        P(("fsdp", "tensor")),
        P(None, None, ("fsdp", "tensor")),
        P(None, ("fsdp", "tensor")),
        P(None, ("fsdp", "tensor")),
        P(None, ("fsdp", "tensor")),
        P(None, "fsdp", "tensor"),
        P(None, ("tensor", "fsdp")),
        P("tensor", "fsdp"),
        P("fsdp", "tensor"),
        P(("tensor", "fsdp")),
        P("tensor", "fsdp"),
        P(("fsdp", "tensor"), None),
    )
    return jax.shard_map(
        body,
        mesh=mesh,
        in_specs=placed,
        out_specs=(
            P(("fsdp", "tensor"), None),
            P(("fsdp", "tensor"), None),
            P(None, None, ("fsdp", "tensor")),
            P(None, ("fsdp", "tensor")),
            P(None, ("fsdp", "tensor")),
            P(None, ("fsdp", "tensor")),
            P(None, "fsdp", "tensor"),
            P(None, ("tensor", "fsdp")),
            P("tensor", "fsdp"),
            P("fsdp", "tensor"),
            P(("tensor", "fsdp")),
            P("tensor", "fsdp"),
        ),
        check_vma=False,
    )
```

profile of v0, /device:TPU:8, one launch (start us, length us, event | category | flops | bytes accessed | tf_op | source)
XLA Modules:
  0.0 2758.3 jit_solution(7685060615061897925)
XLA Ops:
  10.8 63.8 %all-gather.1 = bf16[32,32,2]{1,2,0:T(2,128)(2,1)S(1)} all-gather(bf16[1,32,2]{1,2,0:T(2,128)(2,1)} %bitcast.315), channel_id=1, replica_groups=mesh['fsdp'=8,'tensor'=4] {'fsdp','tensor'}, dimensions={0}, use_global_device_ids=true | all-gather | bytes 4224 | tf_op jit(solution)/shard_map/all_gather | solution.py:196
  75.2 69.1 %all-gather = bf16[32,32,4]{1,2,0:T(4,128)(2,1)S(1)} all-gather(bf16[1,32,4]{1,2,0:T(4,128)(2,1)} %bitcast.311), channel_id=1, replica_groups=mesh['fsdp'=8,'tensor'=4] {'fsdp','tensor'}, dimensions={0}, use_global_device_ids=true | all-gather | bytes 8448 | tf_op jit(solution)/shard_map/all_gather | solution.py:195
  144.4 63.7 %all-gather.2 = bf16[32,32,4]{1,2,0:T(4,128)(2,1)S(1)} all-gather(bf16[1,32,4]{1,2,0:T(4,128)(2,1)} %bitcast.312), channel_id=1, replica_groups=mesh['fsdp'=8,'tensor'=4] {'fsdp','tensor'}, dimensions={0}, use_global_device_ids=true | all-gather | bytes 8448 | tf_op jit(solution)/shard_map/all_gather | solution.py:197
  253.4 124.8 %all-gather.16.cloned.1.call-done = bf16[4096,1024]{0,1:T(8,128)(2,1)} async-done(((bf16[1024,1024]{0,1:T(8,128)(2,1)}), bf16[4096,1024]{0,1:T(8,128)(2,1)}) %all-gather.16.cloned.1.call-update) | async-done | bytes 8388624 | tf_op jit(solution)/shard_map/all_gather | solution.py:226
  412.9 69.0 %while.10 = (s32[]{:T(128)}, bf16[4,1024,256]{2,1,0:T(8,128)(2,1)}, f32[4,4,1024]{2,1,0:T(4,128)}, bf16[4,1024,256]{1,2,0:T(8,128)(2,1)}, s32[4,1024]{1,0:T(4,12...) while((s32[]{:T(128)}, bf16[4,1024,256]{2,1,0:T(8,128)(2,1)}, ...), condition=%wide.region_5.6_spmd, body=%wide.region_2.5_spmd.sunk | while | flops 1125380096 | bytes 62009456 | solution.py:235
  490.7 144.9 %reduce-scatter.25.cloned.1.call-done = bf16[1024,1024]{0,1:T(8,128)(2,1)} async-done(((bf16[4096,1024]{0,1:T(8,128)(2,1)}), bf16[1024,1024]{0,1:T(8,128)(2,1)}) %reduce-scatter.25.cloned.1.call-update) | async-done | bytes 2097168 | tf_op jit(solution)/shard_map/reduce_scatter | solution.py:239
  653.3 12.9 all-gather.22.cloned.1.call-done
  666.3 148.1 %all-gather.20.cloned.1.call-done = bf16[4096,1024]{0,1:T(8,128)(2,1)} async-done(((bf16[1024,1024]{0,1:T(8,128)(2,1)}), bf16[4096,1024]{0,1:T(8,128)(2,1)}) %all-gather.20.cloned.1.call-update) | async-done | bytes 8388624 | tf_op jit(solution)/shard_map/all_gather | solution.py:248
  814.4 16.1 fusion.71
  830.5 15.1 all-gather.24.cloned.1.call-done
  845.6 148.3 %all-gather.26.cloned.1.call-done = bf16[4096,1024]{1,0:T(8,128)(2,1)} async-done(((bf16[1024,1024]{1,0:T(8,128)(2,1)}), bf16[4096,1024]{1,0:T(8,128)(2,1)}) %all-gather.26.cloned.1.call-update) | async-done | bytes 8388624 | tf_op jit(solution)/shard_map/all_gather | solution.py:274
  993.9 52.3 %fusion.59 = (bf16[1024]{0:T(1024)(128)(2,1)}, bf16[4096,1024]{1,0:T(8,128)(2,1)S(1)}, f32[4096,1024]{1,0:T(8,128)}) fusion(f32[4096,1024]{1,0:T(8,128)} %fusion.71, f32[1024]{0:T(1024)S(1)} %bitcast.307, bf16[4096,1024]{1,0:T(8,128)(2,1)} %all-gather.26.cloned.1.call-done, bf16[1024,1024]{1,0:T(8,128)(2,1)} %all-gather.24.cloned.1.call-done), kind=kOutput, calls=%fused_computation.163 | convolution fusion | flops 8900312064 | bytes 52434944 | tf_op jit(solution)/shard_map/dot_general | solution.py:37
  1060.8 12.3 multiply_convert_fusion.1
  1076.4 13.0 convolution_convert_fusion.1
  1093.6 112.6 %reduce-scatter.29.cloned.1.call-done = bf16[1024,1024]{0,1:T(8,128)(2,1)} async-done(((bf16[4096,1024]{0,1:T(8,128)(2,1)}), bf16[1024,1024]{0,1:T(8,128)(2,1)}) %reduce-scatter.29.cloned.1.call-update) | async-done | bytes 2097168 | tf_op jit(solution)/shard_map/reduce_scatter | solution.py:280
  1210.9 142.8 %reduce-scatter.27.cloned.1.call-done = bf16[1024,1024]{0,1:T(8,128)(2,1)} async-done(((bf16[4096,1024]{0,1:T(8,128)(2,1)}), bf16[1024,1024]{0,1:T(8,128)(2,1)}) %reduce-scatter.27.cloned.1.call-update) | async-done | bytes 2097168 | tf_op jit(solution)/shard_map/reduce_scatter | solution.py:252
  1364.5 147.8 %all-gather.28.cloned.1.call-done = bf16[4096,1024]{0,1:T(8,128)(2,1)} async-done(((bf16[1024,1024]{0,1:T(8,128)(2,1)}), bf16[4096,1024]{0,1:T(8,128)(2,1)}) %all-gather.28.cloned.1.call-update) | async-done | bytes 8388624 | tf_op jit(solution)/shard_map/all_gather | solution.py:291
  1521.0 199.2 %while.27 = (s32[]{:T(128)}, bf16[4,1024,256]{1,2,0:T(8,128)(2,1)}, bf16[4,1024,256]{2,1,0:T(8,128)(2,1)}, bf16[4,1024,256]{1,2,0:T(8,128)(2,1)}, bf16[4,1024,25...) while((s32[]{:T(128)}, bf16[4,1024,256]{1,2,0:T(8,128)(2,1)}, ...), condition=%wide.region_15.16_spmd, body=%wide.region_13.15_spmd.sunk | while | flops 2724458496 | bytes 178352336 | solution.py:294
  1746.9 15.5 add_convert_fusion
  1762.4 13.8 convolution_convert_fusion.5
  1778.9 15.1 convolution_convert_fusion.6
  1822.2 85.6 %reduce-scatter.31.cloned.1.call-done = bf16[1024,1024]{0,1:T(8,128)(2,1)} async-done(((bf16[4096,1024]{0,1:T(8,128)(2,1)}), bf16[1024,1024]{0,1:T(8,128)(2,1)}) %reduce-scatter.31.cloned.1.call-update) | async-done | bytes 2097168 | tf_op jit(solution)/shard_map/reduce_scatter | solution.py:323
  1951.6 14.9 copy.130
  1968.3 13.7 all-reduce.1
  1984.6 13.6 reduce-scatter.35.cloned.1.call-done
  2005.3 29.5 %reduce-scatter.43.cloned.1.call-done = bf16[32,2]{1,0:T(8,128)(2,1)} async-done(((bf16[256,2]{1,0:T(8,128)(2,1)}), bf16[32,2]{1,0:T(8,128)(2,1)}) %reduce-scatter.43.cloned.1.call-update) | async-done | bytes 144
  2036.2 36.1 %reduce-scatter.45.cloned.1.call-done = bf16[128,256]{1,0:T(8,128)(2,1)} async-done(((bf16[1024,256]{1,0:T(8,128)(2,1)}), bf16[128,256]{1,0:T(8,128)(2,1)}) %reduce-scatter.45.cloned.1.call-update) | async-done | bytes 65552
  2073.9 40.0 %reduce-scatter.33.cloned.1.call-done = bf16[3,128,256]{2,1,0:T(8,128)(2,1)} async-done(((bf16[3,1024,256]{2,1,0:T(8,128)(2,1)}), bf16[3,128,256]{2,1,0:T(8,128)(2,1)}) %reduce-scatter.33.cloned.1.call-update) | async-done | bytes 196624 | tf_op jit(solution)/shard_map/reduce_scatter | solution.py:352
  2128.5 117.6 %reduce-scatter.39.cloned.1.call-done = f32[32,2]{1,0:T(8,128)} async-done(((f32[1024,2]{1,0:T(8,128)}), f32[32,2]{1,0:T(8,128)}) %reduce-scatter.39.cloned.1.call-update) | async-done | bytes 272
  2247.5 131.5 %reduce-scatter.37.cloned.1.call-done = f32[32,4]{1,0:T(8,128)} async-done(((f32[1024,4]{1,0:T(8,128)}), f32[32,4]{1,0:T(8,128)}) %reduce-scatter.37.cloned.1.call-update) | async-done | bytes 528
  2380.4 131.4 %reduce-scatter.41.cloned.1.call-done = f32[32,4]{1,0:T(8,128)} async-done(((f32[1024,4]{1,0:T(8,128)}), f32[32,4]{1,0:T(8,128)}) %reduce-scatter.41.cloned.1.call-update) | async-done | bytes 528
  2513.2 236.2 %all-reduce.4.cloned.1.call-done = f32[4,768,1024]{1,0,2:T(4,128)} async-done(((f32[4,768,1024]{1,0,2:T(4,128)}), f32[4,768,1024]{1,0,2:T(4,128)}) %all-reduce.4.cloned.1.call-update) | async-done | bytes 12582928
  (397 shorter events, 559.3 us)
Async XLA Ops:
  7.2 210.4 %all-gather.14.cloned.1.call-start = ((), (), s32[]{:S(2)}) async-start(), calls=%async_computation.12 | async-start | bytes 6488064 | tf_op jit(solution)/shard_map/all_gather | solution.py:194
  7.9 245.5 %all-gather.18.cloned.1.call-start = ((), (), s32[]{:S(2)}) async-start(), calls=%async_computation.14 | async-start | bytes 1769472 | tf_op jit(solution)/shard_map/all_gather | solution.py:165
  8.7 369.6 %all-gather.16.cloned.1.call-start = ((), (), s32[]{:S(2)}) async-start(), calls=%async_computation.13 | async-start | bytes 10485760 | tf_op jit(solution)/shard_map/all_gather | solution.py:226
  10.7 216.5 %copy-start.32 = (f32[1024,1]{0,1:T(1,128)}, f32[1024,1]{0,1:T(1,128)S(1)}, u32[]{:S(2)}) copy-start(f32[1024,1]{0,1:T(1,128)S(1)} %get-tuple-element.345) | copy-start | bytes 12292
  10.7 216.5 %copy-start.34 = (f32[1024,1]{0,1:T(1,128)}, f32[1024,1]{0,1:T(1,128)S(1)}, u32[]{:S(2)}) copy-start(f32[1024,1]{0,1:T(1,128)S(1)} %get-tuple-element.346) | copy-start | bytes 12292
  10.7 216.5 %copy-start.36 = (f32[1024,1]{0,1:T(1,128)}, f32[1024,1]{0,1:T(1,128)S(1)}, u32[]{:S(2)}) copy-start(f32[1024,1]{0,1:T(1,128)S(1)} %get-tuple-element.347) | copy-start | bytes 12292
  10.8 216.5 %copy-start.38 = (f32[1024,1]{0,1:T(1,128)}, f32[1024,1]{0,1:T(1,128)S(1)}, u32[]{:S(2)}) copy-start(f32[1024,1]{0,1:T(1,128)S(1)} %get-tuple-element.348) | copy-start | bytes 12292
  75.2 155.2 %copy-start.30 = (f32[1,1024]{1,0:T(1,128)}, f32[1,1024]{1,0:T(1,128)S(1)}, u32[]{:S(2)}) copy-start(f32[1,1024]{1,0:T(1,128)S(1)} %get-tuple-element.350) | copy-start | bytes 12292
  234.0 401.6 %reduce-scatter.25.cloned.1.call-start = ((), (), s32[]{:S(2)}) async-start(), calls=%async_computation.15 | async-start | bytes 10485760 | tf_op jit(solution)/shard_map/reduce_scatter | solution.py:239
  490.0 145.5 %copy-start.46 = (f32[1,1024]{1,0:T(1,128)S(1)}, f32[1,1024]{1,0:T(1,128)}, u32[]{:S(2)}) copy-start(f32[1,1024]{1,0:T(1,128)} %get-tuple-element.343) | copy-start | bytes 12292
  490.0 176.2 %all-gather.22.cloned.1.call-start = ((), (), s32[]{:S(2)}) async-start(), calls=%async_computation.17 | async-start | bytes 2359296 | tf_op jit(solution)/shard_map/all_gather | solution.py:168
  490.6 323.7 %all-gather.20.cloned.1.call-start = ((), (), s32[]{:S(2)}) async-start(), calls=%async_computation.16 | async-start | bytes 10485760 | tf_op jit(solution)/shard_map/all_gather | solution.py:248
  643.0 202.6 %all-gather.24.cloned.1.call-start = ((), (), s32[]{:S(2)}) async-start(), calls=%async_computation.18 | async-start | bytes 2359296 | tf_op jit(solution)/shard_map/all_gather | solution.py:170
  643.8 350.1 %all-gather.26.cloned.1.call-start = ((), (), s32[]{:S(2)}) async-start(), calls=%async_computation.20 | async-start | bytes 10485760 | tf_op jit(solution)/shard_map/all_gather | solution.py:274
  644.5 561.7 %reduce-scatter.29.cloned.1.call-start = ((), (), s32[]{:S(2)}) async-start(), calls=%async_computation.21 | async-start | bytes 10485760 | tf_op jit(solution)/shard_map/reduce_scatter | solution.py:280
  1060.7 293.0 %reduce-scatter.27.cloned.1.call-start = ((), (), s32[]{:S(2)}) async-start(), calls=%async_computation.19 | async-start | bytes 10485760 | tf_op jit(solution)/shard_map/reduce_scatter | solution.py:252
  1089.4 116.8 %copy-start.20 = (f32[1024]{0:T(1024)S(1)}, f32[1024]{0:T(1024)}, u32[]{:S(2)}) copy-start(f32[1024]{0:T(1024)} %copy-done.19) | copy-start | bytes 12292
  1089.5 116.8 %copy-start.25 = (f32[1024]{0:T(1024)S(1)}, f32[1024]{0:T(1024)}, u32[]{:S(2)}) copy-start(f32[1024]{0:T(1024)} %copy-done.24) | copy-start | bytes 12292
  1089.5 422.8 %all-gather.28.cloned.1.call-start = ((), (), s32[]{:S(2)}) async-start(), calls=%async_computation.22 | async-start | bytes 10485760 | tf_op jit(solution)/shard_map/all_gather | solution.py:291
  1093.6 260.1 %copy-start.44 = (f32[1,1024]{1,0:T(1,128)S(1)}, f32[1,1024]{1,0:T(1,128)}, u32[]{:S(2)}) copy-start(f32[1,1024]{1,0:T(1,128)} %get-tuple-element.341) | copy-start | bytes 12292
  1206.2 147.4 %copy-start.10 = (bf16[1024,1024]{0,1:T(8,128)(2,1)S(1)}, bf16[1024,1024]{0,1:T(8,128)(2,1)}, u32[]{:S(2)}) copy-start(bf16[1024,1024]{0,1:T(8,128)(2,1)} %reduce-scatter.29.cloned.1.call-done) | copy-start | bytes 6291460
  1362.7 149.6 %copy-start.15 = (bf16[256,1024]{1,0:T(8,128)(2,1)S(1)}, bf16[256,1024]{1,0:T(8,128)(2,1)}, u32[]{:S(2)}) copy-start(bf16[256,1024]{1,0:T(8,128)(2,1)} %all_gather.53) | copy-start | bytes 1572868
  1364.4 543.5 %reduce-scatter.31.cloned.1.call-start = ((), (), s32[]{:S(2)}) async-start(), calls=%async_computation.23 | async-start | bytes 10485760 | tf_op jit(solution)/shard_map/reduce_scatter | solution.py:323
  1762.4 220.2 %reduce-scatter.47.cloned.1.call-start = ((), (), s32[]{:S(2)}) async-start(), calls=%async_computation.31 | async-start | bytes 2359296
  1778.8 219.4 %reduce-scatter.35.cloned.1.call-start = ((), (), s32[]{:S(2)}) async-start(), calls=%async_computation.25 | async-start | bytes 2359296 | tf_op jit(solution)/shard_map/reduce_scatter | solution.py:361
  1794.0 240.9 %reduce-scatter.43.cloned.1.call-start = ((), (), s32[]{:S(2)}) async-start(), calls=%async_computation.29 | async-start | bytes 73728
  1798.9 273.3 %reduce-scatter.45.cloned.1.call-start = ((), (), s32[]{:S(2)}) async-start(), calls=%async_computation.30 | async-start | bytes 589824
  1805.8 308.1 %reduce-scatter.33.cloned.1.call-start = ((), (), s32[]{:S(2)}) async-start(), calls=%async_computation.24 | async-start | bytes 1769472 | tf_op jit(solution)/shard_map/reduce_scatter | solution.py:352
  1822.0 424.1 %reduce-scatter.39.cloned.1.call-start = ((), (), s32[]{:S(2)}) async-start(), calls=%async_computation.27 | async-start | bytes 540672
  1934.4 444.7 %reduce-scatter.37.cloned.1.call-start = ((), (), s32[]{:S(2)}) async-start(), calls=%async_computation.26 | async-start | bytes 540672
  1939.4 572.5 %reduce-scatter.41.cloned.1.call-start = ((), (), s32[]{:S(2)}) async-start(), calls=%async_computation.28 | async-start | bytes 540672
  1940.7 808.7 %all-reduce.4.cloned.1.call-start = ((), (), s32[]{:S(2)}) async-start(), calls=%async_computation.32 | async-start | bytes 25165824
  (57 other events, 795.4 us)
Sparse Core Ops, SparseCore 0:
  10.9 70.8 all-gather.13
  83.7 24.1 all-gather.17
  234.1 144.1 all-gather.15
  490.2 145.3 reduce-scatter.24
  637.3 28.9 all-gather.21
  667.7 146.6 all-gather.19
  816.2 29.3 all-gather.23
  847.2 146.6 all-gather.25
  1060.8 145.3 reduce-scatter.28
  1208.4 145.1 reduce-scatter.26
  1364.5 147.6 all-gather.27
  1762.5 145.3 reduce-scatter.30
  1911.2 42.2 reduce-scatter.46
  1957.0 41.2 reduce-scatter.34
  2001.6 33.1 reduce-scatter.42
  2038.1 34.1 reduce-scatter.44
  2075.4 38.4 reduce-scatter.32
  2116.0 130.0 reduce-scatter.38
  2248.5 130.5 reduce-scatter.36
  2381.1 130.6 reduce-scatter.40
  2518.9 230.4 all-reduce.3
where the time goes:
time: 2770 us; the launch traced here: 2760 us
  waiting for transfers between devices  1820 us (66%)
  matrix products  401 us (14%)
  blocking collectives  238 us (9%)
  other arithmetic  145 us (5%)
  local copies, waits for them, and re-layouts  134 us (5%)
    unnamed x28, waiting for transfers between devices  686 us
    all_gather x1, waiting for transfers between devices, body(): rows_grad = lax.all_gather(cotangent, 'tensor', axis=0, tiled=True)  148 us
    all_gather x1, waiting for transfers between devices, body(): rows_two = lax.all_gather(input_two, 'tensor', axis=0, tiled=True)  148 us
    all_gather x1, waiting for transfers between devices, body(): rows_branch = lax.all_gather(grad_branch, 'tensor', axis=0, tiled=True)  148 us
    reduce_scatter x1, waiting for transfers between devices, body(): lax.psum_scatter(product(attended, merge_full).astype(jnp.bfloat16), 'ten...  145 us
    reduce_scatter x1, waiting for transfers between devices, body(): lax.psum_scatter(product(lax.slice_in_dim(activated, 0, local_rows * lax....  143 us
    all_gather x1, waiting for transfers between devices, body(): rows_one = lax.all_gather(input_one, 'tensor', axis=0, tiled=True)  125 us
    dot_general x10, matrix products, contract_cols(): lax.dot_general(left, right, (((1,), (1,)), ((), ())), preferred_element_...  118 us
  transfers between devices with their start and end apart: 21, of which 18 were waited for; matrix products, arithmetic and copies ran while one was open for 8% of the time, Pallas kernels for 0%

commit v1 on v0

v1 whole, which is shorter than its diff:
```python
import math
from functools import partial

import jax
import jax.numpy as jnp
from jax import lax
from jax.experimental import pallas as pl
from jax.experimental.pallas import tpu as pltpu
from jax.sharding import PartitionSpec as P

HEAD_DIM = 64
GROUPS = 4
LANES = 128
TILE = 256
EPSILON = 1e-06
VMEM = 56 * 1024 * 1024
F32 = jnp.float32
BF16 = jnp.bfloat16
NN = (((1,), (0,)), ((), ()))
NT = (((1,), (1,)), ((), ()))
TN = (((0,), (0,)), ((), ()))
ANY = pl.BlockSpec(memory_space=pl.ANY)


def dot(left, right, dims=NN):
    return lax.dot_general(left, right, dims, preferred_element_type=F32)


def merged(block):
    return block.reshape(-1, block.shape[-1])


def normalize(values):
    row_mean = jnp.mean(values, axis=-1, keepdims=True)
    centred = values - row_mean
    inv_scale = lax.rsqrt(jnp.mean(centred * centred, axis=-1, keepdims=True) + EPSILON)
    return (centred * inv_scale, inv_scale)


def normalize_back(grad_normed, normed, inv_scale):
    return inv_scale * (
        grad_normed
        - jnp.mean(grad_normed, axis=-1, keepdims=True)
        - normed * jnp.mean(grad_normed * normed, axis=-1, keepdims=True)
    )


def whole(shape):
    return pl.BlockSpec(shape, lambda *_: (0,) * len(shape))


def row_tile(shape):
    return pl.BlockSpec((TILE,) + shape[1:], lambda i, *_: (i,) + (0,) * (len(shape) - 1))


def call(kernel, grid, in_specs, out_specs, out_shape, args, scratch=(), flops=0, exps=0, scalars=(), after=()):
    count = len(args)

    def with_waits(*refs):
        head = refs[: len(scalars) + count]
        return kernel(*head, *refs[len(scalars) + count + len(after) :])

    moved = sum(a.size * a.dtype.itemsize for a in args) + sum(math.prod(s.shape) * s.dtype.itemsize for s in out_shape)
    return pl.pallas_call(
        with_waits,
        grid_spec=pltpu.PrefetchScalarGridSpec(
            num_scalar_prefetch=len(scalars),
            grid=grid,
            in_specs=list(in_specs) + [ANY] * len(after),
            out_specs=list(out_specs),
            scratch_shapes=list(scratch),
        ),
        out_shape=list(out_shape),
        compiler_params=pltpu.CompilerParams(vmem_limit_bytes=VMEM),
        cost_estimate=pl.CostEstimate(flops=int(flops), bytes_accessed=int(moved), transcendentals=int(exps)),
    )(*scalars, *args, *after)


def shaped(shape, dtype):
    return jax.ShapeDtypeStruct(shape, dtype)


def split_kernel(core, array, out, *, wide):
    half = out.shape[1] // 2
    for place in range(half // wide):
        even = array[:, 2 * place * wide : (2 * place + 1) * wide]
        odd = array[:, (2 * place + 1) * wide : (2 * place + 2) * wide]
        at = place * wide
        out[:, at : at + wide] = jnp.where(core[0] == 0, even, odd)
        out[:, half + at : half + at + wide] = jnp.where(core[0] == 0, odd, even)


def split_columns(core, array, wide):
    tile = row_tile(array.shape)
    return call(
        partial(split_kernel, wide=wide),
        (array.shape[0] // TILE,),
        [tile],
        [tile],
        [shaped(array.shape, array.dtype)],
        (array,),
        scalars=(core,),
    )[0]


def output_kernel(core, stream, one, two, bias, out, *, wide):
    half = out.shape[1] // 2
    total = stream[...] + one[...] + two[...] + bias[...]
    if wide % LANES:
        out[...] = total
        return
    for place in range(half // wide):
        at = place * wide
        own, other = total[:, at : at + wide], total[:, half + at : half + at + wide]
        out[:, 2 * at : 2 * at + wide] = jnp.where(core[0] == 0, own, other)
        out[:, 2 * at + wide : 2 * at + 2 * wide] = jnp.where(core[0] == 0, other, own)


def output_rows(core, stream, one, two, bias, wide, after=()):
    tile = row_tile(stream.shape)
    return call(
        partial(output_kernel, wide=wide),
        (stream.shape[0] // TILE,),
        [tile] * 3 + [whole(bias.shape)],
        [tile],
        [shaped(stream.shape, F32)],
        (stream, one, two, bias),
        scalars=(core,),
        after=after,
    )[0]


def finish_feed_kernel(low, high, expand, contract):
    part = low.shape[2]
    for at, ref in ((0, low), (part, high)):
        expand[:, at : at + part] = ref[0].astype(F32)
        contract[at : at + part, :] = ref[1].astype(F32).T


def finish_feed(low, high):
    _, wide, part = low.shape
    return call(
        finish_feed_kernel,
        (1,),
        [whole(low.shape)] * 2,
        [whole((wide, 2 * part)), whole((2 * part, wide))],
        [shaped((wide, 2 * part), F32), shaped((2 * part, wide), F32)],
        (low, high),
    )


def finish_attention_kernel(blocks, attention, merge_out):
    attention[...] = blocks[:3].astype(F32)
    merge_out[...] = blocks[3].astype(F32).T


def finish_attention(blocks):
    _, wide, columns = blocks.shape
    return call(
        finish_attention_kernel,
        (1,),
        [whole(blocks.shape)],
        [whole((3, wide, columns)), whole((columns, wide))],
        [shaped((3, wide, columns), F32), shaped((columns, wide), F32)],
        (blocks,),
    )


def group_rows(band, group, values):
    return jnp.where(band == group, values, jnp.zeros_like(values))


def embed_kernel(present, pix, band, table, bias, gain, shift, lo_own, lo_came, hi_own, hi_came, stream, normed, acc):
    tile = pl.program_id(0)
    half = acc.shape[1] // 2
    width = pix.shape[1]
    acc[...] = table[...]
    for group in range(GROUPS):

        @pl.when(present[tile * GROUPS + group] > 0)
        def _():
            rows = group_rows(band[...], group, pix[...])
            at = pl.ds((group % 2) * width, width)
            own, came = (lo_own, lo_came) if group < 2 else (hi_own, hi_came)
            acc[:, :half] += dot(rows, merged(own[:, :, at]), NT)
            acc[:, half:] += dot(rows, merged(came[:, :, at]), NT)

    total = acc[...]
    for group in range(GROUPS):
        total = total + jnp.where(band[...] == group, bias[group : group + 1, :], 0.0)
    stream[...] = total
    normed[...] = (normalize(total)[0] * gain[...] + shift[...]).astype(BF16)


def embed(present, pixels, band, table, bias, gain, shift, patches, after=()):
    rows, model = table.shape
    args = (pixels, band, table, bias, gain, shift) + patches
    specs = [row_tile(pixels.shape), row_tile(band.shape), row_tile(table.shape)] + [whole(a.shape) for a in args[3:]]
    return call(
        embed_kernel,
        (rows // TILE,),
        specs,
        [row_tile((rows, model))] * 2,
        [shaped((rows, model), F32), shaped((rows, model), BF16)],
        args,
        scratch=[pltpu.VMEM((TILE, model), F32)],
        flops=4 * rows * pixels.shape[1] * model,
        scalars=(present,),
        after=after,
    )


def project_kernel(x, qk_own, qk_came, vm_own, vm_came, bias, query, key, value):
    half = x.shape[1] // 2
    kept, other = x[:, :half], x[:, half:]

    def product(own, came, which):
        return dot(kept, merged(own[which])) + dot(other, merged(came[which]))

    query[...] = (product(qk_own, qk_came, 0) + bias[0:1, :]).astype(BF16)
    key[...] = product(qk_own, qk_came, 1).astype(BF16)
    value[...] = (product(vm_own, vm_came, 0) + bias[1:2, :]).astype(BF16)


def project(x, qk, vm, bias, after=()):
    rows, model = x.shape
    columns = min(256, model)
    weight = lambda a: pl.BlockSpec(a.shape[:-1] + (columns,), lambda i: (0, 0, 0, i))
    first = lambda a: pl.BlockSpec((1,) + a.shape[1:-1] + (columns,), lambda i: (0, 0, 0, i))
    return call(
        project_kernel,
        (model // columns,),
        [whole(x.shape)] + [weight(a) for a in qk] + [first(a) for a in vm] + [pl.BlockSpec((2, columns), lambda i: (0, i))],
        [pl.BlockSpec((rows, columns), lambda i: (0, i))] * 3,
        [shaped((rows, model), BF16)] * 3,
        (x,) + qk + vm + (bias,),
        flops=6 * rows * model * model,
        after=after,
    )


def head_mask(shape, head):
    lane = lax.broadcasted_iota(jnp.int32, shape, 1)
    return (lane < HEAD_DIM) if head == 0 else (lane >= HEAD_DIM)


def only_head(values, head):
    return jnp.where(head_mask(values.shape, head), values, jnp.zeros_like(values))


def attend_kernel(q_ref, k_ref, v_ref, seg_col_ref, seg_row_ref, out_ref, log_ref, bias_ref):
    pair = pl.program_id(0)
    rows = q_ref.shape[0]

    @pl.when(pair == 0)
    def _():
        bias_ref[...] = jnp.where(seg_col_ref[...] == seg_row_ref[...], 0.0, -1e30).astype(F32)
        log_ref[...] = jnp.zeros_like(log_ref)

    keys = k_ref[...]
    value_of = [only_head(v_ref[...], head) for head in range(2)]
    for start in range(0, rows, TILE):
        at = pl.ds(start, TILE)
        query = q_ref[at, :] * jnp.asarray(HEAD_DIM ** (-0.5), BF16)
        lane = lax.broadcasted_iota(jnp.int32, (TILE, LANES), 1)
        logs = log_ref[at, :]
        total = jnp.zeros((TILE, LANES), F32)
        for head in range(2):
            scores = dot(only_head(query, head), keys, NT) + bias_ref[at, :]
            top = jnp.max(scores, axis=1, keepdims=True)
            shifted = jnp.exp(scores - top)
            mass = jnp.sum(shifted, axis=1, keepdims=True)
            total = total + dot(shifted.astype(BF16), value_of[head]) * (1.0 / mass)
            logs = jnp.where(lane == 2 * pair + head, top + jnp.log(mass), logs)
        out_ref[at, :] = total.astype(BF16)
        log_ref[at, :] = logs


def attend(query, key, value, segment, after=()):
    rows, width = query.shape
    block = pl.BlockSpec((rows, LANES), lambda i: (0, i))
    return call(
        attend_kernel,
        (width // LANES,),
        [block, block, block, whole((rows, 1)), whole((1, rows))],
        [block, whole((rows, LANES))],
        [shaped((rows, width), BF16), shaped((rows, LANES), F32)],
        (query, key, value, segment[:, None], segment[None, :]),
        scratch=[pltpu.VMEM((rows, rows), F32)],
        flops=16 * rows * rows * width,
        exps=rows * rows * width // HEAD_DIM,
        after=after,
    )


def attend_back_kernel(
    q_ref, k_ref, v_ref, g_ref, seg_col_ref, seg_row_ref, log_ref, delta_ref, dq_ref, dk_ref, dv_ref, sum_ref, bias_ref, acc_ref, *, base
):
    pair = base + pl.program_id(0)
    rows = q_ref.shape[0]

    @pl.when(pl.program_id(0) == 0)
    def _():
        bias_ref[...] = jnp.where(seg_col_ref[...] == seg_row_ref[...], 0.0, -1e30).astype(F32)

    query = q_ref[...] * jnp.asarray(HEAD_DIM ** (-0.5), BF16)
    grads = g_ref[...]
    query_of = [only_head(query, head) for head in range(2)]
    grads_of = [only_head(grads, head) for head in range(2)]
    acc_ref[...] = jnp.zeros_like(acc_ref)
    value_sum = jnp.zeros((1, LANES), F32)
    for start in range(0, rows, TILE):
        at = pl.ds(start, TILE)
        keys = k_ref[at, :]
        values = v_ref[at, :]
        grad_key = jnp.zeros((TILE, LANES), F32)
        grad_value = jnp.zeros((TILE, LANES), F32)
        for head in range(2):
            key_h = only_head(keys, head)
            log_row = log_ref[pl.ds(2 * pair + head, 1), :]
            delta_row = delta_ref[pl.ds(2 * pair + head, 1), :]
            scores = dot(key_h, query, NT) + bias_ref[at, :]
            probs = jnp.exp(scores - log_row)
            grad_value = grad_value + dot(probs.astype(BF16), grads_of[head])
            grad_probs = dot(only_head(values, head), grads, NT)
            grad_scores = (probs * (grad_probs - delta_row)).astype(BF16)
            grad_key = grad_key + dot(grad_scores, query_of[head])
            acc_ref[...] += dot(key_h, grad_scores, TN)
        grad_value = grad_value.astype(BF16)
        dk_ref[at, :] = grad_key.astype(BF16)
        dv_ref[at, :] = grad_value
        value_sum = value_sum + jnp.sum(grad_value.astype(F32), axis=0, keepdims=True)
    grad_query = (acc_ref[...].T * HEAD_DIM ** (-0.5)).astype(BF16)
    dq_ref[...] = grad_query
    sum_ref[0:1, :] = jnp.sum(grad_query.astype(F32), axis=0, keepdims=True)
    sum_ref[1:2, :] = value_sum


def attend_back(query, key, value, grads, segment, log_rows, delta_rows, base, pairs, after=()):
    rows = query.shape[0]
    width = pairs * LANES
    taken = pl.BlockSpec((rows, LANES), lambda i: (0, base + i))
    given = pl.BlockSpec((rows, LANES), lambda i: (0, i))
    return call(
        partial(attend_back_kernel, base=base),
        (pairs,),
        [taken] * 4 + [whole((rows, 1)), whole((1, rows)), whole(log_rows.shape), whole(delta_rows.shape)],
        [given] * 3 + [pl.BlockSpec((2, LANES), lambda i: (0, i))],
        [shaped((rows, width), BF16)] * 3 + [shaped((2, width), F32)],
        (query, key, value, grads, segment[:, None], segment[None, :], log_rows, delta_rows),
        scratch=[pltpu.VMEM((rows, rows), F32), pltpu.VMEM((LANES, rows), F32)],
        flops=40 * rows * rows * width,
        exps=rows * rows * width // HEAD_DIM,
        after=after,
    )


def merge_kernel(attended, stream, bias, gain, shift, own, came, stream_one, normed):
    half = stream.shape[1] // 2
    stream_one[:, :half] = stream[:, :half] + dot(attended[...], merged(own[0]), NT)
    stream_one[:, half:] = stream[:, half:] + dot(attended[...], merged(came[0]), NT)
    total = stream_one[...] + bias[...]
    stream_one[...] = total
    normed[...] = (normalize(total)[0] * gain[...] + shift[...]).astype(BF16)


def second(array):
    return pl.BlockSpec((1,) + array.shape[1:], lambda *_: (1,) + (0,) * (array.ndim - 1))


def merge(attended, stream, bias, gain, shift, vm, after=()):
    rows, model = stream.shape
    return call(
        merge_kernel,
        (rows // TILE,),
        [row_tile(attended.shape), row_tile(stream.shape)] + [whole((1, model))] * 3 + [second(a) for a in vm],
        [row_tile((rows, model))] * 2,
        [shaped((rows, model), F32), shaped((rows, model), BF16)],
        (attended, stream, bias, gain, shift) + vm,
        flops=2 * rows * model * model,
        after=after,
    )


def gelu_parts(hidden):
    t = 1.0 / (1.0 + (0.3275911 * math.sqrt(0.5)) * jnp.abs(hidden))
    bell = jnp.exp(-0.5 * hidden * hidden)
    poly = t * (
        0.5 * 0.254829592
        + t * (-0.5 * 0.284496736 + t * (0.5 * 1.421413741 + t * (-0.5 * 1.453152027 + t * (0.5 * 1.061405429))))
    )
    tail = poly * bell
    below = jnp.where(hidden >= 0, 1.0 - tail, tail)
    return hidden * below, below + (hidden * (1.0 / math.sqrt(2.0 * math.pi))) * bell


def feed_kernel(
    core, x_ref, g_ref, e_own, e_other, c_own, c_other, b_ref, y_ref, d_ref, keep_ref, send_ref, db_ref, xt_ref, gt_ref, a_ref, h_ref
):
    step = pl.program_id(0)
    rows, model = x_ref.shape
    half = model // 2

    @pl.when(step == 0)
    def _():
        xt_ref[...] = x_ref[...].T
        gt_ref[...] = g_ref[...].T
        y_ref[...] = jnp.zeros_like(y_ref)
        d_ref[...] = jnp.zeros_like(d_ref)

    expand = (merged(e_own[...]), merged(e_other[...]))
    contract = (merged(c_own[...]), merged(c_other[...]))
    sums = jnp.zeros((1, h_ref.shape[1]), F32)
    for start in range(0, rows, TILE):
        at = pl.ds(start, TILE)
        hidden = dot(x_ref[at, :half], expand[0]) + dot(x_ref[at, half:], expand[1]) + b_ref[0]
        grad_active = dot(g_ref[at, :half], contract[0]) + dot(g_ref[at, half:], contract[1])
        active, slope = gelu_parts(hidden)
        active = active.astype(BF16)
        grad_hidden = (grad_active * slope).astype(BF16)
        a_ref[at, :] = active
        h_ref[at, :] = grad_hidden
        sums = sums + jnp.sum(grad_hidden.astype(F32), axis=0, keepdims=True)
        for side in range(2):
            cols = pl.ds(side * half, half)
            y_ref[at, cols] += dot(active, contract[side], NT)
            d_ref[at, cols] += dot(grad_hidden, expand[side], NT)
    db_ref[0] = sums
    for side, ref in ((0, keep_ref), (1, send_ref)):
        cols = pl.ds(side * half, half)
        shape = ref.shape[:1] + ref.shape[3:]
        ref[:, 0, 0] = dot(xt_ref[cols, :], h_ref[...]).astype(BF16).reshape(shape)
        ref[:, 0, 1] = dot(gt_ref[cols, :], a_ref[...]).astype(BF16).reshape(shape)


def feed(core, rows_two, cotangent, weights, bias, which, after=()):
    rows, model = rows_two.shape
    pairs, _, steps, _, wide, unit = weights.shape
    part = unit // 2
    block = (pairs, 1, 1, 1, wide, part)
    weight = lambda side, mat: pl.BlockSpec(
        block, lambda i, core: (0, core[0] if side == 0 else 1 - core[0], i, mat, 0, which)
    )
    grad = pl.BlockSpec((pairs, 1, 2, wide, part), lambda i, core: (0, i, 0, 0, 0))
    return call(
        feed_kernel,
        (steps,),
        [whole((rows, model))] * 2
        + [weight(0, 0), weight(1, 0), weight(0, 1), weight(1, 1)]
        + [pl.BlockSpec((1, 1, part), lambda i, core: (i, 0, 0))],
        [whole((rows, model))] * 2 + [grad, grad, pl.BlockSpec((1, 1, part), lambda i, core: (i, 0, 0))],
        [shaped((rows, model), F32)] * 2
        + [shaped((pairs, steps, 2, wide, part), BF16)] * 2
        + [shaped((steps, 1, part), F32)],
        (rows_two, cotangent, weights, weights, weights, weights, bias),
        scratch=[
            pltpu.VMEM((model, rows), BF16),
            pltpu.VMEM((model, rows), BF16),
            pltpu.VMEM((rows, part), BF16),
            pltpu.VMEM((rows, part), BF16),
        ],
        flops=12 * rows * model * part * steps,
        exps=rows * part * steps,
        scalars=(core,),
        after=after,
    )


def merge_back_kernel(
    d_one, d_two, top, stream_one, attended, gain, own, came, heads, grad_stream, grad_branch, grad_attended, delta, sums
):
    half = top.shape[1] // 2
    grad_two = d_one[...] + d_two[...]
    normed, scale = normalize(stream_one[...])
    cotangent = top[...].astype(F32)
    total = cotangent + normalize_back(grad_two * gain[...], normed, scale)
    grad_stream[...] = total
    low = total.astype(BF16)
    grad_branch[...] = low
    grads = (dot(low[:, :half], merged(own[0])) + dot(low[:, half:], merged(came[0]))).astype(BF16)
    grad_attended[...] = grads
    both = grads.astype(F32) * attended[...].astype(F32)
    delta[...] = lax.dot_general(heads[...], both, NT, precision=lax.Precision.HIGHEST, preferred_element_type=F32)

    @pl.when(pl.program_id(0) == 0)
    def _():
        sums[...] = jnp.zeros_like(sums)

    for row, part in enumerate((grad_two * normed, grad_two, total, cotangent)):
        sums[row : row + 1, :] += jnp.sum(part, axis=0, keepdims=True)


def merge_back(d_one, d_two, top, stream_one, attended, gain, vm, heads, after=()):
    rows, model = stream_one.shape
    tile = row_tile((rows, model))
    return call(
        merge_back_kernel,
        (rows // TILE,),
        [tile] * 5 + [whole((1, model))] + [second(a) for a in vm] + [whole(heads.shape)],
        [tile] * 3 + [pl.BlockSpec((heads.shape[0], TILE), lambda i: (0, i)), whole((8, model))],
        [
            shaped((rows, model), F32),
            shaped((rows, model), BF16),
            shaped((rows, model), BF16),
            shaped((heads.shape[0], rows), F32),
            shaped((8, model), F32),
        ],
        (d_one, d_two, top, stream_one, attended, gain) + vm + (heads,),
        flops=2 * rows * model * model,
        after=after,
    )


def attention_grads_kernel(x, branch, query, key, value, attended, keep, send, xt, bt):
    half = xt.shape[0] // 2

    @pl.when(pl.program_id(0) == 0)
    def _():
        xt[...] = x[...].T
        bt[...] = branch[...].T

    pairs, blocks, _, wide, columns = keep.shape
    for side, ref in ((0, keep), (1, send)):
        at = pl.ds(side * half, half)
        for place, (left, right) in enumerate(((xt, query), (xt, key), (xt, value), (bt, attended))):
            grad = dot(left[at, :], right[...]).astype(BF16)
            for block in range(blocks):
                part = grad[:, block * columns : (block + 1) * columns]
                ref[:, block, place] = part.reshape(pairs, wide, columns)


def attention_grads(x, branch, query, key, value, attended, pairs, steps, base, columns, after=()):
    rows, model = x.shape
    wide = model // (2 * pairs)
    blocks = max(1, LANES // columns)
    column = pl.BlockSpec((rows, blocks * columns), lambda i: (0, i))
    shifted = pl.BlockSpec((rows, blocks * columns), lambda i: (0, base // blocks + i))
    grad = pl.BlockSpec((pairs, blocks, 4, wide, columns), lambda i: (0, i, 0, 0, 0))
    return call(
        attention_grads_kernel,
        (steps // blocks,),
        [whole(x.shape)] * 2 + [column] * 3 + [shifted],
        [grad] * 2,
        [shaped((pairs, steps, 4, wide, columns), BF16)] * 2,
        (x, branch, query, key, value, attended),
        scratch=[pltpu.VMEM((model, rows), BF16)] * 2,
        flops=8 * rows * model * columns * steps,
        after=after,
    )


def project_back_kernel(
    query, key, value, grad_stream, stream, band, gain, qk_own, qk_came, vm_own, vm_came, grad_embed, sums, acc
):
    half = stream.shape[1] // 2
    for side, (qk, vm) in enumerate(((qk_own, vm_own), (qk_came, vm_came))):
        acc[:, side * half : (side + 1) * half] = (
            dot(query[...], merged(qk[0]), NT) + dot(key[...], merged(qk[1]), NT) + dot(value[...], merged(vm[0]), NT)
        )
    grad_one = acc[...]
    normed, scale = normalize(stream[...])
    total = grad_stream[...] + normalize_back(grad_one * gain[...], normed, scale)
    grad_embed[...] = total.astype(BF16)

    @pl.when(pl.program_id(0) == 0)
    def _():
        sums[...] = jnp.zeros_like(sums)

    parts = [group_rows(band[...], group, total) for group in range(GROUPS)] + [grad_one * normed, grad_one]
    for row, part in enumerate(parts):
        sums[row : row + 1, :] += jnp.sum(part, axis=0, keepdims=True)


def project_back(query, key, value, grad_stream, stream, band, gain, qk, vm, after=()):
    rows, model = stream.shape
    tile = row_tile((rows, model))
    first = lambda a: pl.BlockSpec((1,) + a.shape[1:], lambda i: (0, 0, 0, 0))
    return call(
        project_back_kernel,
        (rows // TILE,),
        [tile] * 5 + [row_tile(band.shape), whole((1, model))] + [whole(a.shape) for a in qk] + [first(a) for a in vm],
        [tile, whole((8, model))],
        [shaped((rows, model), BF16), shaped((8, model), F32)],
        (query, key, value, grad_stream, stream, band, gain) + qk + vm,
        scratch=[pltpu.VMEM((TILE, model), F32)],
        flops=6 * rows * model * model,
        after=after,
    )


def patch_grads_kernel(present, grads, pix, band, keep, send, gt, acc, *, base):
    group = base + pl.program_id(0)
    half = gt.shape[0] // 2

    @pl.when(pl.program_id(0) == 0)
    def _():
        gt[...] = grads[...].T

    acc[...] = jnp.zeros_like(acc)
    for tile in range(pix.shape[0] // TILE):

        @pl.when(present[tile * GROUPS + group] > 0)
        def _():
            at = pl.ds(tile * TILE, TILE)
            acc[...] += dot(gt[:, at], group_rows(band[at, :], group, pix[at, :]))

    keep[...] = acc[:half, :].astype(BF16)
    send[...] = acc[half:, :].astype(BF16)


def patch_grads(present, grads, pixels, band, base, after=()):
    rows, model = grads.shape
    width = pixels.shape[1]
    count = GROUPS // 2
    given = pl.BlockSpec((model // 2, width), lambda i, present: (0, i))
    return call(
        partial(patch_grads_kernel, base=base),
        (count,),
        [whole(grads.shape), whole(pixels.shape), whole(band.shape)],
        [given] * 2,
        [shaped((model // 2, count * width), BF16)] * 2,
        (grads, pixels, band),
        scratch=[pltpu.VMEM((model, rows), BF16), pltpu.VMEM((model, width), F32)],
        flops=2 * rows * width * model,
        scalars=(present,),
        after=after,
    )


def pixel_grads_kernel(present, grads, band, lo_own, lo_came, hi_own, hi_came, out):
    tile = pl.program_id(0)
    half = grads.shape[1] // 2
    width = out.shape[1]
    out[...] = jnp.zeros_like(out)
    for group in range(GROUPS):

        @pl.when(present[tile * GROUPS + group] > 0)
        def _():
            at = pl.ds((group % 2) * width, width)
            own, came = (lo_own, lo_came) if group < 2 else (hi_own, hi_came)
            spread = dot(grads[:, :half], merged(own[:, :, at])) + dot(grads[:, half:], merged(came[:, :, at]))
            out[...] = jnp.where(band[...] == group, spread, out[...])


def pixel_grads(present, grads, band, patches, width, after=()):
    rows, model = grads.shape
    return call(
        pixel_grads_kernel,
        (rows // TILE,),
        [row_tile(grads.shape), row_tile(band.shape)] + [whole(a.shape) for a in patches],
        [row_tile((rows, width))],
        [shaped((rows, width), F32)],
        (grads, band) + patches,
        flops=4 * rows * width * model,
        scalars=(present,),
        after=after,
    )[0]


def make_body(fsdp, tensor):
    pairs = fsdp // 2
    t_bits = list(range(tensor.bit_length() - 1))
    f_bits = list(range(1, fsdp.bit_length() - 1))
    up, down = f_bits, f_bits[::-1]

    def swap(array, axis, bit):
        size = fsdp if axis == "fsdp" else tensor
        return lax.ppermute(array, axis, [(i, i ^ (1 << bit)) for i in range(size)])

    def body(
        pixels,
        segment,
        band_group,
        scaled_position,
        patch_weight,
        patch_bias,
        norm_gains,
        vector_biases,
        attention_weight,
        query_value_bias,
        merge_weight,
        expand_weight,
        expand_bias,
        contract_weight,
        cotangent,
    ):
        index = {"fsdp": lax.axis_index("fsdp"), "tensor": lax.axis_index("tensor")}
        core = index["fsdp"] & 1
        rows, pix = pixels.shape
        model = cotangent.shape[1]
        thin = patch_bias.shape[1]
        wide = model // fsdp
        unit = expand_weight.shape[1]
        half_unit = unit // 2
        segment = lax.dynamic_slice_in_dim(segment, index["tensor"] * rows, rows)

        def grow(array, axis, bit, dim):
            came = swap(array, axis, bit)
            mine = ((index[axis] >> bit) & 1) == 1
            return jnp.where(
                mine, jnp.concatenate([came, array], axis=dim), jnp.concatenate([array, came], axis=dim)
            )

        def spread(array, order):
            lead = array.shape[:-2]
            array = array.reshape(lead + (1,) * len(f_bits) + array.shape[-2:])
            for bit in order:
                array = grow(array, "fsdp", bit, len(lead) + len(f_bits) - bit)
            array = array.reshape(lead + (pairs,) + array.shape[-2:])
            return array, swap(array, "fsdp", 0)

        def first_swap(send):
            return swap(send, "fsdp", 0)

        def next_swap(keep, came, bit):
            dim = len(f_bits) - bit
            mine = (index["fsdp"] >> bit) & 1
            take = lambda array, at: lax.dynamic_slice_in_dim(array, at, 1, axis=dim)
            both = lambda at: (take(keep, at).astype(F32) + take(came, at).astype(F32)).astype(keep.dtype)
            return both(mine), swap(both(1 - mine), "fsdp", bit)

        def unfold(array):
            return array.reshape((2,) * len(f_bits) + array.shape[1:])

        def last_sum(keep, came):
            rest = keep.shape[len(f_bits) :]
            return (keep.astype(F32) + came.astype(F32)).astype(keep.dtype).reshape(rest)

        def over_tensor(blocks):
            return lax.psum_scatter(blocks, "tensor", scatter_dimension=0, tiled=False)

        def to_split(array):
            parts = array.reshape(array.shape[0], pairs, 2, wide)
            even, odd = (parts[:, :, i].reshape(array.shape[0], -1) for i in range(2))
            return jnp.where(core == 0, jnp.concatenate([even, odd], axis=1), jnp.concatenate([odd, even], axis=1))

        def from_split(array):
            parts = array.reshape(array.shape[0], 2, pairs, wide)
            mine, other = parts[:, 0], parts[:, 1]
            parts = jnp.where(core == 0, jnp.stack([mine, other], axis=2), jnp.stack([other, mine], axis=2))
            return parts.reshape(array.shape)

        tie = lambda array, *others: lax.optimization_barrier((array,) + others)[0]
        core_at = core[None].astype(jnp.int32)
        aligned = wide % LANES == 0

        both = jnp.stack([expand_weight, contract_weight.T])
        feed_weights = lax.all_gather(both, ("fsdp", "tensor"), axis=0, tiled=False)
        feed_weights = feed_weights.reshape(pairs, 2, tensor, 2, wide, unit)

        patch = patch_weight.reshape(-1, thin).T
        for bit in t_bits:
            patch = grow(patch, "tensor", bit, 0)
        columns = (GROUPS // 2) * pix
        patch_lo = spread(patch[:, :columns], up)
        patch_hi = spread(patch[:, columns:], down)
        patches = patch_lo + patch_hi

        small = jnp.concatenate(
            [patch_bias.reshape(-1), norm_gains.reshape(-1), vector_biases.reshape(-1), query_value_bias.reshape(-1), expand_bias]
        )[None, :]
        small = tie(small, patch)
        for bit in t_bits:
            small = grow(small, "tensor", bit, 0)
        for bit in range(len(f_bits) + 1):
            small = grow(small, "fsdp", bit, 0)
        n_vec = GROUPS + 2 + 4
        cut = n_vec * thin
        small = small.astype(F32)
        vectors = small[:, :cut].reshape(fsdp * tensor, n_vec, thin).transpose(1, 0, 2).reshape(n_vec, model)
        vectors = to_split(vectors)
        patch_bias_rows = vectors[:GROUPS]
        gains = [vectors[GROUPS + i : GROUPS + i + 1] for i in range(2)]
        biases = [vectors[GROUPS + 2 + i : GROUPS + 3 + i] for i in range(4)]
        by_hidden = small[:, cut:].reshape(fsdp, tensor, -1).transpose(1, 0, 2)
        qv_rows = by_hidden[:, :, : 2 * thin].reshape(fsdp * tensor, 2, thin).transpose(1, 0, 2).reshape(2, model)
        unit_bias = by_hidden[:, :, 2 * thin :].reshape(tensor, 2, 1, half_unit)

        attention = jnp.concatenate([attention_weight, merge_weight.T[None]], axis=0)
        attention = tie(attention, patch)
        for bit in t_bits:
            attention = grow(attention, "tensor", bit, 2)
        qk = spread(attention[:2], up)
        vm = spread(attention[2:], down)

        band = band_group[:, None]
        present = jnp.any(band_group.reshape(-1, TILE, 1) == jnp.arange(GROUPS), axis=1).astype(jnp.int32).reshape(-1)
        half_width = model // 2
        column = jnp.arange(model)
        place = column % half_width
        natural = (2 * (place // wide) + (core ^ (column // half_width))) * wide + place % wide
        rates = jnp.exp((natural % half_width).astype(F32) * (-math.log(10000.0) / half_width))
        angles = scaled_position.astype(F32)[:, None] * rates[None, :]
        quarter = model // 4
        table = jnp.concatenate(
            [
                f(angles[:, i * quarter : (i + 1) * quarter])
                for i, f in enumerate((jnp.sin, jnp.cos, jnp.sin, jnp.cos))
            ],
            axis=1,
        )
        top = split_columns(core_at, cotangent, wide) if aligned else to_split(cotangent)
        stream_zero, input_one = embed(present, pixels, band, table, patch_bias_rows, gains[0], biases[0], patches)

        query, key, value = project(input_one, qk, vm, qv_rows)
        attended, logs = attend(query, key, value, segment)
        stream_one, input_two = merge(attended, stream_zero, biases[1], gains[1], biases[2], vm)

        y_low, d_low, keep_low, send_low, units_low = feed(core_at, input_two, top, feed_weights, unit_bias[:, 0], 0)
        came_low = first_swap(send_low)
        y_high, d_high, keep_high, send_high, units_high = feed(core_at, input_two, top, feed_weights, unit_bias[:, 1], 1)
        unit_grads = [units_low, units_high]

        heads = model // HEAD_DIM
        head_rows = (jnp.arange(heads)[:, None] == jnp.arange(model)[None, :] // HEAD_DIM).astype(F32)
        came_high = first_swap(send_high)
        grad_stream_one, grad_branch, grad_attended, delta, sums_two = merge_back(
            d_low, d_high, top, stream_one, attended, gains[1], vm, head_rows, after=(came_low,)
        )
        log_rows = logs[:, :heads].T
        all_pairs = model // LANES
        calls = 4
        each = all_pairs // calls
        back = lambda i, after: attend_back(
            query, key, value, grad_attended, segment, log_rows, delta, i * each, each, after=after
        )
        half_columns = 2 * each * LANES
        per_call = tensor // 2

        def grads_of(two, base, after):
            q, k, v = (jnp.concatenate([p[i] for p in two], axis=1) for i in range(3))
            return (q, k, v), attention_grads(
                input_one, grad_branch, q, k, v, attended, pairs, per_call, base, half_columns // per_call, after=after
            )

        keep_low, came_low = next_swap(unfold(keep_low), unfold(came_low), down[0])
        first = back(0, (came_high,))
        keep_high, came_high = next_swap(unfold(keep_high), unfold(came_high), up[0])
        second_part = back(1, ())
        left, (keep_left, send_left) = grads_of((first, second_part), 0, (came_low,))
        came_left = first_swap(send_left)
        if len(f_bits) > 1:
            keep_low, came_low = next_swap(keep_low, came_low, down[1])
        third = back(2, ())
        fourth = back(3, (came_high, came_left))
        keep_left, came_left = next_swap(unfold(keep_left), unfold(came_left), up[0])
        if len(f_bits) > 1:
            keep_high, came_high = next_swap(keep_high, came_high, up[1])
        right, (keep_right, send_right) = grads_of((third, fourth), per_call, (came_low,))
        came_right = first_swap(send_right)
        for bit in down[2:]:
            keep_low, came_low = next_swap(keep_low, came_low, bit)
        for bit in up[2:]:
            keep_high, came_high = next_swap(keep_high, came_high, bit)
        feed_low = over_tensor(last_sum(keep_low, came_low))
        feed_high = over_tensor(last_sum(keep_high, came_high))
        expand_out, contract_out = finish_feed(feed_low, feed_high)
        grad_query, grad_key, grad_value = (jnp.concatenate([a, b], axis=1) for a, b in zip(left, right))
        grad_qv = jnp.concatenate([p[3] for p in (first, second_part, third, fourth)], axis=1)
        grad_embed, sums_one = project_back(
            grad_query, grad_key, grad_value, grad_stream_one, stream_zero, band, gains[0], qk, vm, after=(came_right, came_high)
        )
        for bit in up[1:]:
            keep_left, came_left = next_swap(keep_left, came_left, bit)
        keep_right, came_right = unfold(keep_right), unfold(came_right)
        for bit in down:
            keep_right, came_right = next_swap(keep_right, came_right, bit)
        grad_attention = over_tensor(
            jnp.concatenate([last_sum(keep_left, came_left), last_sum(keep_right, came_right)], axis=0)
        )
        attention_out, merge_out = finish_attention(grad_attention)

        patch_parts = []
        for base, order in ((0, up), (GROUPS // 2, down)):
            keep, send = patch_grads(present, grad_embed, pixels, band, base)
            shape = (pairs, tensor, thin, columns)
            keep, came = unfold(keep.reshape(shape)), unfold(first_swap(send.reshape(shape)))
            for bit in order:
                keep, came = next_swap(keep, came, bit)
            patch_parts.append(last_sum(keep, came))
        grad_patch = over_tensor(jnp.concatenate(patch_parts, axis=2)).astype(F32).T.reshape(GROUPS, pix, thin)
        pixel_grad = pixel_grads(present, grad_embed, band, patches, pix)
        block_output = output_rows(core_at, stream_one, y_low, y_high, biases[3], wide)
        if not aligned:
            block_output = from_split(block_output)

        vector_grads = from_split(
            jnp.concatenate(
                [sums_one[:GROUPS], sums_one[GROUPS : GROUPS + 1], sums_two[0:1], sums_one[GROUPS + 1 : GROUPS + 2]]
                + [sums_two[2:3], sums_two[1:2], sums_two[3:4]],
                axis=0,
            )
        )
        vector_grads = vector_grads.reshape(n_vec, fsdp * tensor, thin).transpose(1, 0, 2).reshape(fsdp, tensor, cut)
        hidden_grads = jnp.concatenate(
            [
                grad_qv.reshape(2, tensor, fsdp, thin).transpose(2, 1, 0, 3).reshape(fsdp, tensor, 2 * thin),
                jnp.stack(unit_grads, axis=1).reshape(tensor, fsdp, unit // fsdp).transpose(1, 0, 2),
            ],
            axis=2,
        )
        small_grads = jnp.concatenate([vector_grads, hidden_grads], axis=2).reshape(fsdp * tensor, -1)
        for axis, bits in (("fsdp", list(range(len(f_bits) + 1))[::-1]), ("tensor", t_bits[::-1])):
            for bit in bits:
                half = small_grads.shape[0] // 2
                mine = (index[axis] >> bit) & 1
                sent = lax.dynamic_slice_in_dim(small_grads, (1 - mine) * half, half)
                small_grads = lax.dynamic_slice_in_dim(small_grads, mine * half, half) + swap(sent, axis, bit)
        small_grads = small_grads[0]
        mine = small_grads[:cut].reshape(n_vec, thin)
        return (
            block_output,
            pixel_grad,
            grad_patch,
            mine[:GROUPS],
            mine[GROUPS : GROUPS + 2],
            mine[GROUPS + 2 :],
            attention_out,
            small_grads[cut : cut + 2 * thin].reshape(2, thin),
            merge_out,
            expand_out,
            small_grads[cut + 2 * thin :],
            contract_out,
        )

    return body


def solution(mesh):
    every = ("fsdp", "tensor")
    args = (
        P(every, None),
        P("fsdp"),
        P(every),
        P(every),
        P(None, None, every),
        P(None, every),
        P(None, every),
        P(None, every),
        P(None, "fsdp", "tensor"),
        P(None, ("tensor", "fsdp")),
        P("tensor", "fsdp"),
        P("fsdp", "tensor"),
        P(("tensor", "fsdp")),
        P("tensor", "fsdp"),
        P(every, None),
    )
    outs = (P(every, None), P(every, None)) + args[4:14]
    body = make_body(mesh.shape["fsdp"], mesh.shape["tensor"])
    return jax.shard_map(body, mesh=mesh, in_specs=args, out_specs=outs, check_vma=False)
```

time: 2770 us -> 683 us (0.25)
  waiting for transfers between devices: 1820 us -> 206 us
  matrix products: 401 us -> 0 us
  Pallas kernels: 0 us -> 296 us
  blocking collectives: 238 us -> 0 us
  local copies, waits for them, and re-layouts: 134 us -> 32.4 us
  other arithmetic: 145 us -> 73.5 us
  starting transfers between devices: 1.24 us -> 52.4 us
    unnamed x28 -> x5, waiting for transfers between devices: 686 us -> 0.08 us
    all_gather x8 -> x1, waiting for transfers between devices: 597 us -> 0.01 us  [body(): feed_weights = lax.all_gather(both, ('fsdp', 'tensor'), axis=0, tiled=False)]
    reduce_scatter x6 -> x4, waiting for transfers between devices: 540 us -> 0.01 us  [over_tensor(): return lax.psum_scatter(blocks, 'tensor', scatter_dimension=0, tiled=False)]
    dot_general x59 -> x0, matrix products: 396 us -> none  [the longest x10 118 us: contract_cols(): lax.dot_general(left, right, (((1,), (1,)), ((), ())), preferred_element_...]
    pallas_call x0 -> x21, Pallas kernels: none -> 296 us  [call(): pl.pallas_call(with_waits, grid_spec=pltpu.PrefetchScalarGridSpec(num_sca...]
    all_gather x6 -> x0, blocking collectives: 224 us -> none  [the longest x1 69.1 us: body(): lax.all_gather(patch_bias, ('fsdp', 'tensor'), axis=1, tiled=True)]
    ppermute x0 -> x44, waiting for transfers between devices: none -> 206 us  [swap(): return lax.ppermute(array, axis, [(i, i ^ 1 << bit) for i in range(size)])]
    ppermute x0 -> x44, starting transfers between devices: none -> 52 us  [swap(): return lax.ppermute(array, axis, [(i, i ^ 1 << bit) for i in range(size)])]
  transfers between devices with their start and end apart: 21 -> 49, of which waited for: 18 -> 17; matrix products, arithmetic and copies ran while one was open for 8% -> 15% of each run, Pallas kernels for 0% -> 38%
where the time goes in v1:
time: 683 us; the launch traced here: 676 us
  Pallas kernels  296 us (43%)
  waiting for transfers between devices  206 us (30%)
  other arithmetic  73.5 us (11%)
  starting transfers between devices  52.4 us (8%)
  local copies, waits for them, and re-layouts  32.4 us (5%)
  between operations  15.1 us (2%)
    pallas_call x21, Pallas kernels, call(): pl.pallas_call(with_waits, grid_spec=pltpu.PrefetchScalarGridSpec(num_sca...  296 us
    ppermute x44, waiting for transfers between devices, swap(): return lax.ppermute(array, axis, [(i, i ^ 1 << bit) for i in range(size)])  206 us
    ppermute x44, starting transfers between devices, swap(): return lax.ppermute(array, axis, [(i, i ^ 1 << bit) for i in range(size)])  52 us
    convert_element_type x12, other arithmetic, next_swap(): (take(keep, at).astype(F32) + take(came, at).astype(F32)).astype(keep.dtype)  32.1 us
    sin x1, local copies, waits for them, and re-layouts, body(): f(angles[:, i * quarter:(i + 1) * quarter])  14.6 us
  transfers between devices with their start and end apart: 49, of which 17 were waited for; matrix products, arithmetic and copies ran while one was open for 15% of the time, Pallas kernels for 38%

profile of v1, /device:TPU:8, one launch (start us, length us, event | category | flops | bytes accessed | tf_op | source)
XLA Modules:
  0.0 675.6 jit_solution(12220393917411522239)
XLA Ops:
  10.5 6.6 collective-permute-done
  20.0 26.8 %collective-permute-done.1 = bf16[64,3072]{1,0:T(8,128)(2,1)S(1)} collective-permute-done((bf16[64,3072]{1,0:T(8,128)(2,1)S(1)}, bf16[64,3072]{1,0:T(8,128)(2,1)S(1)}, u32[]{:S(2)}, u32[]{:S(2)}) %collective-permute-start.1) | collective-permute-done | bytes 393248 | tf_op jit(solution)/shard_map/ppermute | solution.py:668
  48.6 10.7 %collective-permute-done.13 = bf16[4,128,256]{2,1,0:T(8,128)(2,1)S(1)} collective-permute-done((bf16[4,128,256]{2,1,0:T(8,128)(2,1)S(1)}, bf16[4,128,256]{2,1,0:T(8,128)(2,1)S(1)}, u32[]{:S(2)}, u32[]{:S(2)}) %collective-permute-start.13) | collective-permute-done | bytes 262176 | tf_op jit(solution)/shard_map/ppermute | solution.py:668
  59.4 9.9 %collective-permute-start.14 = (bf16[4,128,512]{2,1,0:T(8,128)(2,1)S(1)}, bf16[4,128,512]{2,1,0:T(8,128)(2,1)S(1)}, u32[]{:S(2)}, u32[]{:S(2)}) collective-permute-start(bf16[4,128,512]{2,1,0:T(8,128)(2,1)S(1)} %maximum_select_fusion.10), channel_id=1, source_target_pairs={{0,2},{1,3},{2,0},{3,1},{4,6},{5,7},{6,4},{7,5},{8,10},{9,11},{10,... | collective-permute-start | bytes 1572872 | tf_op jit(solution)/shard_map/ppermute | solution.py:668
  71.2 26.7 %collective-permute-done.14 = bf16[4,128,512]{2,1,0:T(8,128)(2,1)S(1)} collective-permute-done((bf16[4,128,512]{2,1,0:T(8,128)(2,1)S(1)}, bf16[4,128,512]{2,1,0:T(8,128)(2,1)S(1)}, u32[]{:S(2)}, u32[]{:S(2)}) %collective-permute-start.14) | collective-permute-done | bytes 524320 | tf_op jit(solution)/shard_map/ppermute | solution.py:668
  107.8 15.3 %collective-permute-done.18 = bf16[2,1,1,128,1024]{4,3,0,2,1:T(8,128)(2,1)S(1)} collective-permute-done((bf16[2,1,1,128,1024]{4,3,0,2,1:T(8,128)(2,1)S(1)}, bf16[2,1,1,128,1024]{4,3,0,2,1:T(8,128)(2,1)S(1)}, u32[]{:S(2)}, u32[]{:S(2)}) %collective-permute-start.18) | collective-permute-done | bytes 524320 | tf_op jit(solution)/shard_map/ppermute | solution.py:668
  130.8 12.0 %collective-permute-done.7 = bf16[1,1,128,1536]{3,2,1,0:T(8,128)(2,1)S(1)} collective-permute-done((bf16[1,1,128,1536]{3,2,1,0:T(8,128)(2,1)S(1)}, bf16[1,1,128,1536]{3,2,1,0:T(8,128)(2,1)S(1)}, u32[]{:S(2)}, u32[]{:S(2)}) %collective-permute-start.7) | collective-permute-done | bytes 393248 | tf_op jit(solution)/shard_map/ppermute | solution.py:668
  143.2 25.5 %collective-permute-done.11 = bf16[2,1,128,1536]{3,2,1,0:T(8,128)(2,1)S(1)} collective-permute-done((bf16[2,1,128,1536]{3,2,1,0:T(8,128)(2,1)S(1)}, bf16[2,1,128,1536]{3,2,1,0:T(8,128)(2,1)S(1)}, u32[]{:S(2)}, u32[]{:S(2)}) %collective-permute-start.11) | collective-permute-done | bytes 786464 | tf_op jit(solution)/shard_map/ppermute | solution.py:668
  170.1 20.5 %collective-permute-done.19 = bf16[2,2,1,128,1024]{4,3,0,2,1:T(8,128)(2,1)S(1)} collective-permute-done((bf16[2,2,1,128,1024]{4,3,0,2,1:T(8,128)(2,1)S(1)}, bf16[2,2,1,128,1024]{4,3,0,2,1:T(8,128)(2,1)S(1)}, u32[]{:S(2)}, u32[]{:S(2)}) %collective-permute-start.19) | collective-permute-done | bytes 1048608 | tf_op jit(solution)/shard_map/ppermute | solution.py:668
  196.0 14.6 %slice_sine_fusion.1 = (f32[1024,256]{1,0:T(8,128)S(1)}, f32[1024,256]{1,0:T(8,128)}, f32[1024,256]{1,0:T(8,128)}, f32[1024,256]{1,0:T(8,128)}) fusion(f32[1024,1024]{1,0:T(8,128)S(1)} %broadcast_multiply_fusion), kind=kLoop, calls=%fused_computation.32 | loop fusion | bytes 8388608 | tf_op jit(solution)/shard_map/sin | solution.py:797
  227.9 12.5 %shard_map.238 = (f32[1024,1024]{1,0:T(8,128)}, bf16[1024,1024]{1,0:T(8,128)(2,1)}) custom-call(s32[16]{0:T(128)} %reshape.570.refs_0_, bf16[1024,768]{1,0:T(8,128)(2,1)} %refs_2_.3, s32[1024,1]{1,0:T(8,128)} %copy.117.refs_2_.refs_5_.refs_3_, f32[1024,1024]{1,0:T(8,128)} %pad_maximum_fusion.refs_3_, f32[4,1024]{1,0:T(4,128)} %slice.179.refs_4_, ...), custom_call_target="tpu_custom_call" | custom-call | flops 3221225472 | bytes 18378752 | tf_op jit(solution)/shard_map/pallas_call | solution.py:64
  240.5 11.0 %shard_map.239 = (bf16[1024,1024]{1,0:T(8,128)(2,1)}, bf16[1024,1024]{1,0:T(8,128)(2,1)}, bf16[1024,1024]{1,0:T(8,128)(2,1)}) custom-call(bf16[1024,1024]{1,0:T(8,128)(2,1)} %get-tuple-element.69.refs_0_, bf16[2,4,128,1024]{3,2,1,0:T(8,128)(2,1)} %bitcast.11.refs_1_.refs_7_, bf16[2,4,128,1024]{3,2,1,0:T(8,128)(2,1)} %collective-permute-done.17.refs_2_.refs_8_, ...), custom_call_target="tpu_custom_call" | custom-call | flops 6442450944 | bytes 16785408 | tf_op jit(solution)/shard_map/pallas_call | solution.py:64
  251.5 36.4 %shard_map.240 = (bf16[1024,1024]{1,0:T(8,128)(2,1)}, f32[1024,128]{1,0:T(8,128)}) custom-call(bf16[1024,1024]{1,0:T(8,128)(2,1)} %get-tuple-element.71.refs_0_, bf16[1024,1024]{1,0:T(8,128)(2,1)} %get-tuple-element.72.refs_1_, bf16[1024,1024]{1,0:T(8,128)(2,1)} %get-tuple-element.73.refs_2_, s32[1024,1]{1,0:T(8,128)} %copy.123.refs_3_.refs_4_, ...), custom_call_target="tpu_custom_call" | custom-call | flops 17179869184 | bytes 8921088 | tf_op jit(solution)/shard_map/pallas_call | solution.py:64
  287.8 8.1 %shard_map.241 = (f32[1024,1024]{1,0:T(8,128)}, bf16[1024,1024]{1,0:T(8,128)(2,1)}) custom-call(bf16[1024,1024]{1,0:T(8,128)(2,1)} %get-tuple-element.74.refs_0_.refs_4_.refs_5_, f32[1024,1024]{1,0:T(8,128)} %get-tuple-element.75.refs_1_.refs_4_, f32[1,1024]{1,0:T(1,128)} %get-tuple-element.201.refs_2_, f32[1,1024]{1,0:T(1,128)} %get-tuple-element.200.refs_3_.refs_5_, ...), custom_call_target="tpu_custom_call" | custom-call | flops 2147483648 | bytes 16789504 | tf_op jit(solution)/shard_map/pallas_call | solution.py:64
  295.9 37.4 %shard_map.244 = (f32[1024,1024]{1,0:T(8,128)}, f32[1024,1024]{1,0:T(8,128)}, bf16[4,4,2,128,512]{4,3,2,1,0:T(8,128)(2,1)}, bf16[4,4,2,128,512]{4,3,2,1,0:T(8,128)(2,1)}, f32[4,1,512]{2,1,0:T(1,128)}) custom-call(s32[1]{0:T(128)} %bitcast.refs_0_, bf16[1024,1024]{1,0:T(8,128)(2,1)} %get-tuple-element.77.refs_1_, bf16[1024,1024]{1,0:T(8,128)(2,1)} %shard_map.242.refs_2_, ...), custom_call_target="tpu_custom_call" | custom-call | flops 25769803776 | bytes 88096768 | tf_op jit(solution)/shard_map/pallas_call | solution.py:64
  333.3 37.7 %shard_map.243 = (f32[1024,1024]{1,0:T(8,128)}, f32[1024,1024]{1,0:T(8,128)}, bf16[4,4,2,128,512]{4,3,2,1,0:T(8,128)(2,1)}, bf16[4,4,2,128,512]{4,3,2,1,0:T(8,128)(2,1)}, f32[4,1,512]{2,1,0:T(1,128)}) custom-call(s32[1]{0:T(128)} %bitcast.refs_0_, bf16[1024,1024]{1,0:T(8,128)(2,1)} %get-tuple-element.77.refs_1_, bf16[1024,1024]{1,0:T(8,128)(2,1)} %shard_map.242.refs_2_, ...), custom_call_target="tpu_custom_call" | custom-call | flops 25769803776 | bytes 88096768 | tf_op jit(solution)/shard_map/pallas_call | solution.py:64
  385.8 17.8 %shard_map.246 = (f32[1024,1024]{1,0:T(8,128)}, bf16[1024,1024]{1,0:T(8,128)(2,1)}, bf16[1024,1024]{1,0:T(8,128)(2,1)}, f32[16,1024]{1,0:T(8,128)}, f32[8,1024]{1,0:T(8,128)}) custom-call(f32[1024,1024]{1,0:T(8,128)} %get-tuple-element.80.refs_0_, f32[1024,1024]{1,0:T(8,128)} %get-tuple-element.81.refs_1_, bf16[1024,1024]{1,0:T(8,128)(2,1)} %shard_map.242.refs_2_, ...), custom_call_target="tpu_custom_call" | custom-call | flops 2147483648 | bytes 29528064 | tf_op jit(solution)/shard_map/pallas_call | solution.py:64
  403.7 14.4 %shard_map.248 = (bf16[1024,256]{1,0:T(8,128)(2,1)}, bf16[1024,256]{1,0:T(8,128)(2,1)}, bf16[1024,256]{1,0:T(8,128)(2,1)}, f32[2,256]{1,0:T(2,128)}) custom-call(bf16[1024,1024]{1,0:T(8,128)(2,1)} %get-tuple-element.71.refs_0_, bf16[1024,1024]{1,0:T(8,128)(2,1)} %get-tuple-element.72.refs_1_, bf16[1024,1024]{1,0:T(8,128)(2,1)} %get-tuple-element.73.refs_2_, ...), custom_call_target="tpu_custom_call" | custom-call | flops 10737418240 | bytes 10102784 | tf_op jit(solution)/shard_map/pallas_call | solution.py:64
  418.1 14.7 %shard_map.247 = (bf16[1024,256]{1,0:T(8,128)(2,1)}, bf16[1024,256]{1,0:T(8,128)(2,1)}, bf16[1024,256]{1,0:T(8,128)(2,1)}, f32[2,256]{1,0:T(2,128)}) custom-call(bf16[1024,1024]{1,0:T(8,128)(2,1)} %get-tuple-element.71.refs_0_, bf16[1024,1024]{1,0:T(8,128)(2,1)} %get-tuple-element.72.refs_1_, bf16[1024,1024]{1,0:T(8,128)(2,1)} %get-tuple-element.73.refs_2_, ...), custom_call_target="tpu_custom_call" | custom-call | flops 10737418240 | bytes 10102784 | tf_op jit(solution)/shard_map/pallas_call | solution.py:64
  437.2 10.4 %shard_map.250 = (bf16[4,2,4,128,256]{4,3,2,1,0:T(8,128)(2,1)}, bf16[4,2,4,128,256]{4,3,2,1,0:T(8,128)(2,1)}) custom-call(bf16[1024,1024]{1,0:T(8,128)(2,1)} %get-tuple-element.69.refs_0_, bf16[1024,1024]{1,0:T(8,128)(2,1)} %get-tuple-element.91.refs_1_, bf16[1024,512]{1,0:T(8,128)(2,1)} %pad_maximum_fusion.4.refs_2_, ...), custom_call_target="tpu_custom_call" | custom-call | flops 4294967296 | bytes 13631488 | tf_op jit(solution)/shard_map/pallas_call | solution.py:64
  447.6 14.7 %shard_map.249 = (bf16[1024,256]{1,0:T(8,128)(2,1)}, bf16[1024,256]{1,0:T(8,128)(2,1)}, bf16[1024,256]{1,0:T(8,128)(2,1)}, f32[2,256]{1,0:T(2,128)}) custom-call(bf16[1024,1024]{1,0:T(8,128)(2,1)} %get-tuple-element.71.refs_0_, bf16[1024,1024]{1,0:T(8,128)(2,1)} %get-tuple-element.72.refs_1_, bf16[1024,1024]{1,0:T(8,128)(2,1)} %get-tuple-element.73.refs_2_, ...), custom_call_target="tpu_custom_call" | custom-call | flops 10737418240 | bytes 10102784 | tf_op jit(solution)/shard_map/pallas_call | solution.py:64
  468.6 14.8 %shard_map.251 = (bf16[1024,256]{1,0:T(8,128)(2,1)}, bf16[1024,256]{1,0:T(8,128)(2,1)}, bf16[1024,256]{1,0:T(8,128)(2,1)}, f32[2,256]{1,0:T(2,128)}) custom-call(bf16[1024,1024]{1,0:T(8,128)(2,1)} %get-tuple-element.71.refs_0_, bf16[1024,1024]{1,0:T(8,128)(2,1)} %get-tuple-element.72.refs_1_, bf16[1024,1024]{1,0:T(8,128)(2,1)} %get-tuple-element.73.refs_2_, ...), custom_call_target="tpu_custom_call" | custom-call | flops 10737418240 | bytes 10102784 | tf_op jit(solution)/shard_map/pallas_call | solution.py:64
  487.3 5.9 collective-permute-done.26.refs_6_
  494.2 10.5 %shard_map.252 = (bf16[4,2,4,128,256]{4,3,2,1,0:T(8,128)(2,1)}, bf16[4,2,4,128,256]{4,3,2,1,0:T(8,128)(2,1)}) custom-call(bf16[1024,1024]{1,0:T(8,128)(2,1)} %get-tuple-element.69.refs_0_, bf16[1024,1024]{1,0:T(8,128)(2,1)} %get-tuple-element.91.refs_1_, bf16[1024,512]{1,0:T(8,128)(2,1)} %get-tuple-element.215.refs_2_, ...), custom_call_target="tpu_custom_call" | custom-call | flops 4294967296 | bytes 13631488 | tf_op jit(solution)/shard_map/pallas_call | solution.py:64
  518.7 15.7 %collective-permute-done.40 = bf16[2,1,2,4,128,256]{5,4,3,2,1,0:T(8,128)(2,1)} collective-permute-done((bf16[2,1,2,4,128,256]{5,4,3,2,1,0:T(8,128)(2,1)}, bf16[2,1,2,4,128,256]{5,4,3,2,1,0:T(8,128)(2,1)}, u32[]{:S(2)}, u32[]{:S(2)}) %collective-permute-start.40) | collective-permute-done | bytes 1048608 | tf_op jit(solution)/shard_map/ppermute | solution.py:668
  537.0 16.1 %shard_map.253 = (bf16[1024,1024]{1,0:T(8,128)(2,1)}, f32[8,1024]{1,0:T(8,128)}) custom-call(bf16[1024,1024]{1,0:T(8,128)(2,1)} %get-tuple-element.213.refs_0_, bf16[1024,1024]{1,0:T(8,128)(2,1)} %get-tuple-element.214.refs_1_, bf16[1024,1024]{1,0:T(8,128)(2,1)} %pad_maximum_fusion.3.refs_2_, f32[1024,1024]{1,0:T(8,128)} %get-tuple-element.103.refs_3_, ...), custom_call_target="tpu_custom_call" | custom-call | flops 6442450944 | bytes 25206784 | tf_op jit(solution)/shard_map/pallas_call | solution.py:64
  553.1 8.1 %shard_map.255 = (bf16[512,1536]{1,0:T(8,128)(2,1)}, bf16[512,1536]{1,0:T(8,128)(2,1)}) custom-call(s32[16]{0:T(128)} %reshape.570.refs_0_, bf16[1024,1024]{1,0:T(8,128)(2,1)} %get-tuple-element.105.refs_1_, bf16[1024,768]{1,0:T(8,128)(2,1)} %refs_2_.3, s32[1024,1]{1,0:T(8,128)} %copy.117.refs_2_.refs_5_.refs_3_), custom_call_target="tpu_custom_call" | custom-call | flops 1610612736 | bytes 6819840 | tf_op jit(solution)/shard_map/pallas_call | solution.py:64
  566.4 7.3 %shard_map.256 = (bf16[512,1536]{1,0:T(8,128)(2,1)}, bf16[512,1536]{1,0:T(8,128)(2,1)}) custom-call(s32[16]{0:T(128)} %reshape.570.refs_0_, bf16[1024,1024]{1,0:T(8,128)(2,1)} %get-tuple-element.105.refs_1_, bf16[1024,768]{1,0:T(8,128)(2,1)} %refs_2_.3, s32[1024,1]{1,0:T(8,128)} %copy.117.refs_2_.refs_5_.refs_3_), custom_call_target="tpu_custom_call" | custom-call | flops 1610612736 | bytes 6819840 | tf_op jit(solution)/shard_map/pallas_call | solution.py:64
  579.8 11.0 %collective-permute-done.42 = bf16[1,2,2,4,128,256]{5,4,3,2,1,0:T(8,128)(2,1)} collective-permute-done((bf16[1,2,2,4,128,256]{5,4,3,2,1,0:T(8,128)(2,1)}, bf16[1,2,2,4,128,256]{5,4,3,2,1,0:T(8,128)(2,1)}, u32[]{:S(2)}, u32[]{:S(2)}) %collective-permute-start.42) | collective-permute-done | bytes 1048608 | tf_op jit(solution)/shard_map/ppermute | solution.py:668
  609.3 13.2 %collective-permute-done.30 = bf16[2,1,4,32,1536]{4,3,2,1,0:T(8,128)(2,1)} collective-permute-done((bf16[2,1,4,32,1536]{4,3,2,1,0:T(8,128)(2,1)}, bf16[2,1,4,32,1536]{4,3,2,1,0:T(8,128)(2,1)}, u32[]{:S(2)}, u32[]{:S(2)}) %collective-permute-start.30) | collective-permute-done | bytes 786464 | tf_op jit(solution)/shard_map/ppermute | solution.py:668
  643.1 7.6 %shard_map.245 = f32[1024,1024]{1,0:T(8,128)} custom-call(s32[1]{0:T(128)} %bitcast.refs_0_, f32[1024,1024]{1,0:T(8,128)} %get-tuple-element.76.refs_1_.refs_3_, f32[1024,1024]{1,0:T(8,128)} %get-tuple-element.78.refs_2_, f32[1024,1024]{1,0:T(8,128)} %get-tuple-element.79.refs_3_, f32[1,1024]{1,0:T(1,128)} %get-tuple-element.198.refs_4_), custom_call_target="tpu_custom_call" | custom-call | bytes 16781312 | tf_op jit(solution)/shard_map/pallas_call | solution.py:64
  652.9 9.2 %shard_map.254 = f32[1024,768]{1,0:T(8,128)} custom-call(s32[16]{0:T(128)} %reshape.570.refs_0_, bf16[1024,1024]{1,0:T(8,128)(2,1)} %get-tuple-element.105.refs_1_, s32[1024,1]{1,0:T(8,128)} %copy.117.refs_2_.refs_5_.refs_3_, bf16[4,128,1536]{2,1,0:T(8,128)(2,1)} %bitcast.5.refs_7_.refs_3_, bf16[4,128,1536]{2,1,0:T(8,128)(2,1)} %collective-permute-done.9.refs_8_.refs_4_, ...), custom_call_target="tpu_custom_call" | custom-call | flops 3221225472 | bytes 11538432 | tf_op jit(solution)/shard_map/pallas_call | solution.py:64
  (327 shorter events, 157.2 us)
Async XLA Ops:
  7.2 288.7 %all-gather.3.cloned.1.call-start = ((), (), s32[]{:S(2)}) async-start(), calls=%async_computation.8 | async-start | bytes 17301504 | tf_op jit(solution)/shard_map/all_gather | solution.py:748
  10.3 640.4 %reduce-scatter.11.cloned.1.call-start = ((), (), s32[]{:S(2)}) async-start(), calls=%async_computation.7 | async-start | bytes 1310720 | tf_op jit(solution)/shard_map/reduce_scatter | solution.py:730
  17.1 29.7 %collective-permute-start.1 = (bf16[64,3072]{1,0:T(8,128)(2,1)S(1)}, bf16[64,3072]{1,0:T(8,128)(2,1)S(1)}, u32[]{:S(2)}, u32[]{:S(2)}) collective-permute-start(bf16[64,3072]{1,0:T(8,128)(2,1)S(1)} %maximum_select_fusion.11), channel_id=1, source_target_pairs={{0,2},{1,3},{2,0},{3,1},{4,6},{5,7},{6,4},{7,5},{8,10},{9,11},{10,... | collective-permute-start | bytes 1179656 | tf_op jit(solution)/shard_map/ppermute | solution.py:668
  59.4 38.5 %collective-permute-start.14 = (bf16[4,128,512]{2,1,0:T(8,128)(2,1)S(1)}, bf16[4,128,512]{2,1,0:T(8,128)(2,1)S(1)}, u32[]{:S(2)}, u32[]{:S(2)}) collective-permute-start(bf16[4,128,512]{2,1,0:T(8,128)(2,1)S(1)} %maximum_select_fusion.10), channel_id=1, source_target_pairs={{0,2},{1,3},{2,0},{3,1},{4,6},{5,7},{6,4},{7,5},{8,10},{9,11},{10,... | collective-permute-start | bytes 1572872 | tf_op jit(solution)/shard_map/ppermute | solution.py:668
  69.5 36.6 %collective-permute-start.10 = (bf16[1,1,128,1536]{3,2,1,0:T(8,128)(2,1)S(1)}, bf16[1,1,128,1536]{3,2,1,0:T(8,128)(2,1)S(1)}, u32[]{:S(2)}, u32[]{:S(2)}) collective-permute-start(bf16[1,1,128,1536]{3,2,1,0:T(8,128)(2,1)S(1)} %get-tuple-element.196), channel_id=1, source_target_pairs={{0,16},{4,20},{8,24},{12,28},{16,0},{20,4},{24,8},{28,12},{1,17},{... | collective-permute-start | bytes 1179656 | tf_op jit(solution)/shard_map/ppermute | solution.py:668
  100.0 26.0 %collective-permute-start.15 = (bf16[2,1,1,128,1024]{4,3,0,2,1:T(8,128)(2,1)S(1)}, bf16[2,1,1,128,1024]{4,3,0,2,1:T(8,128)(2,1)S(1)}, u32[]{:S(2)}, u32[]{:S(2)}) collective-permute-start(bf16[2,1,1,128,1024]{4,3,0,2,1:T(8,128)(2,1)S(1)} %get-tuple-element.195), channel_id=1, source_target_pairs={{0,8},{4,12},{8,0},{12,4},{16,24},{20,28},{24,16},{28,20},{1,9},{5... | collective-permute-start | bytes 1572872 | tf_op jit(solution)/shard_map/ppermute | solution.py:668
  101.5 25.3 %collective-permute-start.2 = (bf16[1,512]{1,0:T(2,128)(2,1)S(1)}, bf16[1,512]{1,0:T(2,128)(2,1)S(1)}, u32[]{:S(2)}, u32[]{:S(2)}) collective-permute-start(bf16[1,512]{1,0:T(2,128)(2,1)S(1)} %broadcast_in_dim.14), channel_id=1, source_target_pairs={{0,1},{1,0},{2,3},{3,2},{4,5},{5,4},{6,7},{7,6},{8,9},{9,8},{10,11... | collective-permute-start | bytes 3080 | tf_op jit(solution)/shard_map/ppermute | solution.py:668
  105.6 37.2 %collective-permute-start.7 = (bf16[1,1,128,1536]{3,2,1,0:T(8,128)(2,1)S(1)}, bf16[1,1,128,1536]{3,2,1,0:T(8,128)(2,1)S(1)}, u32[]{:S(2)}, u32[]{:S(2)}) collective-permute-start(bf16[1,1,128,1536]{3,2,1,0:T(8,128)(2,1)S(1)} %get-tuple-element.197), channel_id=1, source_target_pairs={{0,8},{4,12},{8,0},{12,4},{16,24},{20,28},{24,16},{28,20},{1,9},{5... | collective-permute-start | bytes 1179656 | tf_op jit(solution)/shard_map/ppermute | solution.py:668
  106.2 62.4 %collective-permute-start.11 = (bf16[2,1,128,1536]{3,2,1,0:T(8,128)(2,1)S(1)}, bf16[2,1,128,1536]{3,2,1,0:T(8,128)(2,1)S(1)}, u32[]{:S(2)}, u32[]{:S(2)}) collective-permute-start(bf16[2,1,128,1536]{3,2,1,0:T(8,128)(2,1)S(1)} %maximum_select_fusion.9), channel_id=1, source_target_pairs={{0,8},{4,12},{8,0},{12,4},{16,24},{20,28},{24,16},{28,20},{1,9},{5... | collective-permute-start | bytes 2359304 | tf_op jit(solution)/shard_map/ppermute | solution.py:668
  123.3 67.3 %collective-permute-start.19 = (bf16[2,2,1,128,1024]{4,3,0,2,1:T(8,128)(2,1)S(1)}, bf16[2,2,1,128,1024]{4,3,0,2,1:T(8,128)(2,1)S(1)}, u32[]{:S(2)}, u32[]{:S(2)}) collective-permute-start(bf16[2,2,1,128,1024]{4,3,0,2,1:T(8,128)(2,1)S(1)} %maximum_select_fusion.6), channel_id=1, source_target_pairs={{0,8},{4,12},{8,0},{12,4},{16,24},{20,28},{24,16},{28,20},{1,9},{5... | collective-permute-start | bytes 3145736 | tf_op jit(solution)/shard_map/ppermute | solution.py:668
  126.1 65.0 %collective-permute-start.16 = (bf16[2,1,2,128,1024]{4,3,0,2,1:T(8,128)(2,1)S(1)}, bf16[2,1,2,128,1024]{4,3,0,2,1:T(8,128)(2,1)S(1)}, u32[]{:S(2)}, u32[]{:S(2)}) collective-permute-start(bf16[2,1,2,128,1024]{4,3,0,2,1:T(8,128)(2,1)S(1)} %maximum_select_fusion.5), channel_id=1, source_target_pairs={{0,16},{4,20},{8,24},{12,28},{16,0},{20,4},{24,8},{28,12},{1,17},{... | collective-permute-start | bytes 3145736 | tf_op jit(solution)/shard_map/ppermute | solution.py:668
  142.9 51.1 %collective-permute-start.8 = (bf16[1,2,128,1536]{3,2,1,0:T(8,128)(2,1)S(1)}, bf16[1,2,128,1536]{3,2,1,0:T(8,128)(2,1)S(1)}, u32[]{:S(2)}, u32[]{:S(2)}) collective-permute-start(bf16[1,2,128,1536]{3,2,1,0:T(8,128)(2,1)S(1)} %maximum_select_fusion.8), channel_id=1, source_target_pairs={{0,16},{4,20},{8,24},{12,28},{16,0},{20,4},{24,8},{28,12},{1,17},{... | collective-permute-start | bytes 2359304 | tf_op jit(solution)/shard_map/ppermute | solution.py:668
  143.1 67.5 %collective-permute-start.4 = (bf16[4,512]{1,0:T(4,128)(2,1)S(1)}, bf16[4,512]{1,0:T(4,128)(2,1)S(1)}, u32[]{:S(2)}, u32[]{:S(2)}) collective-permute-start(bf16[4,512]{1,0:T(4,128)(2,1)S(1)} %maximum_select_fusion.17), channel_id=1, source_target_pairs={{0,4},{4,0},{8,12},{12,8},{16,20},{20,16},{24,28},{28,24},{1,5},{5... | collective-permute-start | bytes 12296 | tf_op jit(solution)/shard_map/ppermute | solution.py:668
  170.1 57.9 %collective-permute-start.12 = (bf16[4,128,1536]{2,1,0:T(8,128)(2,1)}, bf16[4,128,1536]{2,1,0:T(8,128)(2,1)}, u32[]{:S(2)}, u32[]{:S(2)}) collective-permute-start(bf16[4,128,1536]{2,1,0:T(8,128)(2,1)} %bitcast.7.refs_9_.refs_5_), channel_id=1, source_target_pairs={{0,4},{4,0},{8,12},{12,8},{16,20},{20,16},{24,28},{28,24},{1,5},{5... | collective-permute-start | bytes 4718600 | tf_op jit(solution)/shard_map/ppermute | solution.py:668
  191.1 49.4 %collective-permute-start.20 = (bf16[2,4,128,1024]{3,2,1,0:T(8,128)(2,1)S(1)}, bf16[2,4,128,1024]{3,2,1,0:T(8,128)(2,1)}, u32[]{:S(2)}, u32[]{:S(2)}) collective-permute-start(bf16[2,4,128,1024]{3,2,1,0:T(8,128)(2,1)S(1)} %bitcast.97), channel_id=1, source_target_pairs={{0,4},{4,0},{8,12},{12,8},{16,20},{20,16},{24,28},{28,24},{1,5},{5... | collective-permute-start | bytes 6291464 | tf_op jit(solution)/shard_map/ppermute | solution.py:668
  194.0 46.5 %collective-permute-start.17 = (bf16[2,4,128,1024]{3,2,1,0:T(8,128)(2,1)}, bf16[2,4,128,1024]{3,2,1,0:T(8,128)(2,1)}, u32[]{:S(2)}, u32[]{:S(2)}) collective-permute-start(bf16[2,4,128,1024]{3,2,1,0:T(8,128)(2,1)} %bitcast.11.refs_1_.refs_7_), channel_id=1, source_target_pairs={{0,4},{4,0},{8,12},{12,8},{16,20},{20,16},{24,28},{28,24},{1,5},{5... | collective-permute-start | bytes 6291464 | tf_op jit(solution)/shard_map/ppermute | solution.py:668
  195.4 32.5 %collective-permute-start.9 = (bf16[4,128,1536]{2,1,0:T(8,128)(2,1)}, bf16[4,128,1536]{2,1,0:T(8,128)(2,1)}, u32[]{:S(2)}, u32[]{:S(2)}) collective-permute-start(bf16[4,128,1536]{2,1,0:T(8,128)(2,1)} %bitcast.5.refs_7_.refs_3_), channel_id=1, source_target_pairs={{0,4},{4,0},{8,12},{12,8},{16,20},{20,16},{24,28},{28,24},{1,5},{5... | collective-permute-start | bytes 4718600 | tf_op jit(solution)/shard_map/ppermute | solution.py:668
  333.3 39.8 %collective-permute-start.22 = (bf16[4,4,2,128,512]{4,3,2,1,0:T(8,128)(2,1)}, bf16[4,4,2,128,512]{4,3,2,1,0:T(8,128)(2,1)}, u32[]{:S(2)}, u32[]{:S(2)}) collective-permute-start(bf16[4,4,2,128,512]{4,3,2,1,0:T(8,128)(2,1)} %get-tuple-element.86), channel_id=1, source_target_pairs={{0,4},{4,0},{8,12},{12,8},{16,20},{20,16},{24,28},{28,24},{1,5},{5... | collective-permute-start | bytes 12582920 | tf_op jit(solution)/shard_map/ppermute | solution.py:668
  378.4 84.0 %collective-permute-start.23 = (bf16[2,1,4,2,128,512]{5,4,3,2,1,0:T(8,128)(2,1)S(1)}, bf16[2,1,4,2,128,512]{5,4,3,2,1,0:T(8,128)(2,1)}, u32[]{:S(2)}, u32[]{:S(2)}) collective-permute-start(bf16[2,1,4,2,128,512]{5,4,3,2,1,0:T(8,128)(2,1)S(1)} %get-tuple-element.179), channel_id=1, source_target_pairs={{0,8},{4,12},{8,0},{12,4},{16,24},{20,28},{24,16},{28,20},{1,9},{5... | collective-permute-start | bytes 6291464 | tf_op jit(solution)/shard_map/ppermute | solution.py:668
  385.2 52.0 %collective-permute-start.24 = (bf16[1,2,4,2,128,512]{5,4,3,2,1,0:T(8,128)(2,1)}, bf16[1,2,4,2,128,512]{5,4,3,2,1,0:T(8,128)(2,1)}, u32[]{:S(2)}, u32[]{:S(2)}) collective-permute-start(bf16[1,2,4,2,128,512]{5,4,3,2,1,0:T(8,128)(2,1)} %get-tuple-element.181), channel_id=1, source_target_pairs={{0,16},{4,20},{8,24},{12,28},{16,0},{20,4},{24,8},{28,12},{1,17},{... | collective-permute-start | bytes 6291464 | tf_op jit(solution)/shard_map/ppermute | solution.py:668
  464.9 44.3 %collective-permute-start.28 = (bf16[1,1,4,2,128,512]{5,4,3,2,1,0:T(8,128)(2,1)}, bf16[1,1,4,2,128,512]{5,4,3,2,1,0:T(8,128)(2,1)S(1)}, u32[]{:S(2)}, u32[]{:S(2)}) collective-permute-start(bf16[1,1,4,2,128,512]{5,4,3,2,1,0:T(8,128)(2,1)} %add_convert_fusion.12), channel_id=1, source_target_pairs={{0,16},{4,20},{8,24},{12,28},{16,0},{20,4},{24,8},{28,12},{1,17},{... | collective-permute-start | bytes 3145736 | tf_op jit(solution)/shard_map/ppermute | solution.py:668
  467.9 25.3 %collective-permute-start.26 = (bf16[1,1,4,2,128,512]{5,4,3,2,1,0:T(8,128)(2,1)S(1)}, bf16[1,1,4,2,128,512]{5,4,3,2,1,0:T(8,128)(2,1)S(1)}, u32[]{:S(2)}, u32[]{:S(2)}) collective-permute-start(bf16[1,1,4,2,128,512]{5,4,3,2,1,0:T(8,128)(2,1)S(1)} %add_convert_fusion.13), channel_id=1, source_target_pairs={{0,8},{4,12},{8,0},{12,4},{16,24},{20,28},{24,16},{28,20},{1,9},{5... | collective-permute-start | bytes 3145736 | tf_op jit(solution)/shard_map/ppermute | solution.py:668
  504.7 32.3 %collective-permute-start.27 = (bf16[4,2,4,128,256]{4,3,2,1,0:T(8,128)(2,1)}, bf16[4,2,4,128,256]{4,3,2,1,0:T(8,128)(2,1)}, u32[]{:S(2)}, u32[]{:S(2)}) collective-permute-start(bf16[4,2,4,128,256]{4,3,2,1,0:T(8,128)(2,1)} %get-tuple-element.104), channel_id=1, source_target_pairs={{0,4},{4,0},{8,12},{12,8},{16,20},{20,16},{24,28},{28,24},{1,5},{5... | collective-permute-start | bytes 6291464 | tf_op jit(solution)/shard_map/ppermute | solution.py:668
  508.6 25.9 %collective-permute-start.40 = (bf16[2,1,2,4,128,256]{5,4,3,2,1,0:T(8,128)(2,1)}, bf16[2,1,2,4,128,256]{5,4,3,2,1,0:T(8,128)(2,1)}, u32[]{:S(2)}, u32[]{:S(2)}) collective-permute-start(bf16[2,1,2,4,128,256]{5,4,3,2,1,0:T(8,128)(2,1)} %get-tuple-element.183), channel_id=1, source_target_pairs={{0,8},{4,12},{8,0},{12,4},{16,24},{20,28},{24,16},{28,20},{1,9},{5... | collective-permute-start | bytes 3145736 | tf_op jit(solution)/shard_map/ppermute | solution.py:668
  512.6 138.1 %reduce-scatter.9.cloned.1.call-start = ((), (), s32[]{:S(2)}) async-start(), calls=%async_computation.6 | async-start | bytes 1310720 | tf_op jit(solution)/shard_map/reduce_scatter | solution.py:730
  536.4 40.7 %collective-permute-start.41 = (bf16[1,1,2,4,128,256]{5,4,3,2,1,0:T(8,128)(2,1)}, bf16[1,1,2,4,128,256]{5,4,3,2,1,0:T(8,128)(2,1)}, u32[]{:S(2)}, u32[]{:S(2)}) collective-permute-start(bf16[1,1,2,4,128,256]{5,4,3,2,1,0:T(8,128)(2,1)} %add_convert_fusion.22), channel_id=1, source_target_pairs={{0,16},{4,20},{8,24},{12,28},{16,0},{20,4},{24,8},{28,12},{1,17},{... | collective-permute-start | bytes 1572872 | tf_op jit(solution)/shard_map/ppermute | solution.py:668
  561.2 32.1 %collective-permute-start.29 = (bf16[4,4,32,1536]{3,2,1,0:T(8,128)(2,1)}, bf16[4,4,32,1536]{3,2,1,0:T(8,128)(2,1)}, u32[]{:S(2)}, u32[]{:S(2)}) collective-permute-start(bf16[4,4,32,1536]{3,2,1,0:T(8,128)(2,1)} %bitcast.152), channel_id=1, source_target_pairs={{0,4},{4,0},{8,12},{12,8},{16,20},{20,16},{24,28},{28,24},{1,5},{5... | collective-permute-start | bytes 4718600 | tf_op jit(solution)/shard_map/ppermute | solution.py:668
  564.9 25.9 %collective-permute-start.42 = (bf16[1,2,2,4,128,256]{5,4,3,2,1,0:T(8,128)(2,1)}, bf16[1,2,2,4,128,256]{5,4,3,2,1,0:T(8,128)(2,1)}, u32[]{:S(2)}, u32[]{:S(2)}) collective-permute-start(bf16[1,2,2,4,128,256]{5,4,3,2,1,0:T(8,128)(2,1)} %get-tuple-element.185), channel_id=1, source_target_pairs={{0,16},{4,20},{8,24},{12,28},{16,0},{20,4},{24,8},{28,12},{1,17},{... | collective-permute-start | bytes 3145736 | tf_op jit(solution)/shard_map/ppermute | solution.py:668
  576.5 88.8 %reduce-scatter.7.cloned.1.call-start = ((), (), s32[]{:S(2)}) async-start(), calls=%async_computation.5 | async-start | bytes 1310720 | tf_op jit(solution)/shard_map/reduce_scatter | solution.py:730
  596.1 26.4 %collective-permute-start.30 = (bf16[2,1,4,32,1536]{4,3,2,1,0:T(8,128)(2,1)}, bf16[2,1,4,32,1536]{4,3,2,1,0:T(8,128)(2,1)}, u32[]{:S(2)}, u32[]{:S(2)}) collective-permute-start(bf16[2,1,4,32,1536]{4,3,2,1,0:T(8,128)(2,1)} %get-tuple-element.191), channel_id=1, source_target_pairs={{0,8},{4,12},{8,0},{12,4},{16,24},{20,28},{24,16},{28,20},{1,9},{5... | collective-permute-start | bytes 2359304 | tf_op jit(solution)/shard_map/ppermute | solution.py:668
  597.0 28.2 %collective-permute-start.35 = (f32[16,512]{1,0:T(8,128)S(1)}, f32[16,512]{1,0:T(8,128)S(1)}, u32[]{:S(2)}, u32[]{:S(2)}) collective-permute-start(f32[16,512]{1,0:T(8,128)S(1)} %constant_dynamic-slice_fusion.5), channel_id=1, source_target_pairs={{0,16},{4,20},{8,24},{12,28},{16,0},{20,4},{24,8},{28,12},{1,17},{... | collective-permute-start | bytes 98312 | tf_op jit(solution)/shard_map/ppermute | solution.py:668
  609.3 57.8 %reduce-scatter.5.cloned.1.call-start = ((), (), s32[]{:S(2)}) async-start(), calls=%async_computation.4 | async-start | bytes 983040 | tf_op jit(solution)/shard_map/reduce_scatter | solution.py:730
  (68 other events, 780.0 us)
Sparse Core Ops, SparseCore 0:
  11.0 169.0 all-gather.2
  512.7 25.6 reduce-scatter.10
  576.6 25.6 reduce-scatter.8
  609.4 25.7 reduce-scatter.6
  638.8 22.1 reduce-scatter.4

commit v2 on v1

v2 whole, which is shorter than its diff:
```python
import math
from functools import partial

import jax
import jax.numpy as jnp
from jax import lax
from jax.experimental import pallas as pl
from jax.experimental.pallas import tpu as pltpu
from jax.sharding import PartitionSpec as P

HEAD_DIM = 64
GROUPS = 4
LANES = 128
TILE = 256
EPSILON = 1e-06
VMEM = 56 * 1024 * 1024
F32 = jnp.float32
BF16 = jnp.bfloat16
NN = (((1,), (0,)), ((), ()))
NT = (((1,), (1,)), ((), ()))
TN = (((0,), (0,)), ((), ()))
ANY = pl.BlockSpec(memory_space=pl.ANY)


def dot(left, right, dims=NN):
    return lax.dot_general(left, right, dims, preferred_element_type=F32)


def merged(block):
    return block.reshape(-1, block.shape[-1])


def joined(refs, *mats):
    blocks = [merged(ref[:, t, mat]) for ref in refs for t in range(ref.shape[1]) for mat in mats]
    return jnp.concatenate(blocks, axis=1)


def qkv_joined(refs, mat):
    blocks = [merged(ref[:, t, ref.shape[2] - 3 + mat]) for ref in refs for t in range(ref.shape[1])]
    return jnp.concatenate(blocks, axis=1)


def beside(refs):
    return jnp.concatenate([ref[...] for ref in refs], axis=1)


def normalize(values):
    row_mean = jnp.mean(values, axis=-1, keepdims=True)
    centred = values - row_mean
    inv_scale = lax.rsqrt(jnp.mean(centred * centred, axis=-1, keepdims=True) + EPSILON)
    return (centred * inv_scale, inv_scale)


def normalize_back(grad_normed, normed, inv_scale):
    return inv_scale * (
        grad_normed
        - jnp.mean(grad_normed, axis=-1, keepdims=True)
        - normed * jnp.mean(grad_normed * normed, axis=-1, keepdims=True)
    )


def whole(shape):
    return pl.BlockSpec(shape, lambda *_: (0,) * len(shape))


def row_tile(shape):
    return pl.BlockSpec((TILE,) + shape[1:], lambda i, *_: (i,) + (0,) * (len(shape) - 1))


def call(kernel, grid, in_specs, out_specs, out_shape, args, scratch=(), flops=0, exps=0, scalars=(), after=(), filled=()):
    count = len(args)
    after = tuple(after) + tuple(array for _, array in filled)
    first = len(scalars) + len(args) + len(after) - len(filled)

    def with_waits(*refs):
        head = refs[: len(scalars) + count]
        return kernel(*head, *refs[len(scalars) + count + len(after) :])

    moved = sum(a.size * a.dtype.itemsize for a in args) + sum(math.prod(s.shape) * s.dtype.itemsize for s in out_shape)
    return pl.pallas_call(
        with_waits,
        grid_spec=pltpu.PrefetchScalarGridSpec(
            num_scalar_prefetch=len(scalars),
            grid=grid,
            in_specs=list(in_specs) + [ANY] * len(after),
            out_specs=list(out_specs),
            scratch_shapes=list(scratch),
        ),
        out_shape=list(out_shape),
        input_output_aliases={first + i: out for i, (out, _) in enumerate(filled)},
        compiler_params=pltpu.CompilerParams(vmem_limit_bytes=VMEM),
        cost_estimate=pl.CostEstimate(flops=int(flops), bytes_accessed=int(moved), transcendentals=int(exps)),
    )(*scalars, *args, *after)


def shaped(shape, dtype):
    return jax.ShapeDtypeStruct(shape, dtype)


def split_kernel(core, array, out, turned, *, wide):
    half = out.shape[1] // 2
    for place in range(half // wide):
        even = array[:, 2 * place * wide : (2 * place + 1) * wide]
        odd = array[:, (2 * place + 1) * wide : (2 * place + 2) * wide]
        at = place * wide
        out[:, at : at + wide] = jnp.where(core[0] == 0, even, odd)
        out[:, half + at : half + at + wide] = jnp.where(core[0] == 0, odd, even)
    turned[...] = out[...].T


def turned_tile(shape):
    return pl.BlockSpec((shape[1], TILE), lambda i, *_: (0, i))


def split_columns(core, array, wide):
    tile = row_tile(array.shape)
    return call(
        partial(split_kernel, wide=wide),
        (array.shape[0] // TILE,),
        [tile],
        [tile, turned_tile(array.shape)],
        [shaped(array.shape, array.dtype), shaped(array.shape[::-1], array.dtype)],
        (array,),
        scalars=(core,),
    )


def shares_kernel(expand, contract, e_low, c_low, high):
    part = e_low.shape[1]
    e_low[...] = expand[:, :part]
    c_low[...] = contract[:part, :].T
    high[0] = expand[:, part:]
    high[1] = contract[part:, :].T


def shares(expand, contract, after=()):
    wide, unit = expand.shape
    half = (wide, unit // 2)
    return call(
        shares_kernel,
        (1,),
        [whole(expand.shape), whole(contract.shape)],
        [whole(half)] * 2 + [whole((2,) + half)],
        [shaped(half, BF16)] * 2 + [shaped((2,) + half, BF16)],
        (expand, contract),
        after=after,
    )


def output_kernel(core, stream, one, two, bias, out, *, wide):
    half = out.shape[1] // 2
    total = stream[...] + one[...] + two[...] + bias[...]
    if wide % LANES:
        out[...] = total
        return
    for place in range(half // wide):
        at = place * wide
        own, other = total[:, at : at + wide], total[:, half + at : half + at + wide]
        out[:, 2 * at : 2 * at + wide] = jnp.where(core[0] == 0, own, other)
        out[:, 2 * at + wide : 2 * at + 2 * wide] = jnp.where(core[0] == 0, other, own)


def output_rows(core, stream, one, two, bias, wide, after=()):
    tile = row_tile(stream.shape)
    return call(
        partial(output_kernel, wide=wide),
        (stream.shape[0] // TILE,),
        [tile] * 3 + [whole(bias.shape)],
        [tile],
        [shaped(stream.shape, F32)],
        (stream, one, two, bias),
        scalars=(core,),
        after=after,
    )[0]


def finish_feed_kernel(blocks, expand, contract):
    expand[...] = blocks[0].astype(F32)
    contract[...] = blocks[1].astype(F32).T


def finish_feed(blocks):
    _, wide, unit = blocks.shape
    return call(
        finish_feed_kernel,
        (1,),
        [whole(blocks.shape)],
        [whole((wide, unit)), whole((unit, wide))],
        [shaped((wide, unit), F32), shaped((unit, wide), F32)],
        (blocks,),
    )


def finish_attention_kernel(blocks, attention, merge_out):
    attention[...] = blocks[:3].astype(F32)
    merge_out[...] = blocks[3].astype(F32).T


def finish_attention(blocks):
    _, wide, columns = blocks.shape
    return call(
        finish_attention_kernel,
        (1,),
        [whole(blocks.shape)],
        [whole((3, wide, columns)), whole((columns, wide))],
        [shaped((3, wide, columns), F32), shaped((columns, wide), F32)],
        (blocks,),
    )


def group_rows(band, group, values):
    return jnp.where(band == group, values, jnp.zeros_like(values))


def embed_kernel(present, pix, band, sin_own, cos_own, sin_came, cos_came, bias, gain, shift, lo_own, lo_came, hi_own, hi_came, stream, normed, turned, acc):
    tile = pl.program_id(0)
    half = acc.shape[1] // 2
    width = pix.shape[1]
    acc[...] = beside((sin_own, cos_own, sin_came, cos_came))
    for group in range(GROUPS):

        @pl.when(present[tile * GROUPS + group] > 0)
        def _():
            rows = group_rows(band[...], group, pix[...])
            at = pl.ds((group % 2) * width, width)
            own, came = (lo_own, lo_came) if group < 2 else (hi_own, hi_came)
            acc[:, :half] += dot(rows, merged(own[:, :, at]), NT)
            acc[:, half:] += dot(rows, merged(came[:, :, at]), NT)

    total = acc[...]
    for group in range(GROUPS):
        total = total + jnp.where(band[...] == group, bias[group : group + 1, :], 0.0)
    stream[...] = total
    rows = (normalize(total)[0] * gain[...] + shift[...]).astype(BF16)
    normed[...] = rows
    turned[...] = rows.T


def embed(present, pixels, band, table, bias, gain, shift, patches, after=()):
    rows, model = pixels.shape[0], gain.shape[1]
    args = (pixels, band) + table + (bias, gain, shift) + patches
    specs = [row_tile(a.shape) for a in args[:6]] + [whole(a.shape) for a in args[6:]]
    return call(
        embed_kernel,
        (rows // TILE,),
        specs,
        [row_tile((rows, model))] * 2 + [turned_tile((rows, model))],
        [shaped((rows, model), F32), shaped((rows, model), BF16), shaped((model, rows), BF16)],
        args,
        scratch=[pltpu.VMEM((TILE, model), F32)],
        flops=4 * rows * pixels.shape[1] * model,
        scalars=(present,),
        after=after,
    )


def project_kernel(x, bias, *refs):
    half = x.shape[1] // 2
    count = (len(refs) - 3) // 2
    weights, outs = refs[: 2 * count], refs[2 * count :]
    for mat, out in enumerate(outs):
        total = dot(x[:, :half], qkv_joined(weights[:count], mat)) + dot(x[:, half:], qkv_joined(weights[count:], mat))
        if mat != 1:
            total = total + bias[mat // 2 : mat // 2 + 1, :]
        out[...] = total.astype(BF16)


def project(x, own, came, bias, after=()):
    rows, model = x.shape
    width = bias.shape[1]
    weights = tuple(own) + tuple(came)
    return call(
        project_kernel,
        (rows // TILE,),
        [row_tile(x.shape), whole(bias.shape)] + [whole(w.shape) for w in weights],
        [row_tile((rows, width))] * 3,
        [shaped((rows, width), BF16)] * 3,
        (x, bias) + weights,
        flops=6 * rows * model * width,
        after=after,
    )


def head_mask(shape, head):
    lane = lax.broadcasted_iota(jnp.int32, shape, 1)
    return (lane < HEAD_DIM) if head == 0 else (lane >= HEAD_DIM)


def only_head(values, head):
    return jnp.where(head_mask(values.shape, head), values, jnp.zeros_like(values))


def attend_kernel(q_ref, k_ref, v_ref, seg_col_ref, seg_row_ref, out_ref, log_ref, bias_ref, *, base):
    pair = base + pl.program_id(0)
    rows = q_ref.shape[0]

    @pl.when(pl.program_id(0) == 0)
    def _():
        bias_ref[...] = jnp.where(seg_col_ref[...] == seg_row_ref[...], 0.0, -1e30).astype(F32)
        log_ref[...] = jnp.zeros_like(log_ref)

    keys = k_ref[...]
    value_of = [only_head(v_ref[...], head) for head in range(2)]
    for start in range(0, rows, TILE):
        at = pl.ds(start, TILE)
        query = q_ref[at, :] * jnp.asarray(HEAD_DIM ** (-0.5), BF16)
        lane = lax.broadcasted_iota(jnp.int32, (TILE, LANES), 1)
        logs = log_ref[at, :]
        total = jnp.zeros((TILE, LANES), F32)
        for head in range(2):
            scores = dot(only_head(query, head), keys, NT) + bias_ref[at, :]
            top = jnp.max(scores, axis=1, keepdims=True)
            shifted = jnp.exp(scores - top)
            mass = jnp.sum(shifted, axis=1, keepdims=True)
            total = total + dot(shifted.astype(BF16), value_of[head]) * (1.0 / mass)
            logs = jnp.where(lane == 2 * pair + head, top + jnp.log(mass), logs)
        out_ref[at, :] = total.astype(BF16)
        log_ref[at, :] = logs


def attend(query, key, value, seg, base, skip, pairs, after=()):
    rows = query.shape[0]
    width = pairs * LANES
    block = pl.BlockSpec((rows, LANES), lambda i: (0, skip + i))
    return call(
        partial(attend_kernel, base=base + skip),
        (pairs,),
        [block, block, block, whole((rows, 1)), whole((1, rows))],
        [pl.BlockSpec((rows, LANES), lambda i: (0, i)), whole((rows, LANES))],
        [shaped((rows, width), BF16), shaped((rows, LANES), F32)],
        (query, key, value) + seg,
        scratch=[pltpu.VMEM((rows, rows), F32)],
        flops=16 * rows * rows * width,
        exps=rows * rows * width // HEAD_DIM,
        after=after,
    )


def attend_back_kernel(
    q_ref, k_ref, v_ref, g_ref, seg_col_ref, seg_row_ref, log_ref, delta_ref, dq_ref, dk_ref, dv_ref, sum_ref, bias_ref, acc_ref, *, base
):
    pair = base + pl.program_id(0)
    rows = q_ref.shape[0]

    @pl.when(pl.program_id(0) == 0)
    def _():
        bias_ref[...] = jnp.where(seg_col_ref[...] == seg_row_ref[...], 0.0, -1e30).astype(F32)

    query = q_ref[...] * jnp.asarray(HEAD_DIM ** (-0.5), BF16)
    grads = g_ref[...]
    query_of = [only_head(query, head) for head in range(2)]
    grads_of = [only_head(grads, head) for head in range(2)]
    acc_ref[...] = jnp.zeros_like(acc_ref)
    value_sum = jnp.zeros((1, LANES), F32)
    for start in range(0, rows, TILE):
        at = pl.ds(start, TILE)
        keys = k_ref[at, :]
        values = v_ref[at, :]
        grad_key = jnp.zeros((TILE, LANES), F32)
        grad_value = jnp.zeros((TILE, LANES), F32)
        for head in range(2):
            key_h = only_head(keys, head)
            log_row = log_ref[pl.ds(2 * pair + head, 1), :]
            delta_row = delta_ref[pl.ds(2 * pair + head, 1), :]
            scores = dot(key_h, query, NT) + bias_ref[at, :]
            probs = jnp.exp(scores - log_row)
            grad_value = grad_value + dot(probs.astype(BF16), grads_of[head])
            grad_probs = dot(only_head(values, head), grads, NT)
            grad_scores = (probs * (grad_probs - delta_row)).astype(BF16)
            grad_key = grad_key + dot(grad_scores, query_of[head])
            acc_ref[...] += dot(key_h, grad_scores, TN)
        grad_value = grad_value.astype(BF16)
        dk_ref[at, :] = grad_key.astype(BF16)
        dv_ref[at, :] = grad_value
        value_sum = value_sum + jnp.sum(grad_value.astype(F32), axis=0, keepdims=True)
    grad_query = (acc_ref[...].T * HEAD_DIM ** (-0.5)).astype(BF16)
    dq_ref[...] = grad_query
    sum_ref[0:1, :] = jnp.sum(grad_query.astype(F32), axis=0, keepdims=True)
    sum_ref[1:2, :] = value_sum


def attend_back(query, key, value, grads, seg, log_rows, delta_rows, base, pairs, after=()):
    rows = query.shape[0]
    width = pairs * LANES
    taken = pl.BlockSpec((rows, LANES), lambda i: (0, base + i))
    given = pl.BlockSpec((rows, LANES), lambda i: (0, i))
    return call(
        partial(attend_back_kernel, base=base),
        (pairs,),
        [given] * 3 + [taken, whole((rows, 1)), whole((1, rows)), whole(log_rows.shape), whole(delta_rows.shape)],
        [given] * 3 + [pl.BlockSpec((2, LANES), lambda i: (0, i))],
        [shaped((rows, width), BF16)] * 3 + [shaped((2, width), F32)],
        (query, key, value, grads) + seg + (log_rows, delta_rows),
        scratch=[pltpu.VMEM((rows, rows), F32), pltpu.VMEM((LANES, rows), F32)],
        flops=40 * rows * rows * width,
        exps=rows * rows * width // HEAD_DIM,
        after=after,
    )


def merge_kernel(*refs, count):
    attended = beside(refs[:count])
    stream, bias, gain, shift, own_low, own_high, came_low, came_high, stream_one, normed, turned = refs[count:]
    half = stream.shape[1] // 2
    stream_one[:, :half] = stream[:, :half] + dot(attended, joined((own_low, own_high), 0, 1), NT)
    stream_one[:, half:] = stream[:, half:] + dot(attended, joined((came_low, came_high), 0, 1), NT)
    total = stream_one[...] + bias[...]
    stream_one[...] = total
    rows = (normalize(total)[0] * gain[...] + shift[...]).astype(BF16)
    normed[...] = rows
    turned[...] = rows.T


def first_two(array):
    return pl.BlockSpec(array.shape[:2] + (2,) + array.shape[3:], lambda *_: (0,) * array.ndim)


def merge(attended, stream, bias, gain, shift, weights, after=()):
    rows, model = stream.shape
    return call(
        partial(merge_kernel, count=len(attended)),
        (rows // TILE,),
        [row_tile(a.shape) for a in attended]
        + [row_tile(stream.shape)]
        + [whole((1, model))] * 3
        + [first_two(a) for a in weights],
        [row_tile((rows, model))] * 2 + [turned_tile((rows, model))],
        [shaped((rows, model), F32), shaped((rows, model), BF16), shaped((model, rows), BF16)],
        tuple(attended) + (stream, bias, gain, shift) + weights,
        flops=2 * rows * model * model,
        after=after,
    )


def gelu_parts(hidden):
    t = 1.0 / (1.0 + (0.3275911 * math.sqrt(0.5)) * jnp.abs(hidden))
    bell = jnp.exp(-0.5 * hidden * hidden)
    poly = t * (
        0.5 * 0.254829592
        + t * (-0.5 * 0.284496736 + t * (0.5 * 1.421413741 + t * (-0.5 * 1.453152027 + t * (0.5 * 1.061405429))))
    )
    tail = poly * bell
    below = jnp.where(hidden >= 0, 1.0 - tail, tail)
    return hidden * below, below + (hidden * (1.0 / math.sqrt(2.0 * math.pi))) * bell


def feed_kernel(
    x_ref, xt_ref, g_ref, gt_ref, e_own, e_other, c_own, c_other, b_ref, y_ref, d_ref, *grads
):
    e_keep, e_send, c_keep, c_send, db_ref, a_ref, h_ref = grads
    step = pl.program_id(0)
    rows, model = x_ref.shape
    half = model // 2

    @pl.when(step == 0)
    def _():
        y_ref[...] = jnp.zeros_like(y_ref)
        d_ref[...] = jnp.zeros_like(d_ref)

    expand = (merged(e_own[...]), merged(e_other[...]))
    contract = (merged(c_own[...]), merged(c_other[...]))
    sums = jnp.zeros((1, h_ref.shape[1]), F32)
    for start in range(0, rows, TILE):
        at = pl.ds(start, TILE)
        hidden = dot(x_ref[at, :half], expand[0]) + dot(x_ref[at, half:], expand[1]) + b_ref[0]
        grad_active = dot(g_ref[at, :half], contract[0]) + dot(g_ref[at, half:], contract[1])
        active, slope = gelu_parts(hidden)
        active = active.astype(BF16)
        grad_hidden = (grad_active * slope).astype(BF16)
        a_ref[at, :] = active
        h_ref[at, :] = grad_hidden
        sums = sums + jnp.sum(grad_hidden.astype(F32), axis=0, keepdims=True)
        for side in range(2):
            cols = pl.ds(side * half, half)
            y_ref[at, cols] += dot(active, contract[side], NT)
            d_ref[at, cols] += dot(grad_hidden, expand[side], NT)
    db_ref[0] = sums
    for side, (e_ref, c_ref) in enumerate(((e_keep, c_keep), (e_send, c_send))):
        cols = pl.ds(side * half, half)
        shape = e_ref.shape[:1] + e_ref.shape[2:]
        e_ref[:, 0] = dot(xt_ref[cols, :], h_ref[...]).astype(BF16).reshape(shape)
        c_ref[:, 0] = dot(gt_ref[cols, :], a_ref[...]).astype(BF16).reshape(shape)


def feed(core, rows_two, turned_two, top, turned_top, weights, bias, which, filled=(), after=()):
    rows, model = rows_two.shape
    steps, _, part = bias.shape
    pairs, wide = weights[0].shape[0], weights[0].shape[-2]
    if len(weights) == 1:
        weights = weights * 4
        block = (pairs, 1, 1, 1, wide, part)
        place = lambda side, mat: lambda i, core: (0, core[0] if side == 0 else 1 - core[0], i, mat, 0, 0)
        specs = [pl.BlockSpec(block, place(side, mat)) for mat in range(2) for side in range(2)]
    else:
        specs = [pl.BlockSpec((pairs, 1, wide, part), lambda i, core: (0, i, 0, 0))] * 4
    grad = pl.BlockSpec((pairs, 1, wide, part), lambda i, core: (0, i, 0, which))
    unit = pl.BlockSpec((1, 1, part), lambda i, core: (i, 0, 0))
    return call(
        lambda core, *refs: feed_kernel(*refs),
        (steps,),
        [whole((rows, model)), whole((model, rows))] * 2 + specs + [unit],
        [whole((rows, model))] * 2 + [grad] * 4 + [unit],
        [shaped((rows, model), F32)] * 2
        + [shaped((pairs, steps, wide, 2 * part), BF16)] * 4
        + [shaped((steps, 1, part), F32)],
        (rows_two, turned_two, top, turned_top) + tuple(weights) + (bias,),
        scratch=[pltpu.VMEM((rows, part), BF16)] * 2,
        flops=12 * rows * model * part * steps,
        exps=rows * part * steps,
        scalars=(core,),
        after=after,
        filled=[(2 + i, array) for i, array in enumerate(filled)],
    )


def merge_back_kernel(*refs, count):
    attended = beside(refs[:count])
    d_one, d_two, top, stream_one, gain, own_low, own_high, came_low, came_high, heads = refs[count : count + 10]
    grad_stream, turned, grad_attended, delta, sums = refs[count + 10 :]
    half = top.shape[1] // 2
    grad_two = d_one[...] + d_two[...]
    normed, scale = normalize(stream_one[...])
    cotangent = top[...].astype(F32)
    total = cotangent + normalize_back(grad_two * gain[...], normed, scale)
    grad_stream[...] = total
    low = total.astype(BF16)
    turned[...] = low.T
    grads = dot(low[:, :half], joined((own_low, own_high), 0, 1)) + dot(low[:, half:], joined((came_low, came_high), 0, 1))
    grads = grads.astype(BF16)
    grad_attended[...] = grads
    both = grads.astype(F32) * attended.astype(F32)
    high = both.astype(BF16)
    delta[...] = dot(heads[...], high, NT) + dot(heads[...], (both - high.astype(F32)).astype(BF16), NT)

    @pl.when(pl.program_id(0) == 0)
    def _():
        sums[...] = jnp.zeros_like(sums)

    for row, part in enumerate((grad_two * normed, grad_two, total, cotangent)):
        sums[row : row + 1, :] += jnp.sum(part, axis=0, keepdims=True)


def merge_back(attended, d_one, d_two, top, stream_one, gain, weights, heads, after=()):
    rows, model = stream_one.shape
    tile = row_tile((rows, model))
    return call(
        partial(merge_back_kernel, count=len(attended)),
        (rows // TILE,),
        [row_tile(a.shape) for a in attended]
        + [tile] * 4
        + [whole((1, model))]
        + [first_two(a) for a in weights]
        + [whole(heads.shape)],
        [tile, turned_tile((rows, model)), tile]
        + [pl.BlockSpec((heads.shape[0], TILE), lambda i: (0, i)), whole((8, model))],
        [
            shaped((rows, model), F32),
            shaped((model, rows), BF16),
            shaped((rows, model), BF16),
            shaped((heads.shape[0], rows), F32),
            shaped((8, model), F32),
        ],
        tuple(attended) + (d_one, d_two, top, stream_one, gain) + weights + (heads,),
        flops=2 * rows * model * model,
        after=after,
    )


def attention_grads_kernel(*refs, count):
    xt, bt = refs[:2]
    inputs = [beside(refs[2 + i * count : 2 + (i + 1) * count]) for i in range(3)]
    inputs.append(beside(refs[2 + 3 * count : -4]))
    outs = refs[-4:]
    half = xt.shape[0] // 2
    blocks, steps, _, wide, columns = outs[0].shape
    for place, right in enumerate(inputs):
        left = bt if place == 3 else xt
        for side in range(2):
            ref = outs[2 * (place // 2) + side]
            grad = dot(left[pl.ds(side * half, half), :], right).astype(BF16)
            for step in range(steps):
                part = grad[:, step * columns : (step + 1) * columns]
                ref[:, step, place % 2] = part.reshape(blocks, wide, columns)


def attention_grads(xt, bt, query, key, value, attended, blocks, columns, after=()):
    model, rows = xt.shape
    count = len(query)
    width = sum(a.shape[1] for a in query)
    shape = (blocks, width // columns, 2, model // (2 * blocks), columns)
    args = (xt, bt) + tuple(query) + tuple(key) + tuple(value) + tuple(attended)
    return call(
        partial(attention_grads_kernel, count=count),
        (1,),
        [whole(a.shape) for a in args],
        [whole(shape)] * 4,
        [shaped(shape, BF16)] * 4,
        args,
        flops=8 * rows * model * width,
        after=after,
    )


def project_back_kernel(*refs, count):
    grads = [beside(refs[i * count : (i + 1) * count]) for i in range(3)]
    rest = refs[3 * count :]
    grad_stream, stream, band, gain = rest[:4]
    weights = rest[4:-4]
    grad_embed, turned, sums, acc = rest[-4:]
    half = stream.shape[1] // 2
    each = len(weights) // 2
    for side in range(2):
        held = weights[side * each : (side + 1) * each]
        acc[:, side * half : (side + 1) * half] = sum(
            dot(grad, qkv_joined(held, mat), NT) for mat, grad in enumerate(grads)
        )
    grad_one = acc[...]
    normed, scale = normalize(stream[...])
    total = grad_stream[...] + normalize_back(grad_one * gain[...], normed, scale)
    low = total.astype(BF16)
    grad_embed[...] = low
    turned[...] = low.T

    @pl.when(pl.program_id(0) == 0)
    def _():
        sums[...] = jnp.zeros_like(sums)

    parts = [group_rows(band[...], group, total) for group in range(GROUPS)] + [grad_one * normed, grad_one]
    for row, part in enumerate(parts):
        sums[row : row + 1, :] += jnp.sum(part, axis=0, keepdims=True)


def project_back(query, key, value, grad_stream, stream, band, gain, weights, after=()):
    rows, model = stream.shape
    tile = row_tile((rows, model))
    parts = tuple(query) + tuple(key) + tuple(value)
    return call(
        partial(project_back_kernel, count=len(query)),
        (rows // TILE,),
        [row_tile(a.shape) for a in parts]
        + [tile] * 2
        + [row_tile(band.shape), whole((1, model))]
        + [whole(a.shape) for a in weights],
        [tile, turned_tile((rows, model)), whole((8, model))],
        [shaped((rows, model), BF16), shaped((model, rows), BF16), shaped((8, model), F32)],
        parts + (grad_stream, stream, band, gain) + weights,
        scratch=[pltpu.VMEM((TILE, model), F32)],
        flops=6 * rows * model * model,
        after=after,
    )


def patch_grads_kernel(present, gt, pix, band, keep, send, acc, *, base):
    group = base + pl.program_id(0)
    half = gt.shape[0] // 2
    acc[...] = jnp.zeros_like(acc)
    for tile in range(pix.shape[0] // TILE):

        @pl.when(present[tile * GROUPS + group] > 0)
        def _():
            at = pl.ds(tile * TILE, TILE)
            acc[...] += dot(gt[:, at], group_rows(band[at, :], group, pix[at, :]))

    keep[...] = acc[:half, :].astype(BF16)
    send[...] = acc[half:, :].astype(BF16)


def patch_grads(present, turned, pixels, band, base, after=()):
    model, rows = turned.shape
    width = pixels.shape[1]
    count = GROUPS // 2
    given = pl.BlockSpec((model // 2, width), lambda i, present: (0, i))
    return call(
        partial(patch_grads_kernel, base=base),
        (count,),
        [whole(turned.shape), whole(pixels.shape), whole(band.shape)],
        [given] * 2,
        [shaped((model // 2, count * width), BF16)] * 2,
        (turned, pixels, band),
        scratch=[pltpu.VMEM((model, width), F32)],
        flops=2 * rows * width * model,
        scalars=(present,),
        after=after,
    )


def pixel_grads_kernel(present, grads, band, lo_own, lo_came, hi_own, hi_came, out):
    tile = pl.program_id(0)
    half = grads.shape[1] // 2
    width = out.shape[1]
    out[...] = jnp.zeros_like(out)
    for group in range(GROUPS):

        @pl.when(present[tile * GROUPS + group] > 0)
        def _():
            at = pl.ds((group % 2) * width, width)
            own, came = (lo_own, lo_came) if group < 2 else (hi_own, hi_came)
            spread = dot(grads[:, :half], merged(own[:, :, at])) + dot(grads[:, half:], merged(came[:, :, at]))
            out[...] = jnp.where(band[...] == group, spread, out[...])


def pixel_grads(present, grads, band, patches, width, after=()):
    rows, model = grads.shape
    return call(
        pixel_grads_kernel,
        (rows // TILE,),
        [row_tile(grads.shape), row_tile(band.shape)] + [whole(a.shape) for a in patches],
        [row_tile((rows, width))],
        [shaped((rows, width), F32)],
        (grads, band) + patches,
        flops=4 * rows * width * model,
        scalars=(present,),
        after=after,
    )[0]


def make_body(fsdp, tensor):
    pairs = fsdp // 2
    t_bits = list(range(tensor.bit_length() - 1))
    f_bits = list(range(1, fsdp.bit_length() - 1))
    up, down = f_bits, f_bits[::-1]

    def swap(array, axis, bit):
        size = fsdp if axis == "fsdp" else tensor
        return lax.ppermute(array, axis, [(i, i ^ (1 << bit)) for i in range(size)])

    def body(
        pixels,
        segment,
        band_group,
        scaled_position,
        patch_weight,
        patch_bias,
        norm_gains,
        vector_biases,
        attention_weight,
        query_value_bias,
        merge_weight,
        expand_weight,
        expand_bias,
        contract_weight,
        cotangent,
    ):
        index = {"fsdp": lax.axis_index("fsdp"), "tensor": lax.axis_index("tensor")}
        core = index["fsdp"] & 1
        rows, pix = pixels.shape
        model = cotangent.shape[1]
        thin = patch_bias.shape[1]
        wide = model // fsdp
        unit = expand_weight.shape[1]
        half_unit = unit // 2
        segment = lax.dynamic_slice_in_dim(segment, index["tensor"] * rows, rows)

        def wider(array, came, axis, bit):
            dim = 0 if axis == "tensor" else len(f_bits) - bit
            mine = ((index[axis] >> bit) & 1) == 1
            return jnp.where(
                mine, jnp.concatenate([came, array], axis=dim), jnp.concatenate([array, came], axis=dim)
            )

        def shifts(make):
            count = tensor
            return [
                lax.ppermute(make(d), "tensor", [(i, (i + d) % count) for i in range(count)]) for d in range(1, count)
            ]

        def in_order(array, came):
            parts = jnp.stack([array] + came)[::-1]
            return lax.dynamic_slice_in_dim(jnp.concatenate([parts, parts]), tensor - 1 - index["tensor"], tensor)

        def open_f(array):
            return array.reshape((1,) * len(f_bits) + array.shape)

        def close_f(array):
            return array.reshape((pairs,) + array.shape[len(f_bits) :])

        def other_core(array):
            return swap(array, "fsdp", 0)

        class Pair:
            def __init__(self, one, two):
                self.held = [open_f(one), open_f(two)]
                self.todo = list(zip(up, down))

            def send(self):
                self.bits = self.todo.pop(0)
                return [swap(a, "fsdp", bit) for a, bit in zip(self.held, self.bits)]

            def take(self, came):
                self.held = [wider(a, c, "fsdp", bit) for a, c, bit in zip(self.held, came, self.bits)]

            def drain(self):
                while self.todo:
                    self.take(self.send())

            def closed(self):
                return [close_f(a) for a in self.held]

        def half_sum(keep, came, at, bit):
            dim = len(f_bits) - bit
            take = lambda array: lax.dynamic_slice_in_dim(array, at, 1, axis=dim)
            return (take(keep).astype(F32) + take(came).astype(F32)).astype(keep.dtype)

        class Sum:
            def __init__(self, keep, send, bits):
                self.keep, self.todo = unfold(keep), list(bits)
                self.came = unfold(swap(send, "fsdp", 0))

            def step(self):
                bit = self.todo.pop(0)
                mine = (index["fsdp"] >> bit) & 1
                self.sent = half_sum(self.keep, self.came, 1 - mine, bit)
                self.keep = half_sum(self.keep, self.came, mine, bit)
                self.came = swap(self.sent, "fsdp", bit)
                return self.sent

            def total(self):
                while self.todo:
                    self.step()
                return last_sum(self.keep, self.came)

        def unfold(array):
            return array.reshape((2,) * len(f_bits) + array.shape[1:])

        def last_sum(keep, came):
            rest = keep.shape[len(f_bits) :]
            return (keep.astype(F32) + came.astype(F32)).astype(keep.dtype).reshape(rest)

        def over_tensor(blocks):
            return lax.psum_scatter(blocks, "tensor", scatter_dimension=0, tiled=False)

        def to_split(array):
            parts = array.reshape(array.shape[0], pairs, 2, wide)
            even, odd = (parts[:, :, i].reshape(array.shape[0], -1) for i in range(2))
            return jnp.where(core == 0, jnp.concatenate([even, odd], axis=1), jnp.concatenate([odd, even], axis=1))

        def from_split(array):
            parts = array.reshape(array.shape[0], 2, pairs, wide)
            mine, other = parts[:, 0], parts[:, 1]
            parts = jnp.where(core == 0, jnp.stack([mine, other], axis=2), jnp.stack([other, mine], axis=2))
            return parts.reshape(array.shape)

        tie = lambda array, *others: lax.optimization_barrier((array,) + others)[0]
        core_at = core[None].astype(jnp.int32)
        aligned = wide % LANES == 0

        sync = lax.optimization_barrier
        n_vec = GROUPS + 2 + 4
        cut = n_vec * thin
        columns = (GROUPS // 2) * pix
        rest_up, rest_down = up[1:], down[1:]

        small = jnp.concatenate(
            [patch_bias, norm_gains, vector_biases, query_value_bias, expand_bias.reshape(-1, thin)], axis=0
        )
        extra = small.shape[0]
        small = jnp.pad(small.T, ((0, 0), (0, LANES - extra)))
        patch = jnp.concatenate([patch_weight.reshape(-1, thin).T, small], axis=1)
        attention = jnp.concatenate([attention_weight, merge_weight.T[None]], axis=0)[None]
        t_first, t_rest = t_bits[:1], t_bits[1:]

        def over_t(array, came, bits):
            for i, bit in enumerate(bits):
                array = wider(array, came if i == 0 else swap(array, "tensor", bit), "tensor", bit)
            return array

        def start_t(bits, *arrays):
            return [swap(a, "tensor", bits[0]) for a in arrays]

        def go(*pairs):
            return [p.send() if p.todo else None for p in pairs]

        def done(came, *pairs):
            for c, p in zip(came, pairs):
                if c is not None:
                    p.take(c)

        def both_cores(pair):
            held = pair.closed()
            return held, [other_core(a) for a in held]

        band = band_group[:, None]
        present = jnp.any(band_group.reshape(-1, TILE, 1) == jnp.arange(GROUPS), axis=1).astype(jnp.int32).reshape(-1)
        came = shifts(lambda d: patch)
        e_one, c_one, feed_high = shares(expand_weight, contract_weight)
        e_one, c_one = e_one[None], c_one[None]
        seg = (segment[:, None], segment[None, :])
        came, patch, attention, cotangent, e_one, band, present, seg = sync(
            (came, patch, attention, cotangent, e_one, band, present, seg)
        )
        patch = in_order(patch, came).reshape(tensor * thin, -1)
        patch = Pair(patch[:, :columns], patch[:, columns:])
        came = go(patch)
        came_t = start_t(t_first, attention, e_one)
        if aligned:
            top, turned_top = split_columns(core_at, cotangent, wide)
        else:
            top = to_split(cotangent)
            turned_top = top.T
        came, came_t, top, c_one, scaled_position = sync((came, came_t, top, c_one, scaled_position))
        done(came, patch)
        attention, e_one = (over_t(w, c, t_first) for w, c in zip((attention, e_one), came_t))
        came = go(patch)
        came_t = start_t(t_rest, attention) + start_t(t_first, c_one)
        half_width = model // 2
        column = jnp.arange(model)
        place = column % half_width
        natural = (2 * (place // wide) + (core ^ (column // half_width))) * wide + place % wide
        rates = jnp.exp((natural % half_width).astype(F32) * (-math.log(10000.0) / half_width))
        angles = scaled_position.astype(F32)[:, None] * rates[None, :]
        quarter = model // 4
        table = tuple(
            f(angles[:, i * quarter : (i + 1) * quarter]) for i, f in enumerate((jnp.sin, jnp.cos, jnp.sin, jnp.cos))
        )
        came, came_t, table, e_one = sync((came, came_t, table, e_one))
        done(came, patch)
        patch.drain()
        attention = over_t(attention, came_t[0], t_rest)
        c_one = over_t(c_one, came_t[1], t_first)
        quarter, half_t = tensor // 4, tensor // 2
        outward = [
            attention[i * half_t : (i + 1) * half_t, 3].reshape(quarter, 2, wide, -1) for i in range(2)
        ]
        qkv = [attention[i * quarter : (i + 1) * quarter, :3] for i in range(4)]
        qkv_one = Pair(*qkv[:2])
        qkv_two = Pair(*(jnp.concatenate(two, axis=1) for two in zip(outward, qkv[2:])))
        patch = both_cores(patch)
        came, came_t = go(qkv_one), start_t(t_rest, e_one)
        patch, came, came_t, c_one, feed_high = sync((patch, came, came_t, c_one, feed_high))
        patches = (patch[0][0], patch[1][0], patch[0][1], patch[1][1])
        done(came, qkv_one)
        e_one = over_t(e_one, came_t[0], t_rest)
        came, came_t = go(qkv_one), start_t(t_rest, c_one)
        feed_high = lax.all_gather(feed_high, ("fsdp", "tensor"), axis=0, tiled=False)
        feed_high = feed_high.reshape(pairs, 2, tensor, 2, wide, half_unit)
        small = [held[0] for held in (patch[0][1:], patch[1][1:])]
        small = jnp.stack([held[:, :, columns : columns + extra] for held in small]).astype(F32)
        vectors = small.reshape(model, extra).T
        patch_bias_rows = vectors[:GROUPS]
        gains = [vectors[GROUPS + i : GROUPS + i + 1] for i in range(2)]
        biases = [vectors[GROUPS + 2 + i : GROUPS + 3 + i] for i in range(4)]
        by_hidden = small[:, :, :, n_vec:].reshape(2, pairs, tensor, thin, extra - n_vec)
        by_hidden = jnp.where(core == 0, by_hidden, by_hidden[::-1]).transpose(4, 2, 1, 0, 3)
        qv_rows = by_hidden[:2].reshape(2, model)
        unit_bias = by_hidden[2:].reshape(-1, tensor, fsdp, thin).transpose(1, 2, 0, 3).reshape(tensor, 2, 1, half_unit)

        stream_zero, input_one, turned_one = embed(
            present, pixels, band, table, patch_bias_rows, gains[0], biases[0], patches
        )
        came, came_t, input_one, turned_one = sync((came, came_t, input_one, turned_one))
        done(came, qkv_one)
        qkv_one.drain()
        c_one = over_t(c_one, came_t[0], t_rest)
        feed_one = Pair(e_one, c_one)
        one, came = both_cores(qkv_one), go(qkv_two)
        one, came, input_one, feed_one.held = sync((one, came, input_one, feed_one.held))
        done(came, qkv_two)
        came = go(qkv_two)
        heads_width = model // 2
        each = heads_width // LANES
        first = project(input_one, *one, qv_rows[:, :heads_width])
        attended, logs = [None] * 3, [None] * 3
        attended[0], logs[0] = attend(*first, seg, 0, 0, each // 2)
        came, attended[0] = sync((came, attended[0]))
        done(came, qkv_two)
        qkv_two.drain()
        two, came = both_cores(qkv_two), go(feed_one)
        attended[1], logs[1] = attend(*first, seg, 0, each // 2, each // 2, after=(attended[0],))
        two, came, attended[1], input_one = sync((two, came, attended[1], input_one))
        done(came, feed_one)
        came = go(feed_one)
        last = project(input_one, *two, qv_rows[:, heads_width:])
        attended[2], logs[2] = attend(*last, seg, each, 0, each)
        came, attended[2] = sync((came, attended[2]))
        done(came, feed_one)
        feed_one.drain()
        feed_one = both_cores(feed_one)
        outward = tuple(two[0] + two[1])
        stream_one, input_two, turned_two = merge(attended, stream_zero, biases[1], gains[1], biases[2], outward)
        feed_one, input_two = sync((feed_one, input_two))

        rows_two = (input_two, turned_two, top, turned_top)
        weights = tuple(a for pair in zip(*feed_one) for a in pair)
        y_low, d_low, *grads_low, units_low = feed(core_at, *rows_two, weights, unit_bias[:, 0], 0)
        y_high, d_high, *grads_high, units_high = feed(
            core_at, *rows_two, (feed_high,), unit_bias[:, 1], 1, filled=grads_low, after=(y_low,)
        )
        unit_grads = [units_low, units_high]

        heads = model // HEAD_DIM
        head_rows = (jnp.arange(heads)[:, None] == jnp.arange(model)[None, :] // HEAD_DIM).astype(BF16)
        expand_sum = Sum(grads_high[0], grads_high[1], down)
        contract_sum = Sum(grads_high[2], grads_high[3], up)

        def meet(sums, *arrays):
            waited = sync(([t.came for t in sums],) + arrays)
            for t, came in zip(sums, waited[0]):
                t.came = came
            return waited[1] if len(arrays) == 1 else waited[1:]

        def advance(*sums):
            return [t.step() if t.todo else t.came for t in sums]

        def drain(*sums):
            for t in sums:
                while t.todo:
                    t.step()

        grad_stream_one, turned_branch, grad_attended, delta, sums_two = merge_back(
            attended, d_low, d_high, top, stream_one, gains[1], outward, head_rows
        )
        grad_attended = meet((expand_sum, contract_sum), grad_attended)
        log_rows = sum(logs)[:, :heads].T
        back = lambda i, after: attend_back(
            *(first, last)[i], grad_attended, seg, log_rows, delta, i * each, each, after=after
        )

        def grads_of(part, which, after):
            return attention_grads(
                turned_one, turned_branch, *([p] for p in part[:3]), attended[2 * which : 2 + which], pairs, model // tensor, after=after
            )

        first_part = back(0, advance(expand_sum, contract_sum))
        left = meet((expand_sum, contract_sum), grads_of(first_part, 0, ()))
        waits = advance(expand_sum, contract_sum)
        left_qk, left_vm = Sum(left[0], left[1], down), Sum(left[2], left[3], up)
        second_part = back(1, waits)
        second_part = meet((expand_sum, contract_sum, left_qk, left_vm), second_part)
        drain(expand_sum, contract_sum)
        feed_blocks = jnp.stack([expand_sum.total(), contract_sum.total()], axis=1)
        feed_grads = over_tensor(feed_blocks)
        right = grads_of(second_part, 1, advance(left_qk, left_vm) + [feed_blocks])
        right = meet((left_qk, left_vm), right)
        waits = advance(left_qk, left_vm)
        right_qk, right_vm = Sum(right[0], right[1], down), Sum(right[2], right[3], up)
        parts = (first_part, second_part)
        grad_query, grad_key, grad_value = ([p[i] for p in parts] for i in range(3))
        grad_qv = jnp.concatenate([p[3] for p in parts], axis=1)
        grad_embed, turned_embed, sums_one = project_back(
            grad_query, grad_key, grad_value, grad_stream_one, stream_zero, band, gains[0], tuple(one[0] + two[0] + one[1] + two[1]), after=waits
        )
        grad_embed, turned_embed = meet((left_qk, left_vm, right_qk, right_vm), grad_embed, turned_embed)

        waits = advance(right_qk, right_vm)
        shape = (pairs, tensor, thin, columns)
        lo = patch_grads(present, turned_embed, pixels, band, 0, after=waits)
        hi = patch_grads(present, turned_embed, pixels, band, GROUPS // 2, after=lo[:1])
        lo, hi = meet((right_qk, right_vm), lo, hi)
        lo = Sum(*(a.reshape(shape) for a in lo), up)
        hi = Sum(*(a.reshape(shape) for a in hi), down)
        waits = advance(right_qk, right_vm)

        vector_grads = from_split(
            jnp.concatenate(
                [sums_one[:GROUPS], sums_one[GROUPS : GROUPS + 1], sums_two[0:1], sums_one[GROUPS + 1 : GROUPS + 2]]
                + [sums_two[2:3], sums_two[1:2], sums_two[3:4]],
                axis=0,
            )
        )
        vector_grads = vector_grads.reshape(n_vec, fsdp * tensor, thin).transpose(1, 0, 2).reshape(fsdp, tensor, cut)
        hidden_grads = jnp.concatenate(
            [
                grad_qv.reshape(2, tensor, fsdp, thin).transpose(2, 1, 0, 3).reshape(fsdp, tensor, 2 * thin),
                jnp.stack(unit_grads, axis=1).reshape(tensor, fsdp, unit // fsdp).transpose(1, 0, 2),
            ],
            axis=2,
        )
        small_grads = jnp.concatenate([vector_grads, hidden_grads], axis=2).reshape(fsdp * tensor, -1)
        halvings = [("fsdp", bit) for bit in range(len(f_bits) + 1)[::-1]] + [("tensor", bit) for bit in t_bits[::-1]]

        def small_halves(array, axis, bit):
            half = array.shape[0] // 2
            mine = (index[axis] >> bit) & 1
            return (
                lax.dynamic_slice_in_dim(array, mine * half, half),
                swap(lax.dynamic_slice_in_dim(array, (1 - mine) * half, half), axis, bit),
            )

        small_kept, small_came = small_halves(small_grads, *halvings[0])
        block_output = output_rows(
            core_at, stream_one, y_low, y_high, biases[3], wide, after=waits + [small_kept]
        )
        if not aligned:
            block_output = from_split(block_output)
        small_came, block_output = meet((right_qk, right_vm, lo, hi), small_came, block_output)
        waits = advance(lo, hi)
        drain(left_qk, left_vm, right_qk, right_vm)
        small_kept, small_came = small_halves(small_kept + small_came, *halvings[1])
        pixel_grad = pixel_grads(present, grad_embed, band, patches, pix, after=waits + [small_kept])
        grad_attention = over_tensor(
            jnp.concatenate(
                [
                    jnp.concatenate([left_qk.total(), left_vm.total()], axis=1),
                    jnp.concatenate([right_qk.total(), right_vm.total()], axis=1),
                ],
                axis=0,
            )
        )
        small_came, pixel_grad = meet((lo, hi), small_came, pixel_grad)
        advance(lo, hi)
        drain(lo, hi)
        small_kept, small_came = small_halves(small_kept + small_came, *halvings[2])
        expand_out, contract_out = finish_feed(feed_grads)
        small_came, expand_out, contract_out = meet((lo, hi), small_came, expand_out, contract_out)
        blocks = jnp.concatenate([lo.total(), hi.total()], axis=2)
        own = lambda d: lax.dynamic_index_in_dim(blocks, (index["tensor"] + d) % tensor, 0, keepdims=False)
        came = shifts(own)
        for axis, bit in halvings[3:]:
            small_kept, small_came = small_halves(small_kept + small_came, axis, bit)
        small_grads = small_kept + small_came
        grad_patch = sum([c.astype(F32) for c in came], own(0).astype(F32)).T.reshape(GROUPS, pix, thin)
        attention_out, merge_grad = finish_attention(grad_attention)
        small_grads = small_grads[0]
        mine = small_grads[:cut].reshape(n_vec, thin)
        return (
            block_output,
            pixel_grad,
            grad_patch,
            mine[:GROUPS],
            mine[GROUPS : GROUPS + 2],
            mine[GROUPS + 2 :],
            attention_out,
            small_grads[cut : cut + 2 * thin].reshape(2, thin),
            merge_grad,
            expand_out,
            small_grads[cut + 2 * thin :],
            contract_out,
        )

    return body


def solution(mesh):
    every = ("fsdp", "tensor")
    args = (
        P(every, None),
        P("fsdp"),
        P(every),
        P(every),
        P(None, None, every),
        P(None, every),
        P(None, every),
        P(None, every),
        P(None, "fsdp", "tensor"),
        P(None, ("tensor", "fsdp")),
        P("tensor", "fsdp"),
        P("fsdp", "tensor"),
        P(("tensor", "fsdp")),
        P("tensor", "fsdp"),
        P(every, None),
    )
    outs = (P(every, None), P(every, None)) + args[4:14]
    body = make_body(mesh.shape["fsdp"], mesh.shape["tensor"])
    return jax.shard_map(body, mesh=mesh, in_specs=args, out_specs=outs, check_vma=False)
```

time: 683 us -> 568 us (0.83)
  waiting for transfers between devices: 206 us -> 82.5 us
  other arithmetic: 73.5 us -> 61 us
  starting transfers between devices: 52.4 us -> 63.7 us
  local copies, waits for them, and re-layouts: 32.4 us -> 40.5 us
    ppermute x44 -> x59, waiting for transfers between devices: 206 us -> 49.9 us  [swap(): return lax.ppermute(array, axis, [(i, i ^ 1 << bit) for i in range(size)])]
    ppermute x0 -> x6, waiting for transfers between devices: none -> 32.5 us  [shifts(): lax.ppermute(make(d), 'tensor', [(i, (i + d) % count) for i in range(coun...]
    concatenate x12 -> x4, other arithmetic: 20.7 us -> 1.46 us  [the longest x1 1.08 us: body(): jnp.concatenate([jnp.concatenate([left_qk.total(), left_vm.total()], axis...]
    sin x1 -> x0, local copies, waits for them, and re-layouts: 14.6 us -> none  [body(): f(angles[:, i * quarter:(i + 1) * quarter])]
    cos x0 -> x1, local copies, waits for them, and re-layouts: none -> 14.1 us  [body(): f(angles[:, i * quarter:(i + 1) * quarter])]
    select_n x17 -> x22, other arithmetic: 4.86 us -> 14.7 us  [wider(): jnp.where(mine, jnp.concatenate([came, array], axis=dim), jnp.concatenate...]
    ppermute x0 -> x6, starting transfers between devices: none -> 8.14 us  [shifts(): lax.ppermute(make(d), 'tensor', [(i, (i + d) % count) for i in range(coun...]
    ppermute x44 -> x59, starting transfers between devices: 52 us -> 55.2 us  [swap(): return lax.ppermute(array, axis, [(i, i ^ 1 << bit) for i in range(size)])]
  transfers between devices with their start and end apart: 49 -> 68, of which waited for: 17 -> 22; matrix products, arithmetic and copies ran while one was open for 15% -> 13% of each run, Pallas kernels for 38% -> 46%
where the time goes in v2:
time: 568 us; the launch traced here: 561 us
  Pallas kernels  298 us (52%)
  waiting for transfers between devices  82.5 us (15%)
  starting transfers between devices  63.7 us (11%)
  other arithmetic  61 us (11%)
  local copies, waits for them, and re-layouts  40.5 us (7%)
  between operations  15.7 us (3%)
    pallas_call x23, Pallas kernels, call(): pl.pallas_call(with_waits, grid_spec=pltpu.PrefetchScalarGridSpec(num_sca...  298 us
    ppermute x59, starting transfers between devices, swap(): return lax.ppermute(array, axis, [(i, i ^ 1 << bit) for i in range(size)])  55.2 us
    ppermute x59, waiting for transfers between devices, swap(): return lax.ppermute(array, axis, [(i, i ^ 1 << bit) for i in range(size)])  49.9 us
    ppermute x6, waiting for transfers between devices, shifts(): lax.ppermute(make(d), 'tensor', [(i, (i + d) % count) for i in range(coun...  32.5 us
    convert_element_type x16, other arithmetic, half_sum(): return (take(keep).astype(F32) + take(came).astype(F32)).astype(keep.dtype)  29.3 us
    select_n x22, other arithmetic, wider(): jnp.where(mine, jnp.concatenate([came, array], axis=dim), jnp.concatenate...  14.7 us
    cos x1, local copies, waits for them, and re-layouts, body(): f(angles[:, i * quarter:(i + 1) * quarter])  14.1 us
  transfers between devices with their start and end apart: 68, of which 22 were waited for; matrix products, arithmetic and copies ran while one was open for 13% of the time, Pallas kernels for 46%

profile of v2, /device:TPU:8, one launch (start us, length us, event | category | flops | bytes accessed | tf_op | source)
XLA Modules:
  0.0 561.3 jit_solution(17861727855368867334)
XLA Ops:
  22.8 5.3 collective-permute-done
  38.9 4.5 shard_map.239
  43.4 3.9 collective-permute-done.6
  51.0 14.1 %slice_cosine_fusion = (f32[1024,256]{1,0:T(8,128)}, f32[1024,256]{1,0:T(8,128)}, f32[1024,256]{1,0:T(8,128)}, f32[1024,256]{1,0:T(8,128)}) fusion(f32[1024,1024]{1,0:T(8,128)S(1)} %broadcast_multiply_fusion), kind=kLoop, calls=%fused_computation.34 | loop fusion | bytes 8388608 | tf_op jit(solution)/shard_map/cos | solution.py:913
  65.2 5.4 collective-permute-done.9
  72.3 3.4 collective-permute-start.15
  104.5 13.2 %shard_map.240 = (f32[1024,1024]{1,0:T(8,128)}, bf16[1024,1024]{1,0:T(8,128)(2,1)}, bf16[1024,1024]{1,0:T(8,128)(2,1)}) custom-call(s32[16]{0:T(128)} %reshape.1194.refs_0_, bf16[1024,768]{1,0:T(8,128)(2,1)} %refs_2_.3, s32[1024,1]{1,0:T(8,128)} %copy.155.refs_2_.refs_8_.refs_3_, f32[1024,256]{1,0:T(8,128)} %get-tuple-element.227.refs_3_, ...), custom_call_target="tpu_custom_call" | custom-call | flops 3221225472 | bytes 20738048 | tf_op jit(solution)/shard_map/pallas_call | solution.py:80
  126.7 6.9 %shard_map.241 = (bf16[1024,512]{1,0:T(8,128)(2,1)}, bf16[1024,512]{1,0:T(8,128)(2,1)}, bf16[1024,512]{1,0:T(8,128)(2,1)}) custom-call(bf16[1024,1024]{1,0:T(8,128)(2,1)} %get-tuple-element.263.refs_0_, f32[2,512]{1,0:T(2,128)} %get-tuple-element.500.refs_1_, bf16[4,1,3,128,256]{4,3,2,1,0:T(8,128)(2,1)} %bitcast.171, bf16[4,1,3,128,256]{4,3,2,1,0:T(8,128)(2,1)} %bitcast.168, ...), custom_call_target="tpu_custom_call" | custom-call | flops 3221225472 | bytes 8392704 | tf_op jit(solution)/shard_map/pallas_call | solution.py:80
  133.6 11.1 %shard_map.242 = (bf16[1024,256]{1,0:T(8,128)(2,1)}, f32[1024,128]{1,0:T(8,128)}) custom-call(bf16[1024,512]{1,0:T(8,128)(2,1)} %get-tuple-element.249.refs_0_, bf16[1024,512]{1,0:T(8,128)(2,1)} %get-tuple-element.250.refs_1_, bf16[1024,512]{1,0:T(8,128)(2,1)} %get-tuple-element.251.refs_2_, s32[1024,1]{1,0:T(8,128)} %copy.160.refs_3_.refs_4_, ...), custom_call_target="tpu_custom_call" | custom-call | flops 4294967296 | bytes 4202496 | tf_op jit(solution)/shard_map/pallas_call | solution.py:80
  148.9 11.6 %shard_map.243 = (bf16[1024,256]{1,0:T(8,128)(2,1)}, f32[1024,128]{1,0:T(8,128)}) custom-call(bf16[1024,512]{1,0:T(8,128)(2,1)} %get-tuple-element.249.refs_0_, bf16[1024,512]{1,0:T(8,128)(2,1)} %get-tuple-element.250.refs_1_, bf16[1024,512]{1,0:T(8,128)(2,1)} %get-tuple-element.251.refs_2_, s32[1024,1]{1,0:T(8,128)} %copy.160.refs_3_.refs_4_, ...), custom_call_target="tpu_custom_call" | custom-call | flops 4294967296 | bytes 4202496 | tf_op jit(solution)/shard_map/pallas_call | solution.py:80
  160.6 11.1 %collective-permute-done.27 = bf16[1,1,4,128,512]{4,3,2,1,0:T(8,128)(2,1)S(1)} collective-permute-done((bf16[1,1,4,128,512]{4,3,2,1,0:T(8,128)(2,1)S(1)}, bf16[1,1,4,128,512]{4,3,2,1,0:T(8,128)(2,1)S(1)}, u32[]{:S(2)}, u32[]{:S(2)}) %collective-permute-start.27) | collective-permute-done | bytes 524320 | tf_op jit(solution)/shard_map/ppermute | solution.py:725
  177.5 7.9 %shard_map.244 = (bf16[1024,512]{1,0:T(8,128)(2,1)}, bf16[1024,512]{1,0:T(8,128)(2,1)}, bf16[1024,512]{1,0:T(8,128)(2,1)}) custom-call(bf16[1024,1024]{1,0:T(8,128)(2,1)} %get-tuple-element.263.refs_0_, f32[2,512]{1,0:T(2,128)} %get-tuple-element.499.refs_1_, bf16[4,1,5,128,256]{4,3,2,1,0:T(8,128)(2,1)} %bitcast.152, bf16[4,1,5,128,256]{4,3,2,1,0:T(8,128)(2,1)} %bitcast.147, ...), custom_call_target="tpu_custom_call" | custom-call | flops 3221225472 | bytes 10489856 | tf_op jit(solution)/shard_map/pallas_call | solution.py:80
  185.3 19.6 %shard_map.245 = (bf16[1024,512]{1,0:T(8,128)(2,1)}, f32[1024,128]{1,0:T(8,128)}) custom-call(bf16[1024,512]{1,0:T(8,128)(2,1)} %get-tuple-element.268.refs_0_, bf16[1024,512]{1,0:T(8,128)(2,1)} %get-tuple-element.269.refs_1_, bf16[1024,512]{1,0:T(8,128)(2,1)} %get-tuple-element.270.refs_2_, s32[1024,1]{1,0:T(8,128)} %copy.160.refs_3_.refs_4_, ...), custom_call_target="tpu_custom_call" | custom-call | flops 8589934592 | bytes 4726784 | tf_op jit(solution)/shard_map/pallas_call | solution.py:80
  208.4 8.6 %shard_map.246 = (f32[1024,1024]{1,0:T(8,128)}, bf16[1024,1024]{1,0:T(8,128)(2,1)}, bf16[1024,1024]{1,0:T(8,128)(2,1)}) custom-call(bf16[1024,256]{1,0:T(8,128)(2,1)} %get-tuple-element.259.refs_5_.refs_0_, bf16[1024,256]{1,0:T(8,128)(2,1)} %get-tuple-element.274.refs_1_.refs_6_, bf16[1024,512]{1,0:T(8,128)(2,1)} %get-tuple-element.275.refs_2_.refs_5_, ...), custom_call_target="tpu_custom_call" | custom-call | flops 2147483648 | bytes 19935232 | tf_op jit(solution)/shard_map/pallas_call | solution.py:80
  217.0 37.4 %shard_map.247 = (f32[1024,1024]{1,0:T(8,128)}, f32[1024,1024]{1,0:T(8,128)}, bf16[4,4,128,1024]{3,2,1,0:T(8,128)(2,1)}, bf16[4,4,128,1024]{3,2,1,0:T(8,128)(2,1...) custom-call(s32[1]{0:T(128)} %bitcast.refs_0_, ...), custom_call_target="tpu_custom_call" | custom-call | flops 25769803776 | bytes 41959424 | tf_op jit(solution)/shard_map/pallas_call | solution.py:80
  254.5 37.8 %shard_map.248 = (f32[1024,1024]{1,0:T(8,128)}, f32[1024,1024]{1,0:T(8,128)}, bf16[4,4,128,1024]{3,2,1,0:T(8,128)(2,1)}, bf16[4,4,128,1024]{3,2,1,0:T(8,128)(2,1...) custom-call(s32[1]{0:T(128)} %bitcast.refs_0_, ...), custom_call_target="tpu_custom_call", output_to_operand_aliasing={{2}: (11, {}), {3}: (12, {}), {4}: (13, {}), {5}: (14, {})} | custom-call | flops 25769803776 | bytes 67125248 | tf_op jit(solution)/shard_map/pallas_call | solution.py:80
  294.7 13.9 %shard_map.249 = (f32[1024,1024]{1,0:T(8,128)}, bf16[1024,1024]{1,0:T(8,128)(2,1)}, bf16[1024,1024]{1,0:T(8,128)(2,1)}, f32[16,1024]{1,0:T(8,128)}, f32[8,1024]{1,0:T(8,128)}) custom-call(bf16[1024,256]{1,0:T(8,128)(2,1)} %get-tuple-element.259.refs_5_.refs_0_, bf16[1024,256]{1,0:T(8,128)(2,1)} %get-tuple-element.274.refs_1_.refs_6_, ...), custom_call_target="tpu_custom_call" | custom-call | flops 2147483648 | bytes 30543872 | tf_op jit(solution)/shard_map/pallas_call | solution.py:80
  308.6 6.0 %add_convert_fusion = (bf16[2,1,4,128,1024]{4,3,2,1,0:T(8,128)(2,1)S(1)}, bf16[2,1,4,128,1024]{4,3,2,1,0:T(8,128)(2,1)}) fusion(bf16[2,2,4,128,1024]{4,3,2,1,0:T(8,128)(2,1)} %bitcast.47, s32[]{:T(128)S(6)} %select_n.601, bf16[2,2,4,128,1024]{4,3,2,1,0:T(8,128)(2,1)S(1)} %bitcast.164, s32[]{:T(128)S(6)} %select_n.599), kind=kLoop, calls=%fused_computation | loop fusion | flops 8388608 | bytes 12582920 | tf_op jit(solution)/shard_map/convert_element_type | solution.py:802
  315.2 4.4 add_convert_fusion.1
  321.0 26.5 %shard_map.250 = (bf16[1024,512]{1,0:T(8,128)(2,1)}, bf16[1024,512]{1,0:T(8,128)(2,1)}, bf16[1024,512]{1,0:T(8,128)(2,1)}, f32[2,512]{1,0:T(2,128)}) custom-call(bf16[1024,512]{1,0:T(8,128)(2,1)} %get-tuple-element.249.refs_0_, bf16[1024,512]{1,0:T(8,128)(2,1)} %get-tuple-element.250.refs_1_, bf16[1024,512]{1,0:T(8,128)(2,1)} %get-tuple-element.251.refs_2_, ...), custom_call_target="tpu_custom_call" | custom-call | flops 21474836480 | bytes 8531968 | tf_op jit(solution)/shard_map/pallas_call | solution.py:80
  347.4 8.9 %shard_map.251 = (bf16[4,2,2,128,256]{4,3,2,1,0:T(8,128)(2,1)}, bf16[4,2,2,128,256]{4,3,2,1,0:T(8,128)(2,1)}, bf16[4,2,2,128,256]{4,3,2,1,0:T(8,128)(2,1)}, bf16[4,2,2,128,256]{4,3,2,1,0:T(8,128)(2,1)}) custom-call(bf16[1024,1024]{1,0:T(8,128)(2,1)} %get-tuple-element.302.refs_0_, bf16[1024,1024]{1,0:T(8,128)(2,1)} %get-tuple-element.303.refs_1_, ...), custom_call_target="tpu_custom_call" | custom-call | flops 4294967296 | bytes 12582912 | tf_op jit(solution)/shard_map/pallas_call | solution.py:80
  356.3 6.5 %collective-permute-done.36 = bf16[2,1,4,128,1024]{4,3,2,1,0:T(8,128)(2,1)} collective-permute-done((bf16[2,1,4,128,1024]{4,3,2,1,0:T(8,128)(2,1)}, bf16[2,1,4,128,1024]{4,3,2,1,0:T(8,128)(2,1)}, u32[]{:S(2)}, u32[]{:S(2)}) %collective-permute-start.36) | collective-permute-done | bytes 2097184 | tf_op jit(solution)/shard_map/ppermute | solution.py:725
  362.8 4.5 collective-permute-done.35
  374.9 26.6 %shard_map.252 = (bf16[1024,512]{1,0:T(8,128)(2,1)}, bf16[1024,512]{1,0:T(8,128)(2,1)}, bf16[1024,512]{1,0:T(8,128)(2,1)}, f32[2,512]{1,0:T(2,128)}) custom-call(bf16[1024,512]{1,0:T(8,128)(2,1)} %get-tuple-element.268.refs_0_, bf16[1024,512]{1,0:T(8,128)(2,1)} %get-tuple-element.269.refs_1_, bf16[1024,512]{1,0:T(8,128)(2,1)} %get-tuple-element.270.refs_2_, ...), custom_call_target="tpu_custom_call" | custom-call | flops 21474836480 | bytes 8531968 | tf_op jit(solution)/shard_map/pallas_call | solution.py:80
  412.7 8.9 %shard_map.253 = (bf16[4,2,2,128,256]{4,3,2,1,0:T(8,128)(2,1)}, bf16[4,2,2,128,256]{4,3,2,1,0:T(8,128)(2,1)}, bf16[4,2,2,128,256]{4,3,2,1,0:T(8,128)(2,1)}, bf16[4,2,2,128,256]{4,3,2,1,0:T(8,128)(2,1)}) custom-call(bf16[1024,1024]{1,0:T(8,128)(2,1)} %get-tuple-element.302.refs_0_, bf16[1024,1024]{1,0:T(8,128)(2,1)} %get-tuple-element.303.refs_1_, ...), custom_call_target="tpu_custom_call" | custom-call | flops 4294967296 | bytes 12582912 | tf_op jit(solution)/shard_map/pallas_call | solution.py:80
  428.1 17.3 %shard_map.254 = (bf16[1024,1024]{1,0:T(8,128)(2,1)}, bf16[1024,1024]{1,0:T(8,128)(2,1)}, f32[8,1024]{1,0:T(8,128)}) custom-call(bf16[1024,512]{1,0:T(8,128)(2,1)} %get-tuple-element.309.refs_2_.refs_0_, bf16[1024,512]{1,0:T(8,128)(2,1)} %get-tuple-element.328.refs_2_.refs_1_, bf16[1024,512]{1,0:T(8,128)(2,1)} %get-tuple-element.310.refs_3_.refs_2_, ...), custom_call_target="tpu_custom_call" | custom-call | flops 6442450944 | bytes 27303936 | tf_op jit(solution)/shard_map/pallas_call | solution.py:80
  448.8 7.6 %shard_map.255 = (bf16[512,1536]{1,0:T(8,128)(2,1)}, bf16[512,1536]{1,0:T(8,128)(2,1)}) custom-call(s32[16]{0:T(128)} %reshape.1194.refs_0_, bf16[1024,1024]{1,0:T(8,128)(2,1)} %get-tuple-element.348.refs_1_, bf16[1024,768]{1,0:T(8,128)(2,1)} %refs_2_.3, s32[1024,1]{1,0:T(8,128)} %copy.155.refs_2_.refs_8_.refs_3_, ...), custom_call_target="tpu_custom_call" | custom-call | flops 1610612736 | bytes 6819840 | tf_op jit(solution)/shard_map/pallas_call | solution.py:80
  456.4 6.9 %shard_map.256 = (bf16[512,1536]{1,0:T(8,128)(2,1)}, bf16[512,1536]{1,0:T(8,128)(2,1)}) custom-call(s32[16]{0:T(128)} %reshape.1194.refs_0_, bf16[1024,1024]{1,0:T(8,128)(2,1)} %get-tuple-element.348.refs_1_, bf16[1024,768]{1,0:T(8,128)(2,1)} %refs_2_.3, s32[1024,1]{1,0:T(8,128)} %copy.155.refs_2_.refs_8_.refs_3_, bf16[512,1536]{1,0:T(8,128)(2,1)} %get-tuple-element.365.refs_4_), custom_call_target="tpu_custom_call" | custom-call | flops 1610612736 | bytes 6819840 | tf_op jit(solution)/shard_map/pallas_call | solution.py:80
  471.3 7.8 %shard_map.257 = f32[1024,1024]{1,0:T(8,128)} custom-call(s32[1]{0:T(128)} %bitcast.refs_0_, f32[1024,1024]{1,0:T(8,128)} %get-tuple-element.297.refs_6_.refs_1_, f32[1024,1024]{1,0:T(8,128)} %get-tuple-element.287.refs_10_.refs_2_, f32[1024,1024]{1,0:T(8,128)} %get-tuple-element.363.refs_3_, f32[1,1024]{1,0:T(1,128)} %get-tuple-element.483.refs_4_, ...), custom_call_target="tpu_custom_call" | custom-call | bytes 16781312 | tf_op jit(solution)/shard_map/pallas_call | solution.py:80
  488.8 9.4 %shard_map.258 = f32[1024,768]{1,0:T(8,128)} custom-call(s32[16]{0:T(128)} %reshape.1194.refs_0_, bf16[1024,1024]{1,0:T(8,128)(2,1)} %get-tuple-element.370.refs_1_, s32[1024,1]{1,0:T(8,128)} %copy.155.refs_2_.refs_8_.refs_3_, bf16[4,128,1536]{2,1,0:T(8,128)(2,1)} %bitcast.162, bf16[4,128,1536]{2,1,0:T(8,128)(2,1)} %collective-permute-done.11.refs_11_.refs_4_, ...), custom_call_target="tpu_custom_call" | custom-call | flops 3221225472 | bytes 11800576 | tf_op jit(solution)/shard_map/pallas_call | solution.py:80
  499.4 4.5 collective-permute-done.56
  529.5 17.1 %collective-permute-done.60 = bf16[32,3072]{1,0:T(8,128)(2,1)S(1)} collective-permute-done((bf16[32,3072]{1,0:T(8,128)(2,1)S(1)}, bf16[32,3072]{1,0:T(8,128)(2,1)S(1)}, u32[]{:S(2)}, u32[]{:S(2)}) %collective-permute-start.60) | collective-permute-done | bytes 196640 | tf_op jit(solution)/shard_map/ppermute | solution.py:764
  (418 shorter events, 167.1 us)
Async XLA Ops:
  7.2 247.3 %all-gather.3.cloned.1.call-start = ((), (), s32[]{:S(2)}) async-start(), calls=%async_computation.4 | async-start | bytes 8650752 | tf_op jit(solution)/shard_map/all_gather | solution.py:934
  48.2 22.4 %collective-permute-start.8 = (bf16[2,1,128,1664]{3,2,1,0:T(8,128)(2,1)S(1)}, bf16[2,1,128,1664]{3,2,1,0:T(8,128)(2,1)S(1)}, u32[]{:S(2)}, u32[]{:S(2)}) collective-permute-start(bf16[2,1,128,1664]{3,2,1,0:T(8,128)(2,1)S(1)} %maximum_select_fusion.9), channel_id=1, source_target_pairs={{0,8},{4,12},{8,0},{12,4},{16,24},{20,28},{24,16},{28,20},{1,9},{5... | collective-permute-start | bytes 2555912 | tf_op jit(solution)/shard_map/ppermute | solution.py:725
  48.9 21.7 %collective-permute-start.7 = (bf16[1,2,128,1536]{3,2,1,0:T(8,128)(2,1)S(1)}, bf16[1,2,128,1536]{3,2,1,0:T(8,128)(2,1)S(1)}, u32[]{:S(2)}, u32[]{:S(2)}) collective-permute-start(bf16[1,2,128,1536]{3,2,1,0:T(8,128)(2,1)S(1)} %maximum_select_fusion.10), channel_id=1, source_target_pairs={{0,16},{4,20},{8,24},{12,28},{16,0},{20,4},{24,8},{28,12},{1,17},{... | collective-permute-start | bytes 2359304 | tf_op jit(solution)/shard_map/ppermute | solution.py:725
  49.6 21.0 %collective-permute-start.9 = (bf16[2,4,128,256]{3,2,1,0:T(8,128)(2,1)S(1)}, bf16[2,4,128,256]{3,2,1,0:T(8,128)(2,1)S(1)}, u32[]{:S(2)}, u32[]{:S(2)}) collective-permute-start(bf16[2,4,128,256]{3,2,1,0:T(8,128)(2,1)S(1)} %maximum_select_fusion.15), channel_id=1, source_target_pairs={{0,2},{1,3},{2,0},{3,1},{4,6},{5,7},{6,4},{7,5},{8,10},{9,11},{10,... | collective-permute-start | bytes 1572872 | tf_op jit(solution)/shard_map/ppermute | solution.py:725
  87.8 421.5 %reduce-scatter.3.cloned.1.call-start = ((), (), s32[]{:S(2)}) async-start(), calls=%async_computation.2 | async-start | bytes 2621440 | tf_op jit(solution)/shard_map/reduce_scatter | solution.py:830
  92.1 29.6 %collective-permute-start.22 = (bf16[1,1,1,5,128,256]{5,4,3,2,1,0:T(8,128)(2,1)S(1)}, bf16[1,1,1,5,128,256]{5,4,3,2,1,0:T(8,128)(2,1)}, u32[]{:S(2)}, u32[]{:S(2)}) collective-permute-start(bf16[1,1,1,5,128,256]{5,4,3,2,1,0:T(8,128)(2,1)S(1)} %maximum_bitcast_fusion.1), channel_id=1, source_target_pairs={{0,16},{4,20},{8,24},{12,28},{16,0},{20,4},{24,8},{28,12},{1,17},{... | collective-permute-start | bytes 983048 | tf_op jit(solution)/shard_map/ppermute | solution.py:725
  93.7 28.1 %collective-permute-start.21 = (bf16[1,1,1,5,128,256]{5,4,3,2,1,0:T(8,128)(2,1)S(1)}, bf16[1,1,1,5,128,256]{5,4,3,2,1,0:T(8,128)(2,1)}, u32[]{:S(2)}, u32[]{:S(2)}) collective-permute-start(bf16[1,1,1,5,128,256]{5,4,3,2,1,0:T(8,128)(2,1)S(1)} %maximum_bitcast_fusion), channel_id=1, source_target_pairs={{0,8},{4,12},{8,0},{12,4},{16,24},{20,28},{24,16},{28,20},{1,9},{5... | collective-permute-start | bytes 983048 | tf_op jit(solution)/shard_map/ppermute | solution.py:725
  97.5 20.1 %collective-permute-start.17 = (bf16[2,1,1,3,128,256]{5,4,3,2,1,0:T(8,128)(2,1)S(1)}, bf16[2,1,1,3,128,256]{5,4,3,2,1,0:T(8,128)(2,1)S(1)}, u32[]{:S(2)}, u32[]{:S(2)}) collective-permute-start(bf16[2,1,1,3,128,256]{5,4,3,2,1,0:T(8,128)(2,1)S(1)} %maximum_select_fusion.19), channel_id=1, source_target_pairs={{0,8},{4,12},{8,0},{12,4},{16,24},{20,28},{24,16},{28,20},{1,9},{5... | collective-permute-start | bytes 1179656 | tf_op jit(solution)/shard_map/ppermute | solution.py:725
  123.1 22.7 %collective-permute-start.24 = (bf16[2,1,1,5,128,256]{5,4,3,2,1,0:T(8,128)(2,1)S(1)}, bf16[2,1,1,5,128,256]{5,4,3,2,1,0:T(8,128)(2,1)S(1)}, u32[]{:S(2)}, u32[]{:S(2)}) collective-permute-start(bf16[2,1,1,5,128,256]{5,4,3,2,1,0:T(8,128)(2,1)S(1)} %maximum_select_fusion.14), channel_id=1, source_target_pairs={{0,8},{4,12},{8,0},{12,4},{16,24},{20,28},{24,16},{28,20},{1,9},{5... | collective-permute-start | bytes 1966088 | tf_op jit(solution)/shard_map/ppermute | solution.py:725
  125.8 20.0 %collective-permute-start.23 = (bf16[1,2,1,5,128,256]{5,4,3,2,1,0:T(8,128)(2,1)S(1)}, bf16[1,2,1,5,128,256]{5,4,3,2,1,0:T(8,128)(2,1)S(1)}, u32[]{:S(2)}, u32[]{:S(2)}) collective-permute-start(bf16[1,2,1,5,128,256]{5,4,3,2,1,0:T(8,128)(2,1)S(1)} %maximum_select_fusion.13), channel_id=1, source_target_pairs={{0,16},{4,20},{8,24},{12,28},{16,0},{20,4},{24,8},{28,12},{1,17},{... | collective-permute-start | bytes 1966088 | tf_op jit(solution)/shard_map/ppermute | solution.py:725
  146.0 26.3 %collective-permute-start.26 = (bf16[4,1,5,128,256]{4,3,2,1,0:T(8,128)(2,1)S(1)}, bf16[4,1,5,128,256]{4,3,2,1,0:T(8,128)(2,1)S(1)}, u32[]{:S(2)}, u32[]{:S(2)}) collective-permute-start(bf16[4,1,5,128,256]{4,3,2,1,0:T(8,128)(2,1)S(1)} %bitcast.146), channel_id=1, source_target_pairs={{0,4},{4,0},{8,12},{12,8},{16,20},{20,16},{24,28},{28,24},{1,5},{5... | collective-permute-start | bytes 3932168 | tf_op jit(solution)/shard_map/ppermute | solution.py:725
  146.3 26.0 %collective-permute-start.25 = (bf16[4,1,5,128,256]{4,3,2,1,0:T(8,128)(2,1)S(1)}, bf16[4,1,5,128,256]{4,3,2,1,0:T(8,128)(2,1)S(1)}, u32[]{:S(2)}, u32[]{:S(2)}) collective-permute-start(bf16[4,1,5,128,256]{4,3,2,1,0:T(8,128)(2,1)S(1)} %bitcast.151), channel_id=1, source_target_pairs={{0,4},{4,0},{8,12},{12,8},{16,20},{20,16},{24,28},{28,24},{1,5},{5... | collective-permute-start | bytes 3932168 | tf_op jit(solution)/shard_map/ppermute | solution.py:725
  146.9 24.8 %collective-permute-start.27 = (bf16[1,1,4,128,512]{4,3,2,1,0:T(8,128)(2,1)S(1)}, bf16[1,1,4,128,512]{4,3,2,1,0:T(8,128)(2,1)S(1)}, u32[]{:S(2)}, u32[]{:S(2)}) collective-permute-start(bf16[1,1,4,128,512]{4,3,2,1,0:T(8,128)(2,1)S(1)} %maximum_select_fusion.16), channel_id=1, source_target_pairs={{0,8},{4,12},{8,0},{12,4},{16,24},{20,28},{24,16},{28,20},{1,9},{5... | collective-permute-start | bytes 1572872 | tf_op jit(solution)/shard_map/ppermute | solution.py:725
  147.5 24.9 %collective-permute-start.28 = (bf16[1,1,4,128,512]{4,3,2,1,0:T(8,128)(2,1)S(1)}, bf16[1,1,4,128,512]{4,3,2,1,0:T(8,128)(2,1)S(1)}, u32[]{:S(2)}, u32[]{:S(2)}) collective-permute-start(bf16[1,1,4,128,512]{4,3,2,1,0:T(8,128)(2,1)S(1)} %maximum_select_fusion.17), channel_id=1, source_target_pairs={{0,16},{4,20},{8,24},{12,28},{16,0},{20,4},{24,8},{28,12},{1,17},{... | collective-permute-start | bytes 1572872 | tf_op jit(solution)/shard_map/ppermute | solution.py:725
  172.6 32.3 %collective-permute-start.30 = (bf16[2,1,4,128,512]{4,3,2,1,0:T(8,128)(2,1)S(1)}, bf16[2,1,4,128,512]{4,3,2,1,0:T(8,128)(2,1)S(1)}, u32[]{:S(2)}, u32[]{:S(2)}) collective-permute-start(bf16[2,1,4,128,512]{4,3,2,1,0:T(8,128)(2,1)S(1)} %maximum_select_fusion.8), channel_id=1, source_target_pairs={{0,8},{4,12},{8,0},{12,4},{16,24},{20,28},{24,16},{28,20},{1,9},{5... | collective-permute-start | bytes 3145736 | tf_op jit(solution)/shard_map/ppermute | solution.py:725
  175.5 29.4 %collective-permute-start.29 = (bf16[1,2,4,128,512]{4,3,2,1,0:T(8,128)(2,1)S(1)}, bf16[1,2,4,128,512]{4,3,2,1,0:T(8,128)(2,1)S(1)}, u32[]{:S(2)}, u32[]{:S(2)}) collective-permute-start(bf16[1,2,4,128,512]{4,3,2,1,0:T(8,128)(2,1)S(1)} %maximum_select_fusion.7), channel_id=1, source_target_pairs={{0,16},{4,20},{8,24},{12,28},{16,0},{20,4},{24,8},{28,12},{1,17},{... | collective-permute-start | bytes 3145736 | tf_op jit(solution)/shard_map/ppermute | solution.py:725
  314.7 48.1 %collective-permute-start.36 = (bf16[2,1,4,128,1024]{4,3,2,1,0:T(8,128)(2,1)}, bf16[2,1,4,128,1024]{4,3,2,1,0:T(8,128)(2,1)}, u32[]{:S(2)}, u32[]{:S(2)}) collective-permute-start(bf16[2,1,4,128,1024]{4,3,2,1,0:T(8,128)(2,1)} %get-tuple-element.453.refs_9_), channel_id=1, source_target_pairs={{0,8},{4,12},{8,0},{12,4},{16,24},{20,28},{24,16},{28,20},{1,9},{5... | collective-permute-start | bytes 6291464 | tf_op jit(solution)/shard_map/ppermute | solution.py:725
  319.6 47.7 %collective-permute-start.35 = (bf16[1,2,4,128,1024]{4,3,2,1,0:T(8,128)(2,1)S(1)}, bf16[1,2,4,128,1024]{4,3,2,1,0:T(8,128)(2,1)}, u32[]{:S(2)}, u32[]{:S(2)}) collective-permute-start(bf16[1,2,4,128,1024]{4,3,2,1,0:T(8,128)(2,1)S(1)} %get-tuple-element.455.refs_8_), channel_id=1, source_target_pairs={{0,16},{4,20},{8,24},{12,28},{16,0},{20,4},{24,8},{28,12},{1,17},{... | collective-permute-start | bytes 6291464 | tf_op jit(solution)/shard_map/ppermute | solution.py:725
  369.9 31.5 %collective-permute-start.38 = (bf16[1,1,4,128,1024]{4,3,2,1,0:T(8,128)(2,1)}, bf16[1,1,4,128,1024]{4,3,2,1,0:T(8,128)(2,1)S(1)}, u32[]{:S(2)}, u32[]{:S(2)}) collective-permute-start(bf16[1,1,4,128,1024]{4,3,2,1,0:T(8,128)(2,1)} %add_convert_fusion.8.refs_9_), channel_id=1, source_target_pairs={{0,16},{4,20},{8,24},{12,28},{16,0},{20,4},{24,8},{28,12},{1,17},{... | collective-permute-start | bytes 3145736 | tf_op jit(solution)/shard_map/ppermute | solution.py:725
  372.9 28.6 %collective-permute-start.37 = (bf16[1,1,4,128,1024]{4,3,2,1,0:T(8,128)(2,1)}, bf16[1,1,4,128,1024]{4,3,2,1,0:T(8,128)(2,1)S(1)}, u32[]{:S(2)}, u32[]{:S(2)}) collective-permute-start(bf16[1,1,4,128,1024]{4,3,2,1,0:T(8,128)(2,1)} %add_convert_fusion.9.refs_8_), channel_id=1, source_target_pairs={{0,8},{4,12},{8,0},{12,4},{16,24},{20,28},{24,16},{28,20},{1,9},{5... | collective-permute-start | bytes 3145736 | tf_op jit(solution)/shard_map/ppermute | solution.py:725
  374.4 27.1 %collective-permute-start.39 = (bf16[4,2,2,128,256]{4,3,2,1,0:T(8,128)(2,1)}, bf16[4,2,2,128,256]{4,3,2,1,0:T(8,128)(2,1)S(1)}, u32[]{:S(2)}, u32[]{:S(2)}) collective-permute-start(bf16[4,2,2,128,256]{4,3,2,1,0:T(8,128)(2,1)} %get-tuple-element.319), channel_id=1, source_target_pairs={{0,4},{4,0},{8,12},{12,8},{16,20},{20,16},{24,28},{28,24},{1,5},{5... | collective-permute-start | bytes 3145736 | tf_op jit(solution)/shard_map/ppermute | solution.py:725
  374.4 27.1 %collective-permute-start.40 = (bf16[4,2,2,128,256]{4,3,2,1,0:T(8,128)(2,1)}, bf16[4,2,2,128,256]{4,3,2,1,0:T(8,128)(2,1)}, u32[]{:S(2)}, u32[]{:S(2)}) collective-permute-start(bf16[4,2,2,128,256]{4,3,2,1,0:T(8,128)(2,1)} %get-tuple-element.320), channel_id=1, source_target_pairs={{0,4},{4,0},{8,12},{12,8},{16,20},{20,16},{24,28},{28,24},{1,5},{5... | collective-permute-start | bytes 3145736 | tf_op jit(solution)/shard_map/ppermute | solution.py:725
  423.1 22.4 %collective-permute-start.45 = (bf16[4,2,2,128,256]{4,3,2,1,0:T(8,128)(2,1)}, bf16[4,2,2,128,256]{4,3,2,1,0:T(8,128)(2,1)S(1)}, u32[]{:S(2)}, u32[]{:S(2)}) collective-permute-start(bf16[4,2,2,128,256]{4,3,2,1,0:T(8,128)(2,1)} %get-tuple-element.340), channel_id=1, source_target_pairs={{0,4},{4,0},{8,12},{12,8},{16,20},{20,16},{24,28},{28,24},{1,5},{5... | collective-permute-start | bytes 3145736 | tf_op jit(solution)/shard_map/ppermute | solution.py:725
  423.1 22.4 %collective-permute-start.46 = (bf16[4,2,2,128,256]{4,3,2,1,0:T(8,128)(2,1)}, bf16[4,2,2,128,256]{4,3,2,1,0:T(8,128)(2,1)S(1)}, u32[]{:S(2)}, u32[]{:S(2)}) collective-permute-start(bf16[4,2,2,128,256]{4,3,2,1,0:T(8,128)(2,1)} %get-tuple-element.341), channel_id=1, source_target_pairs={{0,4},{4,0},{8,12},{12,8},{16,20},{20,16},{24,28},{28,24},{1,5},{5... | collective-permute-start | bytes 3145736 | tf_op jit(solution)/shard_map/ppermute | solution.py:725
  424.7 20.8 %collective-permute-start.44 = (bf16[1,1,2,2,128,256]{5,4,3,2,1,0:T(8,128)(2,1)S(1)}, bf16[1,1,2,2,128,256]{5,4,3,2,1,0:T(8,128)(2,1)S(1)}, u32[]{:S(2)}, u32[]{:S(2)}) collective-permute-start(bf16[1,1,2,2,128,256]{5,4,3,2,1,0:T(8,128)(2,1)S(1)} %add_convert_fusion.38.refs_19_), channel_id=1, source_target_pairs={{0,16},{4,20},{8,24},{12,28},{16,0},{20,4},{24,8},{28,12},{1,17},{... | collective-permute-start | bytes 786440 | tf_op jit(solution)/shard_map/ppermute | solution.py:725
  426.6 18.9 %collective-permute-start.43 = (bf16[1,1,2,2,128,256]{5,4,3,2,1,0:T(8,128)(2,1)S(1)}, bf16[1,1,2,2,128,256]{5,4,3,2,1,0:T(8,128)(2,1)S(1)}, u32[]{:S(2)}, u32[]{:S(2)}) collective-permute-start(bf16[1,1,2,2,128,256]{5,4,3,2,1,0:T(8,128)(2,1)S(1)} %add_convert_fusion.39.refs_18_), channel_id=1, source_target_pairs={{0,8},{4,12},{8,0},{12,4},{16,24},{20,28},{24,16},{28,20},{1,9},{5... | collective-permute-start | bytes 786440 | tf_op jit(solution)/shard_map/ppermute | solution.py:725
  448.7 103.8 %reduce-scatter.5.cloned.1.call-start = ((), (), s32[]{:S(2)}) async-start(), calls=%async_computation.3 | async-start | bytes 1310720 | tf_op jit(solution)/shard_map/reduce_scatter | solution.py:830
  481.8 22.1 %collective-permute-start.55 = (bf16[1,2,4,32,1536]{4,3,2,1,0:T(8,128)(2,1)S(1)}, bf16[1,2,4,32,1536]{4,3,2,1,0:T(8,128)(2,1)S(1)}, u32[]{:S(2)}, u32[]{:S(2)}) collective-permute-start(bf16[1,2,4,32,1536]{4,3,2,1,0:T(8,128)(2,1)S(1)} %get-tuple-element.461.refs_8_), channel_id=1, source_target_pairs={{0,16},{4,20},{8,24},{12,28},{16,0},{20,4},{24,8},{28,12},{1,17},{... | collective-permute-start | bytes 2359304 | tf_op jit(solution)/shard_map/ppermute | solution.py:725
  484.8 19.1 %collective-permute-start.54 = (bf16[2,1,4,32,1536]{4,3,2,1,0:T(8,128)(2,1)S(1)}, bf16[2,1,4,32,1536]{4,3,2,1,0:T(8,128)(2,1)S(1)}, u32[]{:S(2)}, u32[]{:S(2)}) collective-permute-start(bf16[2,1,4,32,1536]{4,3,2,1,0:T(8,128)(2,1)S(1)} %get-tuple-element.463.refs_7_), channel_id=1, source_target_pairs={{0,8},{4,12},{8,0},{12,4},{16,24},{20,28},{24,16},{28,20},{1,9},{5... | collective-permute-start | bytes 2359304 | tf_op jit(solution)/shard_map/ppermute | solution.py:725
  522.8 23.8 %collective-permute-start.60 = (bf16[32,3072]{1,0:T(8,128)(2,1)S(1)}, bf16[32,3072]{1,0:T(8,128)(2,1)S(1)}, u32[]{:S(2)}, u32[]{:S(2)}) collective-permute-start(bf16[32,3072]{1,0:T(8,128)(2,1)S(1)} %get-tuple-element.478), channel_id=1, source_target_pairs={{0,1},{1,2},{2,3},{3,0},{4,5},{5,6},{6,7},{7,4},{8,9},{9,10},{10,1... | collective-permute-start | bytes 589832 | tf_op jit(solution)/shard_map/ppermute | solution.py:764
  524.4 25.4 %collective-permute-start.61 = (bf16[32,3072]{1,0:T(8,128)(2,1)S(1)}, bf16[32,3072]{1,0:T(8,128)(2,1)S(1)}, u32[]{:S(2)}, u32[]{:S(2)}) collective-permute-start(bf16[32,3072]{1,0:T(8,128)(2,1)S(1)} %get-tuple-element.479), channel_id=1, source_target_pairs={{0,2},{1,3},{2,0},{3,1},{4,6},{5,7},{6,4},{7,5},{8,10},{9,11},{10,... | collective-permute-start | bytes 589832 | tf_op jit(solution)/shard_map/ppermute | solution.py:764
  525.8 25.9 %collective-permute-start.62 = (bf16[32,3072]{1,0:T(8,128)(2,1)S(1)}, bf16[32,3072]{1,0:T(8,128)(2,1)S(1)}, u32[]{:S(2)}, u32[]{:S(2)}) collective-permute-start(bf16[32,3072]{1,0:T(8,128)(2,1)S(1)} %get-tuple-element.480), channel_id=1, source_target_pairs={{0,3},{1,0},{2,1},{3,2},{4,7},{5,4},{6,5},{7,6},{8,11},{9,8},{10,9... | collective-permute-start | bytes 589832 | tf_op jit(solution)/shard_map/ppermute | solution.py:764
  (109 other events, 1058.6 us)
Sparse Core Ops, SparseCore 0:
  87.9 101.9 all-gather.2
  448.9 42.7 reduce-scatter.2
  509.4 40.2 reduce-scatter.4

commit v3 on v2

--- a/solution.py
+++ b/solution.py
@@ -97,7 +97,7 @@
     return jax.ShapeDtypeStruct(shape, dtype)
 
 
-def split_kernel(core, array, out, turned, *, wide):
+def split_kernel(core, array, out, *, wide):
     half = out.shape[1] // 2
     for place in range(half // wide):
         even = array[:, 2 * place * wide : (2 * place + 1) * wide]
@@ -105,7 +105,6 @@
         at = place * wide
         out[:, at : at + wide] = jnp.where(core[0] == 0, even, odd)
         out[:, half + at : half + at + wide] = jnp.where(core[0] == 0, odd, even)
-    turned[...] = out[...].T
 
 
 def turned_tile(shape):
@@ -118,11 +117,11 @@
         partial(split_kernel, wide=wide),
         (array.shape[0] // TILE,),
         [tile],
-        [tile, turned_tile(array.shape)],
-        [shaped(array.shape, array.dtype), shaped(array.shape[::-1], array.dtype)],
+        [tile],
+        [shaped(array.shape, array.dtype)],
         (array,),
         scalars=(core,),
-    )
+    )[0]
 
 
 def shares_kernel(expand, contract, e_low, c_low, high):
@@ -147,9 +146,10 @@
     )
 
 
-def output_kernel(core, stream, one, two, bias, out, *, wide):
+def output_kernel(core, *refs, wide):
+    *parts, bias, out = refs
     half = out.shape[1] // 2
-    total = stream[...] + one[...] + two[...] + bias[...]
+    total = sum(part[...].astype(F32) for part in parts) + bias[...]
     if wide % LANES:
         out[...] = total
         return
@@ -160,34 +160,37 @@
         out[:, 2 * at + wide : 2 * at + 2 * wide] = jnp.where(core[0] == 0, other, own)
 
 
-def output_rows(core, stream, one, two, bias, wide, after=()):
-    tile = row_tile(stream.shape)
+def output_rows(core, parts, bias, wide, after=()):
+    tile = row_tile(parts[0].shape)
     return call(
         partial(output_kernel, wide=wide),
-        (stream.shape[0] // TILE,),
-        [tile] * 3 + [whole(bias.shape)],
+        (parts[0].shape[0] // TILE,),
+        [tile] * len(parts) + [whole(bias.shape)],
         [tile],
-        [shaped(stream.shape, F32)],
-        (stream, one, two, bias),
+        [shaped(parts[0].shape, F32)],
+        tuple(parts) + (bias,),
         scalars=(core,),
         after=after,
     )[0]
 
 
-def finish_feed_kernel(blocks, expand, contract):
-    expand[...] = blocks[0].astype(F32)
-    contract[...] = blocks[1].astype(F32).T
-
-
-def finish_feed(blocks):
-    _, wide, unit = blocks.shape
+def finish_feed_kernel(low, high, expand, contract):
+    part = low.shape[2]
+    for at, ref in ((0, low), (part, high)):
+        expand[:, at : at + part] = ref[0].astype(F32)
+        contract[at : at + part, :] = ref[1].astype(F32).T
+
+
+def finish_feed(low, high, after=()):
+    _, wide, part = low.shape
     return call(
         finish_feed_kernel,
         (1,),
-        [whole(blocks.shape)],
-        [whole((wide, unit)), whole((unit, wide))],
-        [shaped((wide, unit), F32), shaped((unit, wide), F32)],
-        (blocks,),
+        [whole(low.shape)] * 2,
+        [whole((wide, 2 * part)), whole((2 * part, wide))],
+        [shaped((wide, 2 * part), F32), shaped((2 * part, wide), F32)],
+        (low, high),
+        after=after,
     )
 
 
@@ -208,11 +211,24 @@
     )
 
 
-def group_rows(band, group, values):
-    return jnp.where(band == group, values, jnp.zeros_like(values))
-
-
-def embed_kernel(present, pix, band, sin_own, cos_own, sin_came, cos_came, bias, gain, shift, lo_own, lo_came, hi_own, hi_came, stream, normed, turned, acc):
+def marks_kernel(rows, columns):
+    columns[...] = rows[...].T
+
+
+def marks_of(*rows):
+    count = rows[0].shape[0]
+    rows = jnp.stack(rows + (jnp.zeros((count,), jnp.int32),) * (8 - len(rows))).astype(F32)
+    columns = call(
+        marks_kernel, (1,), [whole(rows.shape)], [whole((count, 8))], [shaped((count, 8), F32)], (rows,)
+    )[0]
+    return rows, columns
+
+
+def group_rows(marks, group, values):
+    return jnp.where(marks[:, 0:1] == jnp.asarray(group, F32), values, jnp.zeros_like(values))
+
+
+def embed_kernel(present, pix, band, sin_own, cos_own, sin_came, cos_came, bias, gain, shift, lo_own, lo_came, hi_own, hi_came, stream, normed, acc):
     tile = pl.program_id(0)
     half = acc.shape[1] // 2
     width = pix.shape[1]
@@ -229,11 +245,9 @@
 
     total = acc[...]
     for group in range(GROUPS):
-        total = total + jnp.where(band[...] == group, bias[group : group + 1, :], 0.0)
+        total = total + jnp.where(band[:, 0:1] == float(group), bias[group : group + 1, :], 0.0)
     stream[...] = total
-    rows = (normalize(total)[0] * gain[...] + shift[...]).astype(BF16)
-    normed[...] = rows
-    turned[...] = rows.T
+    normed[...] = (normalize(total)[0] * gain[...] + shift[...]).astype(BF16)
 
 
 def embed(present, pixels, band, table, bias, gain, shift, patches, after=()):
@@ -244,8 +258,8 @@
         embed_kernel,
         (rows // TILE,),
         specs,
-        [row_tile((rows, model))] * 2 + [turned_tile((rows, model))],
-        [shaped((rows, model), F32), shaped((rows, model), BF16), shaped((model, rows), BF16)],
+        [row_tile((rows, model))] * 2,
+        [shaped((rows, model), F32), shaped((rows, model), BF16)],
         args,
         scratch=[pltpu.VMEM((TILE, model), F32)],
         flops=4 * rows * pixels.shape[1] * model,
@@ -296,7 +310,7 @@
 
     @pl.when(pl.program_id(0) == 0)
     def _():
-        bias_ref[...] = jnp.where(seg_col_ref[...] == seg_row_ref[...], 0.0, -1e30).astype(F32)
+        bias_ref[...] = jnp.where(seg_col_ref[:, 1:2] == seg_row_ref[1:2, :], 0.0, -1e30).astype(F32)
         log_ref[...] = jnp.zeros_like(log_ref)
 
     keys = k_ref[...]
@@ -325,7 +339,7 @@
     return call(
         partial(attend_kernel, base=base + skip),
         (pairs,),
-        [block, block, block, whole((rows, 1)), whole((1, rows))],
+        [block, block, block, whole((rows, 8)), whole((8, rows))],
         [pl.BlockSpec((rows, LANES), lambda i: (0, i)), whole((rows, LANES))],
         [shaped((rows, width), BF16), shaped((rows, LANES), F32)],
         (query, key, value) + seg,
@@ -344,7 +358,7 @@
 
     @pl.when(pl.program_id(0) == 0)
     def _():
-        bias_ref[...] = jnp.where(seg_col_ref[...] == seg_row_ref[...], 0.0, -1e30).astype(F32)
+        bias_ref[...] = jnp.where(seg_col_ref[:, 1:2] == seg_row_ref[1:2, :], 0.0, -1e30).astype(F32)
 
     query = q_ref[...] * jnp.asarray(HEAD_DIM ** (-0.5), BF16)
     grads = g_ref[...]
@@ -387,7 +401,7 @@
     return call(
         partial(attend_back_kernel, base=base),
         (pairs,),
-        [given] * 3 + [taken, whole((rows, 1)), whole((1, rows)), whole(log_rows.shape), whole(delta_rows.shape)],
+        [given] * 3 + [taken, whole((rows, 8)), whole((8, rows)), whole(log_rows.shape), whole(delta_rows.shape)],
         [given] * 3 + [pl.BlockSpec((2, LANES), lambda i: (0, i))],
         [shaped((rows, width), BF16)] * 3 + [shaped((2, width), F32)],
         (query, key, value, grads) + seg + (log_rows, delta_rows),
@@ -400,33 +414,34 @@
 
 def merge_kernel(*refs, count):
     attended = beside(refs[:count])
-    stream, bias, gain, shift, own_low, own_high, came_low, came_high, stream_one, normed, turned = refs[count:]
+    logs = sum(ref[...] for ref in refs[count : 2 * count])
+    stream, bias, gain, shift, own_low, own_high, came_low, came_high = refs[2 * count : 2 * count + 8]
+    stream_one, normed, log_rows = refs[2 * count + 8 :]
+    log_rows[...] = logs.T
     half = stream.shape[1] // 2
     stream_one[:, :half] = stream[:, :half] + dot(attended, joined((own_low, own_high), 0, 1), NT)
     stream_one[:, half:] = stream[:, half:] + dot(attended, joined((came_low, came_high), 0, 1), NT)
     total = stream_one[...] + bias[...]
     stream_one[...] = total
-    rows = (normalize(total)[0] * gain[...] + shift[...]).astype(BF16)
-    normed[...] = rows
-    turned[...] = rows.T
+    normed[...] = (normalize(total)[0] * gain[...] + shift[...]).astype(BF16)
 
 
 def first_two(array):
     return pl.BlockSpec(array.shape[:2] + (2,) + array.shape[3:], lambda *_: (0,) * array.ndim)
 
 
-def merge(attended, stream, bias, gain, shift, weights, after=()):
+def merge(attended, logs, stream, bias, gain, shift, weights, after=()):
     rows, model = stream.shape
     return call(
         partial(merge_kernel, count=len(attended)),
         (rows // TILE,),
-        [row_tile(a.shape) for a in attended]
+        [row_tile(a.shape) for a in tuple(attended) + tuple(logs)]
         + [row_tile(stream.shape)]
         + [whole((1, model))] * 3
         + [first_two(a) for a in weights],
-        [row_tile((rows, model))] * 2 + [turned_tile((rows, model))],
-        [shaped((rows, model), F32), shaped((rows, model), BF16), shaped((model, rows), BF16)],
-        tuple(attended) + (stream, bias, gain, shift) + weights,
+        [row_tile((rows, model))] * 2 + [turned_tile((rows, LANES))],
+        [shaped((rows, model), F32), shaped((rows, model), BF16), shaped((LANES, rows), F32)],
+        tuple(attended) + tuple(logs) + (stream, bias, gain, shift) + weights,
         flops=2 * rows * model * model,
         after=after,
     )
@@ -444,67 +459,62 @@
     return hidden * below, below + (hidden * (1.0 / math.sqrt(2.0 * math.pi))) * bell
 
 
-def feed_kernel(
-    x_ref, xt_ref, g_ref, gt_ref, e_own, e_other, c_own, c_other, b_ref, y_ref, d_ref, *grads
-):
-    e_keep, e_send, c_keep, c_send, db_ref, a_ref, h_ref = grads
+def feed_kernel(x_ref, g_ref, e_own, e_other, c_own, c_other, b_ref, y_ref, d_ref, *refs):
+    e_keep, e_send, c_keep, c_send, db_ref, a_ref, h_ref, y_sum, d_sum = refs
     step = pl.program_id(0)
-    rows, model = x_ref.shape
-    half = model // 2
+    half = x_ref.shape[1] // 2
 
     @pl.when(step == 0)
     def _():
-        y_ref[...] = jnp.zeros_like(y_ref)
-        d_ref[...] = jnp.zeros_like(d_ref)
-
-    expand = (merged(e_own[...]), merged(e_other[...]))
-    contract = (merged(c_own[...]), merged(c_other[...]))
-    sums = jnp.zeros((1, h_ref.shape[1]), F32)
-    for start in range(0, rows, TILE):
-        at = pl.ds(start, TILE)
-        hidden = dot(x_ref[at, :half], expand[0]) + dot(x_ref[at, half:], expand[1]) + b_ref[0]
-        grad_active = dot(g_ref[at, :half], contract[0]) + dot(g_ref[at, half:], contract[1])
-        active, slope = gelu_parts(hidden)
-        active = active.astype(BF16)
-        grad_hidden = (grad_active * slope).astype(BF16)
-        a_ref[at, :] = active
-        h_ref[at, :] = grad_hidden
-        sums = sums + jnp.sum(grad_hidden.astype(F32), axis=0, keepdims=True)
-        for side in range(2):
-            cols = pl.ds(side * half, half)
-            y_ref[at, cols] += dot(active, contract[side], NT)
-            d_ref[at, cols] += dot(grad_hidden, expand[side], NT)
-    db_ref[0] = sums
+        y_sum[...] = jnp.zeros_like(y_sum)
+        d_sum[...] = jnp.zeros_like(d_sum)
+
+    expand = jnp.concatenate([merged(e_own[...]), merged(e_other[...])], axis=0)
+    contract = jnp.concatenate([merged(c_own[...]), merged(c_other[...])], axis=0)
+    hidden = dot(x_ref[...], expand) + b_ref[0]
+    grad_active = dot(g_ref[...], contract)
+    active, slope = gelu_parts(hidden)
+    a_ref[...] = active.astype(BF16)
+    grad_hidden = (grad_active * slope).astype(BF16)
+    h_ref[...] = grad_hidden
+    db_ref[0] = jnp.sum(grad_hidden.astype(F32), axis=0, keepdims=True)
+    y_sum[...] += dot(a_ref[...], contract, NT)
+    d_sum[...] += dot(h_ref[...], expand, NT)
     for side, (e_ref, c_ref) in enumerate(((e_keep, c_keep), (e_send, c_send))):
         cols = pl.ds(side * half, half)
         shape = e_ref.shape[:1] + e_ref.shape[2:]
-        e_ref[:, 0] = dot(xt_ref[cols, :], h_ref[...]).astype(BF16).reshape(shape)
-        c_ref[:, 0] = dot(gt_ref[cols, :], a_ref[...]).astype(BF16).reshape(shape)
-
-
-def feed(core, rows_two, turned_two, top, turned_top, weights, bias, which, filled=(), after=()):
+        e_ref[:, 0] = dot(x_ref[:, cols], h_ref[...], TN).astype(BF16).reshape(shape)
+        c_ref[:, 0] = dot(g_ref[:, cols], a_ref[...], TN).astype(BF16).reshape(shape)
+
+    @pl.when(step == pl.num_programs(0) - 1)
+    def _():
+        y_ref[...] = y_sum[...].astype(BF16)
+        d_ref[...] = d_sum[...].astype(BF16)
+
+
+def feed(core, rows_two, top, weights, bias, base, steps, filled=(), after=()):
     rows, model = rows_two.shape
-    steps, _, part = bias.shape
+    blocks, _, part = bias.shape
     pairs, wide = weights[0].shape[0], weights[0].shape[-2]
     if len(weights) == 1:
         weights = weights * 4
         block = (pairs, 1, 1, 1, wide, part)
-        place = lambda side, mat: lambda i, core: (0, core[0] if side == 0 else 1 - core[0], i, mat, 0, 0)
+        place = lambda side, mat: lambda i, core: (0, core[0] if side == 0 else 1 - core[0], base + i, mat, 0, 0)
         specs = [pl.BlockSpec(block, place(side, mat)) for mat in range(2) for side in range(2)]
     else:
-        specs = [pl.BlockSpec((pairs, 1, wide, part), lambda i, core: (0, i, 0, 0))] * 4
-    grad = pl.BlockSpec((pairs, 1, wide, part), lambda i, core: (0, i, 0, which))
-    unit = pl.BlockSpec((1, 1, part), lambda i, core: (i, 0, 0))
+        specs = [pl.BlockSpec((pairs, 1, wide, part), lambda i, core: (0, base + i, 0, 0))] * 4
+    grad = pl.BlockSpec((pairs, 1, wide, part), lambda i, core: (0, base + i, 0, 0))
+    unit = pl.BlockSpec((1, 1, part), lambda i, core: (base + i, 0, 0))
     return call(
         lambda core, *refs: feed_kernel(*refs),
         (steps,),
-        [whole((rows, model)), whole((model, rows))] * 2 + specs + [unit],
+        [whole((rows, model))] * 2 + specs + [unit],
         [whole((rows, model))] * 2 + [grad] * 4 + [unit],
-        [shaped((rows, model), F32)] * 2
-        + [shaped((pairs, steps, wide, 2 * part), BF16)] * 4
-        + [shaped((steps, 1, part), F32)],
-        (rows_two, turned_two, top, turned_top) + tuple(weights) + (bias,),
-        scratch=[pltpu.VMEM((rows, part), BF16)] * 2,
+        [shaped((rows, model), BF16)] * 2
+        + [shaped((pairs, blocks, wide, part), BF16)] * 4
+        + [shaped((blocks, 1, part), F32)],
+        (rows_two, top) + tuple(weights) + (bias,),
+        scratch=[pltpu.VMEM((rows, part), BF16)] * 2 + [pltpu.VMEM((rows, model), F32)] * 2,
         flops=12 * rows * model * part * steps,
         exps=rows * part * steps,
         scalars=(core,),
@@ -513,18 +523,19 @@
     )
 
 
-def merge_back_kernel(*refs, count):
+def merge_back_kernel(*refs, count, parts):
     attended = beside(refs[:count])
-    d_one, d_two, top, stream_one, gain, own_low, own_high, came_low, came_high, heads = refs[count : count + 10]
-    grad_stream, turned, grad_attended, delta, sums = refs[count + 10 :]
+    grad_two = sum(ref[...].astype(F32) for ref in refs[count : count + parts])
+    refs = refs[count + parts :]
+    top, stream_one, gain, own_low, own_high, came_low, came_high, heads = refs[:8]
+    grad_stream, branch, grad_attended, delta, sums = refs[8:]
     half = top.shape[1] // 2
-    grad_two = d_one[...] + d_two[...]
     normed, scale = normalize(stream_one[...])
     cotangent = top[...].astype(F32)
     total = cotangent + normalize_back(grad_two * gain[...], normed, scale)
     grad_stream[...] = total
     low = total.astype(BF16)
-    turned[...] = low.T
+    branch[...] = low
     grads = dot(low[:, :half], joined((own_low, own_high), 0, 1)) + dot(low[:, half:], joined((came_low, came_high), 0, 1))
     grads = grads.astype(BF16)
     grad_attended[...] = grads
@@ -540,37 +551,39 @@
         sums[row : row + 1, :] += jnp.sum(part, axis=0, keepdims=True)
 
 
-def merge_back(attended, d_one, d_two, top, stream_one, gain, weights, heads, after=()):
+def merge_back(attended, grads, top, stream_one, gain, weights, heads, after=()):
     rows, model = stream_one.shape
     tile = row_tile((rows, model))
     return call(
-        partial(merge_back_kernel, count=len(attended)),
+        partial(merge_back_kernel, count=len(attended), parts=len(grads)),
         (rows // TILE,),
         [row_tile(a.shape) for a in attended]
-        + [tile] * 4
+        + [tile] * (len(grads) + 2)
         + [whole((1, model))]
         + [first_two(a) for a in weights]
         + [whole(heads.shape)],
-        [tile, turned_tile((rows, model)), tile]
+        [tile] * 3
         + [pl.BlockSpec((heads.shape[0], TILE), lambda i: (0, i)), whole((8, model))],
         [
             shaped((rows, model), F32),
-            shaped((model, rows), BF16),
+            shaped((rows, model), BF16),
             shaped((rows, model), BF16),
             shaped((heads.shape[0], rows), F32),
             shaped((8, model), F32),
         ],
-        tuple(attended) + (d_one, d_two, top, stream_one, gain) + weights + (heads,),
+        tuple(attended) + tuple(grads) + (top, stream_one, gain) + weights + (heads,),
         flops=2 * rows * model * model,
         after=after,
     )
 
 
 def attention_grads_kernel(*refs, count):
-    xt, bt = refs[:2]
+    x, branch, xt, bt = refs[0], refs[1], refs[-2], refs[-1]
+    xt[...] = x[...].T
+    bt[...] = branch[...].T
     inputs = [beside(refs[2 + i * count : 2 + (i + 1) * count]) for i in range(3)]
-    inputs.append(beside(refs[2 + 3 * count : -4]))
-    outs = refs[-4:]
+    inputs.append(beside(refs[2 + 3 * count : -6]))
+    outs = refs[-6:-2]
     half = xt.shape[0] // 2
     blocks, steps, _, wide, columns = outs[0].shape
     for place, right in enumerate(inputs):
@@ -583,12 +596,12 @@
                 ref[:, step, place % 2] = part.reshape(blocks, wide, columns)
 
 
-def attention_grads(xt, bt, query, key, value, attended, blocks, columns, after=()):
-    model, rows = xt.shape
+def attention_grads(x, branch, query, key, value, attended, blocks, columns, after=()):
+    rows, model = x.shape
     count = len(query)
     width = sum(a.shape[1] for a in query)
     shape = (blocks, width // columns, 2, model // (2 * blocks), columns)
-    args = (xt, bt) + tuple(query) + tuple(key) + tuple(value) + tuple(attended)
+    args = (x, branch) + tuple(query) + tuple(key) + tuple(value) + tuple(attended)
     return call(
         partial(attention_grads_kernel, count=count),
         (1,),
@@ -596,6 +609,7 @@
         [whole(shape)] * 4,
         [shaped(shape, BF16)] * 4,
         args,
+        scratch=[pltpu.VMEM((model, rows), BF16)] * 2,
         flops=8 * rows * model * width,
         after=after,
     )
@@ -605,8 +619,8 @@
     grads = [beside(refs[i * count : (i + 1) * count]) for i in range(3)]
     rest = refs[3 * count :]
     grad_stream, stream, band, gain = rest[:4]
-    weights = rest[4:-4]
-    grad_embed, turned, sums, acc = rest[-4:]
+    weights = rest[4:-3]
+    grad_embed, sums, acc = rest[-3:]
     half = stream.shape[1] // 2
     each = len(weights) // 2
     for side in range(2):
@@ -617,9 +631,7 @@
     grad_one = acc[...]
     normed, scale = normalize(stream[...])
     total = grad_stream[...] + normalize_back(grad_one * gain[...], normed, scale)
-    low = total.astype(BF16)
-    grad_embed[...] = low
-    turned[...] = low.T
+    grad_embed[...] = total.astype(BF16)
 
     @pl.when(pl.program_id(0) == 0)
     def _():
@@ -641,8 +653,8 @@
         + [tile] * 2
         + [row_tile(band.shape), whole((1, model))]
         + [whole(a.shape) for a in weights],
-        [tile, turned_tile((rows, model)), whole((8, model))],
-        [shaped((rows, model), BF16), shaped((model, rows), BF16), shaped((8, model), F32)],
+        [tile, whole((8, model))],
+        [shaped((rows, model), BF16), shaped((8, model), F32)],
         parts + (grad_stream, stream, band, gain) + weights,
         scratch=[pltpu.VMEM((TILE, model), F32)],
         flops=6 * rows * model * model,
@@ -650,35 +662,40 @@
     )
 
 
-def patch_grads_kernel(present, gt, pix, band, keep, send, acc, *, base):
-    group = base + pl.program_id(0)
-    half = gt.shape[0] // 2
+def patch_grads_kernel(present, grads, pix, band, lo_keep, lo_send, hi_keep, hi_send, acc):
+    group = pl.program_id(0)
+    half = grads.shape[1] // 2
     acc[...] = jnp.zeros_like(acc)
     for tile in range(pix.shape[0] // TILE):
 
         @pl.when(present[tile * GROUPS + group] > 0)
         def _():
             at = pl.ds(tile * TILE, TILE)
-            acc[...] += dot(gt[:, at], group_rows(band[at, :], group, pix[at, :]))
-
-    keep[...] = acc[:half, :].astype(BF16)
-    send[...] = acc[half:, :].astype(BF16)
-
-
-def patch_grads(present, turned, pixels, band, base, after=()):
-    model, rows = turned.shape
+            acc[...] += dot(grads[at, :], group_rows(band[at, :], group, pix[at, :]), TN)
+
+    for place, (keep, send) in enumerate(((lo_keep, lo_send), (hi_keep, hi_send))):
+
+        @pl.when(group // 2 == place)
+        def _():
+            keep[...] = acc[:half, :].astype(BF16)
+            send[...] = acc[half:, :].astype(BF16)
+
+
+def patch_grads(present, grads, pixels, band, after=()):
+    rows, model = grads.shape
     width = pixels.shape[1]
     count = GROUPS // 2
-    given = pl.BlockSpec((model // 2, width), lambda i, present: (0, i))
-    return call(
-        partial(patch_grads_kernel, base=base),
-        (count,),
-        [whole(turned.shape), whole(pixels.shape), whole(band.shape)],
-        [given] * 2,
-        [shaped((model // 2, count * width), BF16)] * 2,
-        (turned, pixels, band),
+    low = pl.BlockSpec((model // 2, width), lambda i, present: (0, jnp.minimum(i, count - 1)))
+    high = pl.BlockSpec((model // 2, width), lambda i, present: (0, jnp.maximum(i - count, 0)))
+    return call(
+        patch_grads_kernel,
+        (GROUPS,),
+        [whole(grads.shape), whole(pixels.shape), whole(band.shape)],
+        [low, low, high, high],
+        [shaped((model // 2, count * width), BF16)] * 4,
+        (grads, pixels, band),
         scratch=[pltpu.VMEM((model, width), F32)],
-        flops=2 * rows * width * model,
+        flops=4 * rows * width * model,
         scalars=(present,),
         after=after,
     )
@@ -696,7 +713,7 @@
             at = pl.ds((group % 2) * width, width)
             own, came = (lo_own, lo_came) if group < 2 else (hi_own, hi_came)
             spread = dot(grads[:, :half], merged(own[:, :, at])) + dot(grads[:, half:], merged(came[:, :, at]))
-            out[...] = jnp.where(band[...] == group, spread, out[...])
+            out[...] = jnp.where(band[:, 0:1] == float(group), spread, out[...])
 
 
 def pixel_grads(present, grads, band, patches, width, after=()):
@@ -854,7 +871,7 @@
             [patch_bias, norm_gains, vector_biases, query_value_bias, expand_bias.reshape(-1, thin)], axis=0
         )
         extra = small.shape[0]
-        small = jnp.pad(small.T, ((0, 0), (0, LANES - extra)))
+        small = jnp.pad(lax.optimization_barrier(small).T, ((0, 0), (0, LANES - extra)))
         patch = jnp.concatenate([patch_weight.reshape(-1, thin).T, small], axis=1)
         attention = jnp.concatenate([attention_weight, merge_weight.T[None]], axis=0)[None]
         t_first, t_rest = t_bits[:1], t_bits[1:]
@@ -879,29 +896,28 @@
             held = pair.closed()
             return held, [other_core(a) for a in held]
 
-        band = band_group[:, None]
         present = jnp.any(band_group.reshape(-1, TILE, 1) == jnp.arange(GROUPS), axis=1).astype(jnp.int32).reshape(-1)
         came = shifts(lambda d: patch)
         e_one, c_one, feed_high = shares(expand_weight, contract_weight)
         e_one, c_one = e_one[None], c_one[None]
-        seg = (segment[:, None], segment[None, :])
+        mark_rows, band = marks_of(band_group, segment)
+        seg = (band, mark_rows)
         came, patch, attention, cotangent, e_one, band, present, seg = sync(
             (came, patch, attention, cotangent, e_one, band, present, seg)
         )
         patch = in_order(patch, came).reshape(tensor * thin, -1)
         patch = Pair(patch[:, :columns], patch[:, columns:])
         came = go(patch)
-        came_t = start_t(t_first, attention, e_one)
+        came_t = start_t(t_first, attention)
         if aligned:
-            top, turned_top = split_columns(core_at, cotangent, wide)
+            top = split_columns(core_at, cotangent, wide)
         else:
             top = to_split(cotangent)
-            turned_top = top.T
-        came, came_t, top, c_one, scaled_position = sync((came, came_t, top, c_one, scaled_position))
+        came, came_t, top, e_one, c_one, scaled_position = sync((came, came_t, top, e_one, c_one, scaled_position))
         done(came, patch)
-        attention, e_one = (over_t(w, c, t_first) for w, c in zip((attention, e_one), came_t))
+        attention = over_t(attention, came_t[0], t_first)
         came = go(patch)
-        came_t = start_t(t_rest, attention) + start_t(t_first, c_one)
+        came_t = start_t(t_rest, attention) + start_t(t_first, e_one, c_one)
         half_width = model // 2
         column = jnp.arange(model)
         place = column % half_width
@@ -912,11 +928,15 @@
         table = tuple(
             f(angles[:, i * quarter : (i + 1) * quarter]) for i, f in enumerate((jnp.sin, jnp.cos, jnp.sin, jnp.cos))
         )
-        came, came_t, table, e_one = sync((came, came_t, table, e_one))
+        hidden = jnp.arange(model)
+        owner, block = hidden // thin % fsdp, hidden // (thin * fsdp)
+        source = ((((owner & 1) ^ core) * pairs + owner // 2) * tensor + block) * thin + hidden % thin
+        to_hidden = (hidden[:, None] == source[None, :]).astype(BF16)
+        came, came_t, table, to_hidden = sync((came, came_t, table, to_hidden))
         done(came, patch)
         patch.drain()
         attention = over_t(attention, came_t[0], t_rest)
-        c_one = over_t(c_one, came_t[1], t_first)
+        e_one, c_one = (over_t(w, c, t_first) for w, c in zip((e_one, c_one), came_t[1:]))
         quarter, half_t = tensor // 4, tensor // 2
         outward = [
             attention[i * half_t : (i + 1) * half_t, 3].reshape(quarter, 2, wide, -1) for i in range(2)
@@ -926,28 +946,24 @@
         qkv_two = Pair(*(jnp.concatenate(two, axis=1) for two in zip(outward, qkv[2:])))
         patch = both_cores(patch)
         came, came_t = go(qkv_one), start_t(t_rest, e_one)
-        patch, came, came_t, c_one, feed_high = sync((patch, came, came_t, c_one, feed_high))
+        patch, came, came_t, c_one, band = sync((patch, came, came_t, c_one, band))
         patches = (patch[0][0], patch[1][0], patch[0][1], patch[1][1])
         done(came, qkv_one)
         e_one = over_t(e_one, came_t[0], t_rest)
         came, came_t = go(qkv_one), start_t(t_rest, c_one)
-        feed_high = lax.all_gather(feed_high, ("fsdp", "tensor"), axis=0, tiled=False)
-        feed_high = feed_high.reshape(pairs, 2, tensor, 2, wide, half_unit)
         small = [held[0] for held in (patch[0][1:], patch[1][1:])]
         small = jnp.stack([held[:, :, columns : columns + extra] for held in small]).astype(F32)
         vectors = small.reshape(model, extra).T
         patch_bias_rows = vectors[:GROUPS]
         gains = [vectors[GROUPS + i : GROUPS + i + 1] for i in range(2)]
         biases = [vectors[GROUPS + 2 + i : GROUPS + 3 + i] for i in range(4)]
-        by_hidden = small[:, :, :, n_vec:].reshape(2, pairs, tensor, thin, extra - n_vec)
-        by_hidden = jnp.where(core == 0, by_hidden, by_hidden[::-1]).transpose(4, 2, 1, 0, 3)
-        qv_rows = by_hidden[:2].reshape(2, model)
-        unit_bias = by_hidden[2:].reshape(-1, tensor, fsdp, thin).transpose(1, 2, 0, 3).reshape(tensor, 2, 1, half_unit)
-
-        stream_zero, input_one, turned_one = embed(
+        by_hidden = dot(vectors[n_vec:].astype(BF16), to_hidden)
+        qv_rows = by_hidden[:2]
+
+        stream_zero, input_one = embed(
             present, pixels, band, table, patch_bias_rows, gains[0], biases[0], patches
         )
-        came, came_t, input_one, turned_one = sync((came, came_t, input_one, turned_one))
+        came, came_t, input_one, qkv_two.held = sync((came, came_t, input_one, qkv_two.held))
         done(came, qkv_one)
         qkv_one.drain()
         c_one = over_t(c_one, came_t[0], t_rest)
@@ -961,7 +977,9 @@
         first = project(input_one, *one, qv_rows[:, :heads_width])
         attended, logs = [None] * 3, [None] * 3
         attended[0], logs[0] = attend(*first, seg, 0, 0, each // 2)
-        came, attended[0] = sync((came, attended[0]))
+        came, attended[0], feed_high = sync((came, attended[0], feed_high))
+        feed_high = lax.all_gather(feed_high, ("fsdp", "tensor"), axis=0, tiled=False)
+        feed_high = feed_high.reshape(pairs, 2, tensor, 2, wide, half_unit)
         done(came, qkv_two)
         qkv_two.drain()
         two, came = both_cores(qkv_two), go(feed_one)
@@ -976,22 +994,13 @@
         feed_one.drain()
         feed_one = both_cores(feed_one)
         outward = tuple(two[0] + two[1])
-        stream_one, input_two, turned_two = merge(attended, stream_zero, biases[1], gains[1], biases[2], outward)
-        feed_one, input_two = sync((feed_one, input_two))
-
-        rows_two = (input_two, turned_two, top, turned_top)
-        weights = tuple(a for pair in zip(*feed_one) for a in pair)
-        y_low, d_low, *grads_low, units_low = feed(core_at, *rows_two, weights, unit_bias[:, 0], 0)
-        y_high, d_high, *grads_high, units_high = feed(
-            core_at, *rows_two, (feed_high,), unit_bias[:, 1], 1, filled=grads_low, after=(y_low,)
-        )
-        unit_grads = [units_low, units_high]
-
-        heads = model // HEAD_DIM
-        head_rows = (jnp.arange(heads)[:, None] == jnp.arange(model)[None, :] // HEAD_DIM).astype(BF16)
-        expand_sum = Sum(grads_high[0], grads_high[1], down)
-        contract_sum = Sum(grads_high[2], grads_high[3], up)
-
+        stream_one, input_two, log_rows = merge(
+            attended, logs, stream_zero, biases[1], gains[1], biases[2], outward
+        )
+        feed_one, input_two, by_hidden = sync((feed_one, input_two, by_hidden))
+        unit_bias = by_hidden[2:].reshape(-1, tensor, fsdp, thin).transpose(1, 2, 0, 3).reshape(tensor, 2, 1, half_unit)
+
+        rows_two = (input_two, top)
         def meet(sums, *arrays):
             waited = sync(([t.came for t in sums],) + arrays)
             for t, came in zip(sums, waited[0]):
@@ -1006,29 +1015,56 @@
                 while t.todo:
                     t.step()
 
-        grad_stream_one, turned_branch, grad_attended, delta, sums_two = merge_back(
-            attended, d_low, d_high, top, stream_one, gains[1], outward, head_rows
-        )
-        grad_attended = meet((expand_sum, contract_sum), grad_attended)
-        log_rows = sum(logs)[:, :heads].T
+        weights = tuple(a for pair in zip(*feed_one) for a in pair)
+        y_low, d_low, *grads_low, units_low = feed(core_at, *rows_two, weights, unit_bias[:, 0], 0, tensor)
+        low = [Sum(grads_low[0], grads_low[1], down), Sum(grads_low[2], grads_low[3], up)]
+        share = max(1, tensor // 4)
+        y_mid, d_mid, *grads_mid, units_mid = feed(
+            core_at, *rows_two, (feed_high,), unit_bias[:, 1], 0, share, after=(y_low,)
+        )
+        y_mid = meet(low, y_mid)
+        y_high, d_high, *grads_high, units_high = feed(
+            core_at,
+            *rows_two,
+            (feed_high,),
+            unit_bias[:, 1],
+            share,
+            tensor - share,
+            filled=grads_mid + [units_mid],
+            after=[y_mid] + advance(*low),
+        )
+        y_high, *grads_high = meet(low, y_high, *grads_high)
+        high = [Sum(grads_high[0], grads_high[1], down), Sum(grads_high[2], grads_high[3], up)]
+        unit_grads = [units_low, units_high]
+        outs = [y_low, y_mid, y_high]
+
+        heads = model // HEAD_DIM
+        head_rows = (jnp.arange(heads)[:, None] == jnp.arange(model)[None, :] // HEAD_DIM).astype(BF16)
+        grad_stream_one, grad_branch, grad_attended, delta, sums_two = merge_back(
+            attended, [d_low, d_mid, d_high], top, stream_one, gains[1], outward, head_rows, after=advance(*low)
+        )
+        grad_attended = meet(low + high, grad_attended)
         back = lambda i, after: attend_back(
             *(first, last)[i], grad_attended, seg, log_rows, delta, i * each, each, after=after
         )
 
         def grads_of(part, which, after):
             return attention_grads(
-                turned_one, turned_branch, *([p] for p in part[:3]), attended[2 * which : 2 + which], pairs, model // tensor, after=after
+                input_one, grad_branch, *([p] for p in part[:3]), attended[2 * which : 2 + which], pairs, model // tensor, after=after
             )
 
-        first_part = back(0, advance(expand_sum, contract_sum))
-        left = meet((expand_sum, contract_sum), grads_of(first_part, 0, ()))
-        waits = advance(expand_sum, contract_sum)
+        first_part = back(0, advance(*high))
+        drain(*low)
+        low_blocks = jnp.stack([t.total() for t in low], axis=1)
+        feed_grads_low = over_tensor(low_blocks)
+        left = meet(high, grads_of(first_part, 0, (low_blocks,)))
+        waits = advance(*high)
         left_qk, left_vm = Sum(left[0], left[1], down), Sum(left[2], left[3], up)
         second_part = back(1, waits)
-        second_part = meet((expand_sum, contract_sum, left_qk, left_vm), second_part)
-        drain(expand_sum, contract_sum)
-        feed_blocks = jnp.stack([expand_sum.total(), contract_sum.total()], axis=1)
-        feed_grads = over_tensor(feed_blocks)
+        second_part = meet(high + [left_qk, left_vm], second_part)
+        drain(*high)
+        feed_blocks = jnp.stack([t.total() for t in high], axis=1)
+        feed_grads_high = over_tensor(feed_blocks)
         right = grads_of(second_part, 1, advance(left_qk, left_vm) + [feed_blocks])
         right = meet((left_qk, left_vm), right)
         waits = advance(left_qk, left_vm)
@@ -1036,19 +1072,16 @@
         parts = (first_part, second_part)
         grad_query, grad_key, grad_value = ([p[i] for p in parts] for i in range(3))
         grad_qv = jnp.concatenate([p[3] for p in parts], axis=1)
-        grad_embed, turned_embed, sums_one = project_back(
+        grad_embed, sums_one = project_back(
             grad_query, grad_key, grad_value, grad_stream_one, stream_zero, band, gains[0], tuple(one[0] + two[0] + one[1] + two[1]), after=waits
         )
-        grad_embed, turned_embed = meet((left_qk, left_vm, right_qk, right_vm), grad_embed, turned_embed)
+        grad_embed = meet((left_qk, left_vm, right_qk, right_vm), grad_embed)
 
         waits = advance(right_qk, right_vm)
         shape = (pairs, tensor, thin, columns)
-        lo = patch_grads(present, turned_embed, pixels, band, 0, after=waits)
-        hi = patch_grads(present, turned_embed, pixels, band, GROUPS // 2, after=lo[:1])
-        lo, hi = meet((right_qk, right_vm), lo, hi)
-        lo = Sum(*(a.reshape(shape) for a in lo), up)
-        hi = Sum(*(a.reshape(shape) for a in hi), down)
-        waits = advance(right_qk, right_vm)
+        patch_kept = meet((right_qk, right_vm), patch_grads(present, grad_embed, pixels, band, after=waits))
+        lo = Sum(*(a.reshape(shape) for a in patch_kept[:2]), up)
+        hi = Sum(*(a.reshape(shape) for a in patch_kept[2:]), down)
 
         vector_grads = from_split(
             jnp.concatenate(
@@ -1066,27 +1099,32 @@
             axis=2,
         )
         small_grads = jnp.concatenate([vector_grads, hidden_grads], axis=2).reshape(fsdp * tensor, -1)
-        halvings = [("fsdp", bit) for bit in range(len(f_bits) + 1)[::-1]] + [("tensor", bit) for bit in t_bits[::-1]]
+        small_grads = small_grads.reshape((2,) * (len(f_bits) + 1 + len(t_bits)) + (-1,))
 
         def small_halves(array, axis, bit):
-            half = array.shape[0] // 2
+            dim = (len(f_bits) - bit) if axis == "fsdp" else len(f_bits) + len(t_bits) - bit
             mine = (index[axis] >> bit) & 1
-            return (
-                lax.dynamic_slice_in_dim(array, mine * half, half),
-                swap(lax.dynamic_slice_in_dim(array, (1 - mine) * half, half), axis, bit),
-            )
-
-        small_kept, small_came = small_halves(small_grads, *halvings[0])
-        block_output = output_rows(
-            core_at, stream_one, y_low, y_high, biases[3], wide, after=waits + [small_kept]
-        )
+            take = lambda at: lax.dynamic_slice_in_dim(array, at, 1, axis=dim)
+            return take(mine), swap(take(1 - mine), axis, bit)
+
+        def small_steps(kept, came, axis, bits):
+            for bit in bits:
+                kept, came = small_halves(kept + came, axis, bit)
+            return kept, came
+
+        small_kept, small_came = small_halves(small_grads, "fsdp", 0)
+        waits = advance(right_qk, right_vm)
+        small_came = meet((lo, hi), small_came)
+        waits += advance(lo, hi)
+        small_kept, small_came = small_steps(small_kept, small_came, "tensor", t_bits)
+        block_output = output_rows(core_at, [stream_one] + outs, biases[3], wide, after=waits)
         if not aligned:
             block_output = from_split(block_output)
-        small_came, block_output = meet((right_qk, right_vm, lo, hi), small_came, block_output)
-        waits = advance(lo, hi)
-        drain(left_qk, left_vm, right_qk, right_vm)
-        small_kept, small_came = small_halves(small_kept + small_came, *halvings[1])
-        pixel_grad = pixel_grads(present, grad_embed, band, patches, pix, after=waits + [small_kept])
+        pixel_grad = pixel_grads(present, grad_embed, band, patches, pix, after=[block_output])
+        small_came, pixel_grad = meet((lo, hi, left_qk, left_vm, right_qk, right_vm), small_came, pixel_grad)
+        advance(lo, hi)
+        small_kept, small_came = small_steps(small_kept, small_came, "fsdp", f_bits)
+        drain(lo, hi, left_qk, left_vm, right_qk, right_vm)
         grad_attention = over_tensor(
             jnp.concatenate(
                 [
@@ -1096,18 +1134,12 @@
                 axis=0,
             )
         )
-        small_came, pixel_grad = meet((lo, hi), small_came, pixel_grad)
-        advance(lo, hi)
-        drain(lo, hi)
-        small_kept, small_came = small_halves(small_kept + small_came, *halvings[2])
-        expand_out, contract_out = finish_feed(feed_grads)
-        small_came, expand_out, contract_out = meet((lo, hi), small_came, expand_out, contract_out)
+        small_came = meet((lo, hi), small_came)
         blocks = jnp.concatenate([lo.total(), hi.total()], axis=2)
+        expand_out, contract_out = finish_feed(feed_grads_low, feed_grads_high, after=[blocks])
         own = lambda d: lax.dynamic_index_in_dim(blocks, (index["tensor"] + d) % tensor, 0, keepdims=False)
         came = shifts(own)
-        for axis, bit in halvings[3:]:
-            small_kept, small_came = small_halves(small_kept + small_came, axis, bit)
-        small_grads = small_kept + small_came
+        small_grads = (small_kept + small_came).reshape(1, -1)
         grad_patch = sum([c.astype(F32) for c in came], own(0).astype(F32)).T.reshape(GROUPS, pix, thin)
         attention_out, merge_grad = finish_attention(grad_attention)
         small_grads = small_grads[0]

time: 568 us -> 546 us (0.961)
  waiting for transfers between devices: 82.5 us -> 70 us
  other arithmetic: 61 us -> 48.6 us
    ppermute x59 -> x65, waiting for transfers between devices: 49.9 us -> 37.7 us  [swap(): return lax.ppermute(array, axis, [(i, i ^ 1 << bit) for i in range(size)])]
    convert_element_type x16 -> x20, other arithmetic: 29.3 us -> 21.8 us  [half_sum(): return (take(keep).astype(F32) + take(came).astype(F32)).astype(keep.dtype)]
    unnamed x150 -> x200, local copies, waits for them, and re-layouts: 6.9 us -> 13.6 us
    select_n x22, other arithmetic: 14.7 us -> 8.91 us  [wider(): jnp.where(mine, jnp.concatenate([came, array], axis=dim), jnp.concatenate...]
    ppermute x59 -> x65, starting transfers between devices: 55.2 us -> 57 us  [swap(): return lax.ppermute(array, axis, [(i, i ^ 1 << bit) for i in range(size)])]
    pallas_call x23 -> x24, Pallas kernels: 298 us -> 298 us  [call(): pl.pallas_call(with_waits, grid_spec=pltpu.PrefetchScalarGridSpec(num_sca...]
  transfers between devices with their start and end apart: 68 -> 75, of which waited for: 22 -> 25; matrix products, arithmetic and copies ran while one was open for 13% -> 12% of each run, Pallas kernels for 46% -> 55%
where the time goes in v3:
time: 546 us; the launch traced here: 541 us
  Pallas kernels  298 us (55%)
  waiting for transfers between devices  70 us (13%)
  starting transfers between devices  65.2 us (12%)
  other arithmetic  48.6 us (9%)
  local copies, waits for them, and re-layouts  43.1 us (8%)
  between operations  15.7 us (3%)
    pallas_call x24, Pallas kernels, call(): pl.pallas_call(with_waits, grid_spec=pltpu.PrefetchScalarGridSpec(num_sca...  298 us
    ppermute x65, starting transfers between devices, swap(): return lax.ppermute(array, axis, [(i, i ^ 1 << bit) for i in range(size)])  57 us
    ppermute x65, waiting for transfers between devices, swap(): return lax.ppermute(array, axis, [(i, i ^ 1 << bit) for i in range(size)])  37.7 us
    ppermute x6, waiting for transfers between devices, shifts(): lax.ppermute(make(d), 'tensor', [(i, (i + d) % count) for i in range(coun...  32.2 us
    convert_element_type x20, other arithmetic, half_sum(): return (take(keep).astype(F32) + take(came).astype(F32)).astype(keep.dtype)  21.8 us
    cos x1, local copies, waits for them, and re-layouts, body(): f(angles[:, i * quarter:(i + 1) * quarter])  14.2 us
    unnamed x200, local copies, waits for them, and re-layouts  13.6 us
  transfers between devices with their start and end apart: 75, of which 25 were waited for; matrix products, arithmetic and copies ran while one was open for 12% of the time, Pallas kernels for 55%

profile of v3, /device:TPU:8, one launch (start us, length us, event | category | flops | bytes accessed | tf_op | source)
XLA Modules:
  0.0 541.4 jit_solution(11729294047689386873)
XLA Ops:
  28.1 3.2 collective-permute-done.1
  39.2 4.3 shard_map.240.refs_2_.refs_6_
  52.1 14.2 %slice_cosine_fusion = (f32[1024,256]{1,0:T(8,128)}, f32[1024,256]{1,0:T(8,128)}, f32[1024,256]{1,0:T(8,128)}, f32[1024,256]{1,0:T(8,128)}) fusion(f32[1024,1024]{1,0:T(8,128)S(1)} %broadcast_multiply_fusion), kind=kLoop, calls=%fused_computation.32 | loop fusion | bytes 8388608 | tf_op jit(solution)/shard_map/cos | solution.py:929
  66.3 4.4 collective-permute-done.8
  72.0 3.5 collective-permute-start.15
  79.5 4.4 collective-permute-done.13
  92.5 3.4 collective-permute-start.18
  95.9 12.7 %shard_map.241 = (f32[1024,1024]{1,0:T(8,128)}, bf16[1024,1024]{1,0:T(8,128)(2,1)}) custom-call(s32[16]{0:T(128)} %reshape.1282.refs_0_, bf16[1024,768]{1,0:T(8,128)(2,1)} %refs_2_.1, f32[1024,8]{1,0:T(8,128)} %shard_map.239.refs_2_.refs_3_.refs_4_.refs_8_, f32[1024,256]{1,0:T(8,128)} %get-tuple-element.243.refs_3_, f32[1024,256]{1,0:T(8,128)} %get-tuple-element.244.refs_4_, ...), custom_call_target="tpu_custom_call" | custom-call | flops 3221225472 | bytes 18669568 | tf_op jit(solution)/shard_map/pallas_call | solution.py:80
  113.6 7.0 %collective-permute-done.21 = bf16[1,1,1,5,128,256]{5,4,3,2,1,0:T(8,128)(2,1)S(1)} collective-permute-done((bf16[1,1,1,5,128,256]{5,4,3,2,1,0:T(8,128)(2,1)S(1)}, bf16[1,1,1,5,128,256]{5,4,3,2,1,0:T(8,128)(2,1)S(1)}, u32[]{:S(2)}, u32[]{:S(2)}) %collective-permute-start.21) | collective-permute-done | bytes 327712 | tf_op jit(solution)/shard_map/ppermute | solution.py:742
  123.7 6.9 %shard_map.242 = (bf16[1024,512]{1,0:T(8,128)(2,1)}, bf16[1024,512]{1,0:T(8,128)(2,1)}, bf16[1024,512]{1,0:T(8,128)(2,1)}) custom-call(bf16[1024,1024]{1,0:T(8,128)(2,1)} %get-tuple-element.283.refs_0_, f32[2,512]{1,0:T(2,128)} %get-tuple-element.520.refs_1_, bf16[4,1,3,128,256]{4,3,2,1,0:T(8,128)(2,1)} %bitcast.178, bf16[4,1,3,128,256]{4,3,2,1,0:T(8,128)(2,1)} %bitcast.175, ...), custom_call_target="tpu_custom_call" | custom-call | flops 3221225472 | bytes 8392704 | tf_op jit(solution)/shard_map/pallas_call | solution.py:80
  130.6 11.6 %shard_map.243 = (bf16[1024,256]{1,0:T(8,128)(2,1)}, f32[1024,128]{1,0:T(8,128)}) custom-call(bf16[1024,512]{1,0:T(8,128)(2,1)} %get-tuple-element.267.refs_0_, bf16[1024,512]{1,0:T(8,128)(2,1)} %get-tuple-element.268.refs_1_, bf16[1024,512]{1,0:T(8,128)(2,1)} %get-tuple-element.269.refs_2_, f32[1024,8]{1,0:T(8,128)} %shard_map.239.refs_2_.refs_3_.refs_4_.refs_8_, ...), custom_call_target="tpu_custom_call" | custom-call | flops 4294967296 | bytes 4259840 | tf_op jit(solution)/shard_map/pallas_call | solution.py:80
  146.3 11.1 %shard_map.244 = (bf16[1024,256]{1,0:T(8,128)(2,1)}, f32[1024,128]{1,0:T(8,128)}) custom-call(bf16[1024,512]{1,0:T(8,128)(2,1)} %get-tuple-element.267.refs_0_, bf16[1024,512]{1,0:T(8,128)(2,1)} %get-tuple-element.268.refs_1_, bf16[1024,512]{1,0:T(8,128)(2,1)} %get-tuple-element.269.refs_2_, f32[1024,8]{1,0:T(8,128)} %shard_map.239.refs_2_.refs_3_.refs_4_.refs_8_, ...), custom_call_target="tpu_custom_call" | custom-call | flops 4294967296 | bytes 4259840 | tf_op jit(solution)/shard_map/pallas_call | solution.py:80
  157.4 3.4 collective-permute-done.27
  164.2 7.6 %shard_map.245 = (bf16[1024,512]{1,0:T(8,128)(2,1)}, bf16[1024,512]{1,0:T(8,128)(2,1)}, bf16[1024,512]{1,0:T(8,128)(2,1)}) custom-call(bf16[1024,1024]{1,0:T(8,128)(2,1)} %get-tuple-element.283.refs_0_, f32[2,512]{1,0:T(2,128)} %get-tuple-element.519.refs_1_, bf16[4,1,5,128,256]{4,3,2,1,0:T(8,128)(2,1)} %bitcast.161, bf16[4,1,5,128,256]{4,3,2,1,0:T(8,128)(2,1)} %bitcast.156, ...), custom_call_target="tpu_custom_call" | custom-call | flops 3221225472 | bytes 10489856 | tf_op jit(solution)/shard_map/pallas_call | solution.py:80
  171.7 19.6 %shard_map.246 = (bf16[1024,512]{1,0:T(8,128)(2,1)}, f32[1024,128]{1,0:T(8,128)}) custom-call(bf16[1024,512]{1,0:T(8,128)(2,1)} %get-tuple-element.288.refs_0_, bf16[1024,512]{1,0:T(8,128)(2,1)} %get-tuple-element.289.refs_1_, bf16[1024,512]{1,0:T(8,128)(2,1)} %get-tuple-element.290.refs_2_, f32[1024,8]{1,0:T(8,128)} %shard_map.239.refs_2_.refs_3_.refs_4_.refs_8_, ...), custom_call_target="tpu_custom_call" | custom-call | flops 8589934592 | bytes 4784128 | tf_op jit(solution)/shard_map/pallas_call | solution.py:80
  195.4 10.2 %shard_map.247 = (f32[1024,1024]{1,0:T(8,128)}, bf16[1024,1024]{1,0:T(8,128)(2,1)}, f32[128,1024]{1,0:T(8,128)}) custom-call(bf16[1024,256]{1,0:T(8,128)(2,1)} %get-tuple-element.274.refs_5_.refs_0_, bf16[1024,256]{1,0:T(8,128)(2,1)} %get-tuple-element.280.refs_1_.refs_6_, bf16[1024,512]{1,0:T(8,128)(2,1)} %get-tuple-element.292.refs_2_.refs_5_, ...), custom_call_target="tpu_custom_call" | custom-call | flops 2147483648 | bytes 19935232 | tf_op jit(solution)/shard_map/pallas_call | solution.py:80
  207.9 36.5 %shard_map.248 = (bf16[1024,1024]{1,0:T(8,128)(2,1)}, bf16[1024,1024]{1,0:T(8,128)(2,1)}, bf16[4,4,128,512]{3,2,1,0:T(8,128)(2,1)}, bf16[4,4,128,512]{3,2,1,0:T(...) custom-call(s32[1]{0:T(128)} %bitcast.refs_0_, ...), custom_call_target="tpu_custom_call" | custom-call | flops 25769803776 | bytes 25182208 | tf_op jit(solution)/shard_map/pallas_call | solution.py:80
  244.9 11.7 %shard_map.249 = (bf16[1024,1024]{1,0:T(8,128)(2,1)}, bf16[1024,1024]{1,0:T(8,128)(2,1)}, bf16[4,4,128,512]{3,2,1,0:T(8,128)(2,1)}, bf16[4,4,128,512]{3,2,1,0:T(...) custom-call(s32[1]{0:T(128)} %bitcast.refs_0_, ...), custom_call_target="tpu_custom_call" | custom-call | flops 6442450944 | bytes 50348032 | tf_op jit(solution)/shard_map/pallas_call | solution.py:80
  262.9 29.5 %shard_map.250 = (bf16[1024,1024]{1,0:T(8,128)(2,1)}, bf16[1024,1024]{1,0:T(8,128)(2,1)}, bf16[4,4,128,512]{3,2,1,0:T(8,128)(2,1)}, bf16[4,4,128,512]{3,2,1,0:T(...) custom-call(s32[1]{0:T(128)} %bitcast.refs_0_, ...), custom_call_target="tpu_custom_call", output_to_operand_aliasing={{2}: (11, {}), {3}: (12, {}), {4}: (13, {}), {5}: (14, {}),... | custom-call | flops 19327352832 | bytes 50348032 | tf_op jit(solution)/shard_map/pallas_call | solution.py:80
  299.3 13.3 %shard_map.251 = (f32[1024,1024]{1,0:T(8,128)}, bf16[1024,1024]{1,0:T(8,128)(2,1)}, bf16[1024,1024]{1,0:T(8,128)(2,1)}, f32[16,1024]{1,0:T(8,128)}, f32[8,1024]{1,0:T(8,128)}) custom-call(bf16[1024,256]{1,0:T(8,128)(2,1)} %get-tuple-element.274.refs_5_.refs_0_, bf16[1024,256]{1,0:T(8,128)(2,1)} %get-tuple-element.280.refs_1_.refs_6_, ...), custom_call_target="tpu_custom_call" | custom-call | flops 2147483648 | bytes 28446720 | tf_op jit(solution)/shard_map/pallas_call | solution.py:80
  314.1 3.3 add_convert_fusion
  321.2 26.8 %shard_map.252 = (bf16[1024,512]{1,0:T(8,128)(2,1)}, bf16[1024,512]{1,0:T(8,128)(2,1)}, bf16[1024,512]{1,0:T(8,128)(2,1)}, f32[2,512]{1,0:T(2,128)}) custom-call(bf16[1024,512]{1,0:T(8,128)(2,1)} %get-tuple-element.267.refs_0_, bf16[1024,512]{1,0:T(8,128)(2,1)} %get-tuple-element.268.refs_1_, bf16[1024,512]{1,0:T(8,128)(2,1)} %get-tuple-element.269.refs_2_, ...), custom_call_target="tpu_custom_call" | custom-call | flops 21474836480 | bytes 9048064 | tf_op jit(solution)/shard_map/pallas_call | solution.py:80
  350.8 8.9 %shard_map.253 = (bf16[4,2,2,128,256]{4,3,2,1,0:T(8,128)(2,1)}, bf16[4,2,2,128,256]{4,3,2,1,0:T(8,128)(2,1)}, bf16[4,2,2,128,256]{4,3,2,1,0:T(8,128)(2,1)}, bf16[4,2,2,128,256]{4,3,2,1,0:T(8,128)(2,1)}) custom-call(bf16[1024,1024]{1,0:T(8,128)(2,1)} %get-tuple-element.283.refs_0_, bf16[1024,1024]{1,0:T(8,128)(2,1)} %get-tuple-element.341.refs_1_, ...), custom_call_target="tpu_custom_call" | custom-call | flops 4294967296 | bytes 12582912 | tf_op jit(solution)/shard_map/pallas_call | solution.py:80
  363.7 26.7 %shard_map.254 = (bf16[1024,512]{1,0:T(8,128)(2,1)}, bf16[1024,512]{1,0:T(8,128)(2,1)}, bf16[1024,512]{1,0:T(8,128)(2,1)}, f32[2,512]{1,0:T(2,128)}) custom-call(bf16[1024,512]{1,0:T(8,128)(2,1)} %get-tuple-element.288.refs_0_, bf16[1024,512]{1,0:T(8,128)(2,1)} %get-tuple-element.289.refs_1_, bf16[1024,512]{1,0:T(8,128)(2,1)} %get-tuple-element.290.refs_2_, ...), custom_call_target="tpu_custom_call" | custom-call | flops 21474836480 | bytes 9048064 | tf_op jit(solution)/shard_map/pallas_call | solution.py:80
  396.1 8.9 %shard_map.255 = (bf16[4,2,2,128,256]{4,3,2,1,0:T(8,128)(2,1)}, bf16[4,2,2,128,256]{4,3,2,1,0:T(8,128)(2,1)}, bf16[4,2,2,128,256]{4,3,2,1,0:T(8,128)(2,1)}, bf16[4,2,2,128,256]{4,3,2,1,0:T(8,128)(2,1)}) custom-call(bf16[1024,1024]{1,0:T(8,128)(2,1)} %get-tuple-element.283.refs_0_, bf16[1024,1024]{1,0:T(8,128)(2,1)} %get-tuple-element.341.refs_1_, ...), custom_call_target="tpu_custom_call" | custom-call | flops 4294967296 | bytes 12582912 | tf_op jit(solution)/shard_map/pallas_call | solution.py:80
  410.2 17.3 %shard_map.256 = (bf16[1024,1024]{1,0:T(8,128)(2,1)}, f32[8,1024]{1,0:T(8,128)}) custom-call(bf16[1024,512]{1,0:T(8,128)(2,1)} %get-tuple-element.345.refs_2_.refs_0_, bf16[1024,512]{1,0:T(8,128)(2,1)} %get-tuple-element.366.refs_2_.refs_1_, bf16[1024,512]{1,0:T(8,128)(2,1)} %get-tuple-element.346.refs_3_.refs_2_, ...), custom_call_target="tpu_custom_call" | custom-call | flops 6442450944 | bytes 25235456 | tf_op jit(solution)/shard_map/pallas_call | solution.py:80
  433.2 11.1 %shard_map.257 = (bf16[512,1536]{1,0:T(8,128)(2,1)}, bf16[512,1536]{1,0:T(8,128)(2,1)}, bf16[512,1536]{1,0:T(8,128)(2,1)}, bf16[512,1536]{1,0:T(8,128)(2,1)}) custom-call(s32[16]{0:T(128)} %reshape.1282.refs_0_, bf16[1024,1024]{1,0:T(8,128)(2,1)} %get-tuple-element.385.refs_1_, bf16[1024,768]{1,0:T(8,128)(2,1)} %refs_2_.1, ...), custom_call_target="tpu_custom_call" | custom-call | flops 3221225472 | bytes 9994240 | tf_op jit(solution)/shard_map/pallas_call | solution.py:80
  459.6 7.1 %shard_map.258.refs_7_ = f32[1024,1024]{1,0:T(8,128)} custom-call(s32[1]{0:T(128)} %bitcast.refs_0_, f32[1024,1024]{1,0:T(8,128)} %get-tuple-element.297.refs_7_.refs_1_, bf16[1024,1024]{1,0:T(8,128)(2,1)} %get-tuple-element.308.refs_8_.refs_2_, bf16[1024,1024]{1,0:T(8,128)(2,1)} %get-tuple-element.313.refs_8_.refs_3_, ...), custom_call_target="tpu_custom_call" | custom-call | bytes 14684160 | tf_op jit(solution)/shard_map/pallas_call | solution.py:80
  469.7 9.2 %shard_map.259 = f32[1024,768]{1,0:T(8,128)} custom-call(s32[16]{0:T(128)} %reshape.1282.refs_0_, bf16[1024,1024]{1,0:T(8,128)(2,1)} %get-tuple-element.385.refs_1_, f32[1024,8]{1,0:T(8,128)} %shard_map.239.refs_2_.refs_3_.refs_4_.refs_8_, bf16[4,128,1536]{2,1,0:T(8,128)(2,1)} %bitcast.171, bf16[4,128,1536]{2,1,0:T(8,128)(2,1)} %collective-permute-done.11.refs_11_.refs_4_, ...), custom_call_target="tpu_custom_call" | custom-call | flops 3221225472 | bytes 11829248 | tf_op jit(solution)/shard_map/pallas_call | solution.py:80
  490.6 5.0 collective-permute-done.67
  507.8 12.2 %collective-permute-done.68 = bf16[32,3072]{1,0:T(8,128)(2,1)S(1)} collective-permute-done((bf16[32,3072]{1,0:T(8,128)(2,1)S(1)}, bf16[32,3072]{1,0:T(8,128)(2,1)S(1)}, u32[]{:S(2)}, u32[]{:S(2)}) %collective-permute-start.68) | collective-permute-done | bytes 196640 | tf_op jit(solution)/shard_map/ppermute | solution.py:781
  520.0 10.1 %collective-permute-done.69 = bf16[32,3072]{1,0:T(8,128)(2,1)S(1)} collective-permute-done((bf16[32,3072]{1,0:T(8,128)(2,1)S(1)}, bf16[32,3072]{1,0:T(8,128)(2,1)S(1)}, u32[]{:S(2)}, u32[]{:S(2)}) %collective-permute-start.69) | collective-permute-done | bytes 196640 | tf_op jit(solution)/shard_map/ppermute | solution.py:781
  (485 shorter events, 160.8 us)
Async XLA Ops:
  7.2 237.7 %all-gather.3.cloned.1.call-start = ((), (), s32[]{:S(2)}) async-start(), calls=%async_computation.6 | async-start | bytes 8650752 | tf_op jit(solution)/shard_map/all_gather | solution.py:981
  46.3 24.4 %collective-permute-start.7 = (bf16[2,1,128,1664]{3,2,1,0:T(8,128)(2,1)S(1)}, bf16[2,1,128,1664]{3,2,1,0:T(8,128)(2,1)S(1)}, u32[]{:S(2)}, u32[]{:S(2)}) collective-permute-start(bf16[2,1,128,1664]{3,2,1,0:T(8,128)(2,1)S(1)} %maximum_select_fusion.9), channel_id=1, source_target_pairs={{0,8},{4,12},{8,0},{12,4},{16,24},{20,28},{24,16},{28,20},{1,9},{5... | collective-permute-start | bytes 2555912 | tf_op jit(solution)/shard_map/ppermute | solution.py:742
  48.0 22.7 %collective-permute-start.6 = (bf16[1,2,128,1536]{3,2,1,0:T(8,128)(2,1)S(1)}, bf16[1,2,128,1536]{3,2,1,0:T(8,128)(2,1)S(1)}, u32[]{:S(2)}, u32[]{:S(2)}) collective-permute-start(bf16[1,2,128,1536]{3,2,1,0:T(8,128)(2,1)S(1)} %maximum_select_fusion.10), channel_id=1, source_target_pairs={{0,16},{4,20},{8,24},{12,28},{16,0},{20,4},{24,8},{28,12},{1,17},{... | collective-permute-start | bytes 2359304 | tf_op jit(solution)/shard_map/ppermute | solution.py:742
  49.1 21.5 %collective-permute-start.8 = (bf16[2,4,128,256]{3,2,1,0:T(8,128)(2,1)S(1)}, bf16[2,4,128,256]{3,2,1,0:T(8,128)(2,1)S(1)}, u32[]{:S(2)}, u32[]{:S(2)}) collective-permute-start(bf16[2,4,128,256]{3,2,1,0:T(8,128)(2,1)S(1)} %maximum_select_fusion.15), channel_id=1, source_target_pairs={{0,2},{1,3},{2,0},{3,1},{4,6},{5,7},{6,4},{7,5},{8,10},{9,11},{10,... | collective-permute-start | bytes 1572872 | tf_op jit(solution)/shard_map/ppermute | solution.py:742
  87.2 21.4 %collective-permute-start.17 = (bf16[2,1,1,3,128,256]{5,4,3,2,1,0:T(8,128)(2,1)S(1)}, bf16[2,1,1,3,128,256]{5,4,3,2,1,0:T(8,128)(2,1)S(1)}, u32[]{:S(2)}, u32[]{:S(2)}) collective-permute-start(bf16[2,1,1,3,128,256]{5,4,3,2,1,0:T(8,128)(2,1)S(1)} %maximum_select_fusion.19), channel_id=1, source_target_pairs={{0,8},{4,12},{8,0},{12,4},{16,24},{20,28},{24,16},{28,20},{1,9},{5... | collective-permute-start | bytes 1179656 | tf_op jit(solution)/shard_map/ppermute | solution.py:742
  89.7 18.9 %collective-permute-start.16 = (bf16[1,2,1,3,128,256]{5,4,3,2,1,0:T(8,128)(2,1)S(1)}, bf16[1,2,1,3,128,256]{5,4,3,2,1,0:T(8,128)(2,1)S(1)}, u32[]{:S(2)}, u32[]{:S(2)}) collective-permute-start(bf16[1,2,1,3,128,256]{5,4,3,2,1,0:T(8,128)(2,1)S(1)} %maximum_select_fusion.18), channel_id=1, source_target_pairs={{0,16},{4,20},{8,24},{12,28},{16,0},{20,4},{24,8},{28,12},{1,17},{... | collective-permute-start | bytes 1179656 | tf_op jit(solution)/shard_map/ppermute | solution.py:742
  121.0 21.2 %collective-permute-start.24 = (bf16[2,1,1,5,128,256]{5,4,3,2,1,0:T(8,128)(2,1)S(1)}, bf16[2,1,1,5,128,256]{5,4,3,2,1,0:T(8,128)(2,1)S(1)}, u32[]{:S(2)}, u32[]{:S(2)}) collective-permute-start(bf16[2,1,1,5,128,256]{5,4,3,2,1,0:T(8,128)(2,1)S(1)} %maximum_select_fusion.14), channel_id=1, source_target_pairs={{0,8},{4,12},{8,0},{12,4},{16,24},{20,28},{24,16},{28,20},{1,9},{5... | collective-permute-start | bytes 1966088 | tf_op jit(solution)/shard_map/ppermute | solution.py:742
  122.7 19.6 %collective-permute-start.23 = (bf16[1,2,1,5,128,256]{5,4,3,2,1,0:T(8,128)(2,1)S(1)}, bf16[1,2,1,5,128,256]{5,4,3,2,1,0:T(8,128)(2,1)S(1)}, u32[]{:S(2)}, u32[]{:S(2)}) collective-permute-start(bf16[1,2,1,5,128,256]{5,4,3,2,1,0:T(8,128)(2,1)S(1)} %maximum_select_fusion.13), channel_id=1, source_target_pairs={{0,16},{4,20},{8,24},{12,28},{16,0},{20,4},{24,8},{28,12},{1,17},{... | collective-permute-start | bytes 1966088 | tf_op jit(solution)/shard_map/ppermute | solution.py:742
  143.2 362.5 %reduce-scatter.6.cloned.1.call-start = ((), (), s32[]{:S(2)}) async-start(), calls=%async_computation.4 | async-start | bytes 1310720 | tf_op jit(solution)/shard_map/reduce_scatter | solution.py:847
  161.6 32.0 %collective-permute-start.30 = (bf16[2,1,4,128,512]{4,3,2,1,0:T(8,128)(2,1)S(1)}, bf16[2,1,4,128,512]{4,3,2,1,0:T(8,128)(2,1)S(1)}, u32[]{:S(2)}, u32[]{:S(2)}) collective-permute-start(bf16[2,1,4,128,512]{4,3,2,1,0:T(8,128)(2,1)S(1)} %maximum_select_fusion.8), channel_id=1, source_target_pairs={{0,8},{4,12},{8,0},{12,4},{16,24},{20,28},{24,16},{28,20},{1,9},{5... | collective-permute-start | bytes 3145736 | tf_op jit(solution)/shard_map/ppermute | solution.py:742
  163.0 30.6 %collective-permute-start.29 = (bf16[1,2,4,128,512]{4,3,2,1,0:T(8,128)(2,1)S(1)}, bf16[1,2,4,128,512]{4,3,2,1,0:T(8,128)(2,1)S(1)}, u32[]{:S(2)}, u32[]{:S(2)}) collective-permute-start(bf16[1,2,4,128,512]{4,3,2,1,0:T(8,128)(2,1)S(1)} %maximum_select_fusion.7), channel_id=1, source_target_pairs={{0,16},{4,20},{8,24},{12,28},{16,0},{20,4},{24,8},{28,12},{1,17},{... | collective-permute-start | bytes 3145736 | tf_op jit(solution)/shard_map/ppermute | solution.py:742
  259.0 33.4 %collective-permute-start.36 = (bf16[2,1,4,128,512]{4,3,2,1,0:T(8,128)(2,1)S(1)}, bf16[2,1,4,128,512]{4,3,2,1,0:T(8,128)(2,1)S(1)}, u32[]{:S(2)}, u32[]{:S(2)}) collective-permute-start(bf16[2,1,4,128,512]{4,3,2,1,0:T(8,128)(2,1)S(1)} %get-tuple-element.479.refs_10_), channel_id=1, source_target_pairs={{0,8},{4,12},{8,0},{12,4},{16,24},{20,28},{24,16},{28,20},{1,9},{5... | collective-permute-start | bytes 3145736 | tf_op jit(solution)/shard_map/ppermute | solution.py:742
  261.8 30.5 %collective-permute-start.35 = (bf16[1,2,4,128,512]{4,3,2,1,0:T(8,128)(2,1)}, bf16[1,2,4,128,512]{4,3,2,1,0:T(8,128)(2,1)S(1)}, u32[]{:S(2)}, u32[]{:S(2)}) collective-permute-start(bf16[1,2,4,128,512]{4,3,2,1,0:T(8,128)(2,1)} %get-tuple-element.481.refs_9_), channel_id=1, source_target_pairs={{0,16},{4,20},{8,24},{12,28},{16,0},{20,4},{24,8},{28,12},{1,17},{... | collective-permute-start | bytes 3145736 | tf_op jit(solution)/shard_map/ppermute | solution.py:742
  293.7 19.0 %collective-permute-start.39 = (bf16[4,4,128,512]{3,2,1,0:T(8,128)(2,1)}, bf16[4,4,128,512]{3,2,1,0:T(8,128)(2,1)S(1)}, u32[]{:S(2)}, u32[]{:S(2)}) collective-permute-start(bf16[4,4,128,512]{3,2,1,0:T(8,128)(2,1)} %get-tuple-element.332), channel_id=1, source_target_pairs={{0,4},{4,0},{8,12},{12,8},{16,20},{20,16},{24,28},{28,24},{1,5},{5... | collective-permute-start | bytes 6291464 | tf_op jit(solution)/shard_map/ppermute | solution.py:742
  293.7 19.0 %collective-permute-start.40 = (bf16[4,4,128,512]{3,2,1,0:T(8,128)(2,1)}, bf16[4,4,128,512]{3,2,1,0:T(8,128)(2,1)S(1)}, u32[]{:S(2)}, u32[]{:S(2)}) collective-permute-start(bf16[4,4,128,512]{3,2,1,0:T(8,128)(2,1)} %get-tuple-element.333), channel_id=1, source_target_pairs={{0,4},{4,0},{8,12},{12,8},{16,20},{20,16},{24,28},{28,24},{1,5},{5... | collective-permute-start | bytes 6291464 | tf_op jit(solution)/shard_map/ppermute | solution.py:742
  317.4 42.3 %collective-permute-start.42 = (bf16[2,1,4,128,512]{4,3,2,1,0:T(8,128)(2,1)}, bf16[2,1,4,128,512]{4,3,2,1,0:T(8,128)(2,1)S(1)}, u32[]{:S(2)}, u32[]{:S(2)}) collective-permute-start(bf16[2,1,4,128,512]{4,3,2,1,0:T(8,128)(2,1)} %get-tuple-element.475.refs_9_), channel_id=1, source_target_pairs={{0,8},{4,12},{8,0},{12,4},{16,24},{20,28},{24,16},{28,20},{1,9},{5... | collective-permute-start | bytes 3145736 | tf_op jit(solution)/shard_map/ppermute | solution.py:742
  320.2 39.6 %collective-permute-start.41 = (bf16[1,2,4,128,512]{4,3,2,1,0:T(8,128)(2,1)}, bf16[1,2,4,128,512]{4,3,2,1,0:T(8,128)(2,1)}, u32[]{:S(2)}, u32[]{:S(2)}) collective-permute-start(bf16[1,2,4,128,512]{4,3,2,1,0:T(8,128)(2,1)} %get-tuple-element.477.refs_8_), channel_id=1, source_target_pairs={{0,16},{4,20},{8,24},{12,28},{16,0},{20,4},{24,8},{28,12},{1,17},{... | collective-permute-start | bytes 3145736 | tf_op jit(solution)/shard_map/ppermute | solution.py:742
  359.9 30.5 %collective-permute-start.44 = (bf16[1,1,4,128,512]{4,3,2,1,0:T(8,128)(2,1)S(1)}, bf16[1,1,4,128,512]{4,3,2,1,0:T(8,128)(2,1)S(1)}, u32[]{:S(2)}, u32[]{:S(2)}) collective-permute-start(bf16[1,1,4,128,512]{4,3,2,1,0:T(8,128)(2,1)S(1)} %add_convert_fusion.24.refs_9_), channel_id=1, source_target_pairs={{0,16},{4,20},{8,24},{12,28},{16,0},{20,4},{24,8},{28,12},{1,17},{... | collective-permute-start | bytes 1572872 | tf_op jit(solution)/shard_map/ppermute | solution.py:742
  361.0 29.4 %collective-permute-start.45 = (bf16[4,2,2,128,256]{4,3,2,1,0:T(8,128)(2,1)}, bf16[4,2,2,128,256]{4,3,2,1,0:T(8,128)(2,1)S(1)}, u32[]{:S(2)}, u32[]{:S(2)}) collective-permute-start(bf16[4,2,2,128,256]{4,3,2,1,0:T(8,128)(2,1)} %get-tuple-element.357), channel_id=1, source_target_pairs={{0,4},{4,0},{8,12},{12,8},{16,20},{20,16},{24,28},{28,24},{1,5},{5... | collective-permute-start | bytes 3145736 | tf_op jit(solution)/shard_map/ppermute | solution.py:742
  361.0 29.4 %collective-permute-start.46 = (bf16[4,2,2,128,256]{4,3,2,1,0:T(8,128)(2,1)}, bf16[4,2,2,128,256]{4,3,2,1,0:T(8,128)(2,1)S(1)}, u32[]{:S(2)}, u32[]{:S(2)}) collective-permute-start(bf16[4,2,2,128,256]{4,3,2,1,0:T(8,128)(2,1)} %get-tuple-element.358), channel_id=1, source_target_pairs={{0,4},{4,0},{8,12},{12,8},{16,20},{20,16},{24,28},{28,24},{1,5},{5... | collective-permute-start | bytes 3145736 | tf_op jit(solution)/shard_map/ppermute | solution.py:742
  362.7 27.7 %collective-permute-start.43 = (bf16[1,1,4,128,512]{4,3,2,1,0:T(8,128)(2,1)S(1)}, bf16[1,1,4,128,512]{4,3,2,1,0:T(8,128)(2,1)S(1)}, u32[]{:S(2)}, u32[]{:S(2)}) collective-permute-start(bf16[1,1,4,128,512]{4,3,2,1,0:T(8,128)(2,1)S(1)} %add_convert_fusion.25.refs_8_), channel_id=1, source_target_pairs={{0,8},{4,12},{8,0},{12,4},{16,24},{20,28},{24,16},{28,20},{1,9},{5... | collective-permute-start | bytes 1572872 | tf_op jit(solution)/shard_map/ppermute | solution.py:742
  407.3 20.3 %collective-permute-start.51 = (bf16[4,2,2,128,256]{4,3,2,1,0:T(8,128)(2,1)}, bf16[4,2,2,128,256]{4,3,2,1,0:T(8,128)(2,1)S(1)}, u32[]{:S(2)}, u32[]{:S(2)}) collective-permute-start(bf16[4,2,2,128,256]{4,3,2,1,0:T(8,128)(2,1)} %get-tuple-element.378), channel_id=1, source_target_pairs={{0,4},{4,0},{8,12},{12,8},{16,20},{20,16},{24,28},{28,24},{1,5},{5... | collective-permute-start | bytes 3145736 | tf_op jit(solution)/shard_map/ppermute | solution.py:742
  407.3 20.4 %collective-permute-start.52 = (bf16[4,2,2,128,256]{4,3,2,1,0:T(8,128)(2,1)}, bf16[4,2,2,128,256]{4,3,2,1,0:T(8,128)(2,1)}, u32[]{:S(2)}, u32[]{:S(2)}) collective-permute-start(bf16[4,2,2,128,256]{4,3,2,1,0:T(8,128)(2,1)} %get-tuple-element.379), channel_id=1, source_target_pairs={{0,4},{4,0},{8,12},{12,8},{16,20},{20,16},{24,28},{28,24},{1,5},{5... | collective-permute-start | bytes 3145736 | tf_op jit(solution)/shard_map/ppermute | solution.py:742
  407.8 97.9 %reduce-scatter.8.cloned.1.call-start = ((), (), s32[]{:S(2)}) async-start(), calls=%async_computation.5 | async-start | bytes 1310720 | tf_op jit(solution)/shard_map/reduce_scatter | solution.py:847
  408.0 19.6 %collective-permute-start.50 = (bf16[1,1,2,2,128,256]{5,4,3,2,1,0:T(8,128)(2,1)S(1)}, bf16[1,1,2,2,128,256]{5,4,3,2,1,0:T(8,128)(2,1)S(1)}, u32[]{:S(2)}, u32[]{:S(2)}) collective-permute-start(bf16[1,1,2,2,128,256]{5,4,3,2,1,0:T(8,128)(2,1)S(1)} %add_convert_fusion.48.refs_19_), channel_id=1, source_target_pairs={{0,16},{4,20},{8,24},{12,28},{16,0},{20,4},{24,8},{28,12},{1,17},{... | collective-permute-start | bytes 786440 | tf_op jit(solution)/shard_map/ppermute | solution.py:742
  446.9 86.0 %reduce-scatter.4.cloned.1.call-start = ((), (), s32[]{:S(2)}) async-start(), calls=%async_computation.3 | async-start | bytes 1310720 | tf_op jit(solution)/shard_map/reduce_scatter | solution.py:847
  450.3 28.7 %collective-permute-start.61 = (bf16[1,1,2,2,128,256]{5,4,3,2,1,0:T(8,128)(2,1)S(1)}, bf16[1,1,2,2,128,256]{5,4,3,2,1,0:T(8,128)(2,1)S(1)}, u32[]{:S(2)}, u32[]{:S(2)}) collective-permute-start(bf16[1,1,2,2,128,256]{5,4,3,2,1,0:T(8,128)(2,1)S(1)} %add_convert_fusion.46.refs_7_), channel_id=1, source_target_pairs={{0,16},{4,20},{8,24},{12,28},{16,0},{20,4},{24,8},{28,12},{1,17},{... | collective-permute-start | bytes 786440 | tf_op jit(solution)/shard_map/ppermute | solution.py:742
  455.5 26.6 %collective-permute-start.59 = (bf16[1,2,4,32,1536]{4,3,2,1,0:T(8,128)(2,1)S(1)}, bf16[1,2,4,32,1536]{4,3,2,1,0:T(8,128)(2,1)S(1)}, u32[]{:S(2)}, u32[]{:S(2)}) collective-permute-start(bf16[1,2,4,32,1536]{4,3,2,1,0:T(8,128)(2,1)S(1)} %get-tuple-element.487.refs_9_), channel_id=1, source_target_pairs={{0,16},{4,20},{8,24},{12,28},{16,0},{20,4},{24,8},{28,12},{1,17},{... | collective-permute-start | bytes 2359304 | tf_op jit(solution)/shard_map/ppermute | solution.py:742
  457.0 25.1 %collective-permute-start.58 = (bf16[2,1,4,32,1536]{4,3,2,1,0:T(8,128)(2,1)S(1)}, bf16[2,1,4,32,1536]{4,3,2,1,0:T(8,128)(2,1)S(1)}, u32[]{:S(2)}, u32[]{:S(2)}) collective-permute-start(bf16[2,1,4,32,1536]{4,3,2,1,0:T(8,128)(2,1)S(1)} %get-tuple-element.489.refs_8_), channel_id=1, source_target_pairs={{0,8},{4,12},{8,0},{12,4},{16,24},{20,28},{24,16},{28,20},{1,9},{5... | collective-permute-start | bytes 2359304 | tf_op jit(solution)/shard_map/ppermute | solution.py:742
  458.7 23.4 %collective-permute-start.60 = (bf16[1,1,2,2,128,256]{5,4,3,2,1,0:T(8,128)(2,1)S(1)}, bf16[1,1,2,2,128,256]{5,4,3,2,1,0:T(8,128)(2,1)}, u32[]{:S(2)}, u32[]{:S(2)}) collective-permute-start(bf16[1,1,2,2,128,256]{5,4,3,2,1,0:T(8,128)(2,1)S(1)} %add_convert_fusion.47.refs_6_), channel_id=1, source_target_pairs={{0,8},{4,12},{8,0},{12,4},{16,24},{20,28},{24,16},{28,20},{1,9},{5... | collective-permute-start | bytes 786440 | tf_op jit(solution)/shard_map/ppermute | solution.py:742
  503.2 26.9 %collective-permute-start.69 = (bf16[32,3072]{1,0:T(8,128)(2,1)S(1)}, bf16[32,3072]{1,0:T(8,128)(2,1)S(1)}, u32[]{:S(2)}, u32[]{:S(2)}) collective-permute-start(bf16[32,3072]{1,0:T(8,128)(2,1)S(1)} %get-tuple-element.505), channel_id=1, source_target_pairs={{0,2},{1,3},{2,0},{3,1},{4,6},{5,7},{6,4},{7,5},{8,10},{9,11},{10,... | collective-permute-start | bytes 589832 | tf_op jit(solution)/shard_map/ppermute | solution.py:781
  504.2 27.8 %collective-permute-start.70 = (bf16[32,3072]{1,0:T(8,128)(2,1)S(1)}, bf16[32,3072]{1,0:T(8,128)(2,1)S(1)}, u32[]{:S(2)}, u32[]{:S(2)}) collective-permute-start(bf16[32,3072]{1,0:T(8,128)(2,1)S(1)} %get-tuple-element.506), channel_id=1, source_target_pairs={{0,3},{1,0},{2,1},{3,2},{4,7},{5,4},{6,5},{7,6},{8,11},{9,8},{10,9... | collective-permute-start | bytes 589832 | tf_op jit(solution)/shard_map/ppermute | solution.py:781
  (141 other events, 1059.8 us)
Sparse Core Ops, SparseCore 0:
  143.3 86.1 all-gather.2
  407.9 24.5 reduce-scatter.5
  447.0 24.7 reduce-scatter.7
  490.8 39.5 reduce-scatter.3

commit v4 on v3

--- a/solution.py
+++ b/solution.py
@@ -12,6 +12,7 @@
 GROUPS = 4
 LANES = 128
 TILE = 256
+LONG = 512
 EPSILON = 1e-06
 VMEM = 56 * 1024 * 1024
 F32 = jnp.float32
@@ -63,8 +64,8 @@
     return pl.BlockSpec(shape, lambda *_: (0,) * len(shape))
 
 
-def row_tile(shape):
-    return pl.BlockSpec((TILE,) + shape[1:], lambda i, *_: (i,) + (0,) * (len(shape) - 1))
+def row_tile(shape, tile=TILE):
+    return pl.BlockSpec((tile,) + shape[1:], lambda i, *_: (i,) + (0,) * (len(shape) - 1))
 
 
 def call(kernel, grid, in_specs, out_specs, out_shape, args, scratch=(), flops=0, exps=0, scalars=(), after=(), filled=()):
@@ -107,15 +108,15 @@
         out[:, half + at : half + at + wide] = jnp.where(core[0] == 0, odd, even)
 
 
-def turned_tile(shape):
-    return pl.BlockSpec((shape[1], TILE), lambda i, *_: (0, i))
+def turned_tile(shape, tile=TILE):
+    return pl.BlockSpec((shape[1], tile), lambda i, *_: (0, i))
 
 
 def split_columns(core, array, wide):
-    tile = row_tile(array.shape)
+    tile = row_tile(array.shape, LONG)
     return call(
         partial(split_kernel, wide=wide),
-        (array.shape[0] // TILE,),
+        (array.shape[0] // LONG,),
         [tile],
         [tile],
         [shaped(array.shape, array.dtype)],
@@ -161,10 +162,10 @@
 
 
 def output_rows(core, parts, bias, wide, after=()):
-    tile = row_tile(parts[0].shape)
+    tile = row_tile(parts[0].shape, LONG)
     return call(
         partial(output_kernel, wide=wide),
-        (parts[0].shape[0] // TILE,),
+        (parts[0].shape[0] // LONG,),
         [tile] * len(parts) + [whole(bias.shape)],
         [tile],
         [shaped(parts[0].shape, F32)],
@@ -285,9 +286,9 @@
     weights = tuple(own) + tuple(came)
     return call(
         project_kernel,
-        (rows // TILE,),
-        [row_tile(x.shape), whole(bias.shape)] + [whole(w.shape) for w in weights],
-        [row_tile((rows, width))] * 3,
+        (rows // LONG,),
+        [row_tile(x.shape, LONG), whole(bias.shape)] + [whole(w.shape) for w in weights],
+        [row_tile((rows, width), LONG)] * 3,
         [shaped((rows, width), BF16)] * 3,
         (x, bias) + weights,
         flops=6 * rows * model * width,
@@ -434,12 +435,12 @@
     rows, model = stream.shape
     return call(
         partial(merge_kernel, count=len(attended)),
-        (rows // TILE,),
-        [row_tile(a.shape) for a in tuple(attended) + tuple(logs)]
-        + [row_tile(stream.shape)]
+        (rows // LONG,),
+        [row_tile(a.shape, LONG) for a in tuple(attended) + tuple(logs)]
+        + [row_tile(stream.shape, LONG)]
         + [whole((1, model))] * 3
         + [first_two(a) for a in weights],
-        [row_tile((rows, model))] * 2 + [turned_tile((rows, LANES))],
+        [row_tile((rows, model), LONG)] * 2 + [turned_tile((rows, LANES), LONG)],
         [shaped((rows, model), F32), shaped((rows, model), BF16), shaped((LANES, rows), F32)],
         tuple(attended) + tuple(logs) + (stream, bias, gain, shift) + weights,
         flops=2 * rows * model * model,
@@ -553,17 +554,17 @@
 
 def merge_back(attended, grads, top, stream_one, gain, weights, heads, after=()):
     rows, model = stream_one.shape
-    tile = row_tile((rows, model))
+    tile = row_tile((rows, model), LONG)
     return call(
         partial(merge_back_kernel, count=len(attended), parts=len(grads)),
-        (rows // TILE,),
-        [row_tile(a.shape) for a in attended]
+        (rows // LONG,),
+        [row_tile(a.shape, LONG) for a in attended]
         + [tile] * (len(grads) + 2)
         + [whole((1, model))]
         + [first_two(a) for a in weights]
         + [whole(heads.shape)],
         [tile] * 3
-        + [pl.BlockSpec((heads.shape[0], TILE), lambda i: (0, i)), whole((8, model))],
+        + [pl.BlockSpec((heads.shape[0], LONG), lambda i: (0, i)), whole((8, model))],
         [
             shaped((rows, model), F32),
             shaped((rows, model), BF16),
@@ -857,7 +858,6 @@
             parts = jnp.where(core == 0, jnp.stack([mine, other], axis=2), jnp.stack([other, mine], axis=2))
             return parts.reshape(array.shape)
 
-        tie = lambda array, *others: lax.optimization_barrier((array,) + others)[0]
         core_at = core[None].astype(jnp.int32)
         aligned = wide % LANES == 0
 
@@ -945,12 +945,11 @@
         qkv_one = Pair(*qkv[:2])
         qkv_two = Pair(*(jnp.concatenate(two, axis=1) for two in zip(outward, qkv[2:])))
         patch = both_cores(patch)
-        came, came_t = go(qkv_one), start_t(t_rest, e_one)
-        patch, came, came_t, c_one, band = sync((patch, came, came_t, c_one, band))
+        came = go(qkv_one)
+        patch, came, e_one, c_one, band = sync((patch, came, e_one, c_one, band))
         patches = (patch[0][0], patch[1][0], patch[0][1], patch[1][1])
         done(came, qkv_one)
-        e_one = over_t(e_one, came_t[0], t_rest)
-        came, came_t = go(qkv_one), start_t(t_rest, c_one)
+        came, came_t = go(qkv_one), start_t(t_rest, e_one)
         small = [held[0] for held in (patch[0][1:], patch[1][1:])]
         small = jnp.stack([held[:, :, columns : columns + extra] for held in small]).astype(F32)
         vectors = small.reshape(model, extra).T
@@ -966,18 +965,18 @@
         came, came_t, input_one, qkv_two.held = sync((came, came_t, input_one, qkv_two.held))
         done(came, qkv_one)
         qkv_one.drain()
-        c_one = over_t(c_one, came_t[0], t_rest)
-        feed_one = Pair(e_one, c_one)
+        e_one = over_t(e_one, came_t[0], t_rest)
         one, came = both_cores(qkv_one), go(qkv_two)
-        one, came, input_one, feed_one.held = sync((one, came, input_one, feed_one.held))
+        one, came, input_one, c_one = sync((one, came, input_one, c_one))
         done(came, qkv_two)
-        came = go(qkv_two)
+        came, came_t = go(qkv_two), start_t(t_rest, c_one)
         heads_width = model // 2
         each = heads_width // LANES
         first = project(input_one, *one, qv_rows[:, :heads_width])
         attended, logs = [None] * 3, [None] * 3
         attended[0], logs[0] = attend(*first, seg, 0, 0, each // 2)
-        came, attended[0], feed_high = sync((came, attended[0], feed_high))
+        came, came_t, attended[0], feed_high = sync((came, came_t, attended[0], feed_high))
+        feed_one = Pair(e_one, over_t(c_one, came_t[0], t_rest))
         feed_high = lax.all_gather(feed_high, ("fsdp", "tensor"), axis=0, tiled=False)
         feed_high = feed_high.reshape(pairs, 2, tensor, 2, wide, half_unit)
         done(came, qkv_two)

time: 546 us -> 543 us (level)
    select_n x22 -> x21, other arithmetic: 8.91 us -> 11.1 us  [wider(): jnp.where(mine, jnp.concatenate([came, array], axis=dim), jnp.concatenate...]
  transfers between devices with their start and end apart: 75 -> 75, of which waited for: 25 -> 21; matrix products, arithmetic and copies ran while one was open for 12% -> 13% of each run, Pallas kernels for 55% -> 54%
where the time goes in v4:
time: 543 us; the launch traced here: 539 us
  Pallas kernels  294 us (54%)
  waiting for transfers between devices  70.3 us (13%)
  starting transfers between devices  63.7 us (12%)
  other arithmetic  51.3 us (9%)
  local copies, waits for them, and re-layouts  42.9 us (8%)
  between operations  15.8 us (3%)
    pallas_call x24, Pallas kernels, call(): pl.pallas_call(with_waits, grid_spec=pltpu.PrefetchScalarGridSpec(num_sca...  294 us
    ppermute x65, starting transfers between devices, swap(): return lax.ppermute(array, axis, [(i, i ^ 1 << bit) for i in range(size)])  53.7 us
    ppermute x65, waiting for transfers between devices, swap(): return lax.ppermute(array, axis, [(i, i ^ 1 << bit) for i in range(size)])  39.9 us
    ppermute x6, waiting for transfers between devices, shifts(): lax.ppermute(make(d), 'tensor', [(i, (i + d) % count) for i in range(coun...  30.4 us
    convert_element_type x20, other arithmetic, half_sum(): return (take(keep).astype(F32) + take(came).astype(F32)).astype(keep.dtype)  23.1 us
    cos x1, local copies, waits for them, and re-layouts, body(): f(angles[:, i * quarter:(i + 1) * quarter])  14.2 us
    unnamed x200, local copies, waits for them, and re-layouts  13.2 us
    select_n x21, other arithmetic, wider(): jnp.where(mine, jnp.concatenate([came, array], axis=dim), jnp.concatenate...  11.1 us
  transfers between devices with their start and end apart: 75, of which 21 were waited for; matrix products, arithmetic and copies ran while one was open for 13% of the time, Pallas kernels for 54%

profile of v4, /device:TPU:8, one launch (start us, length us, event | category | flops | bytes accessed | tf_op | source)
XLA Modules:
  0.0 538.9 jit_solution(16565851999680617734)
XLA Ops:
  28.1 3.2 collective-permute-done.1
  39.2 3.0 shard_map.240.refs_2_.refs_6_
  52.1 14.2 %slice_cosine_fusion = (f32[1024,256]{1,0:T(8,128)}, f32[1024,256]{1,0:T(8,128)}, f32[1024,256]{1,0:T(8,128)}, f32[1024,256]{1,0:T(8,128)}) fusion(f32[1024,1024]{1,0:T(8,128)S(1)} %broadcast_multiply_fusion), kind=kLoop, calls=%fused_computation.32 | loop fusion | bytes 8388608 | tf_op jit(solution)/shard_map/cos | solution.py:929
  66.3 4.4 collective-permute-done.8
  77.0 4.2 collective-permute-done.13
  88.8 3.4 collective-permute-start.17
  92.2 12.7 %shard_map.241 = (f32[1024,1024]{1,0:T(8,128)}, bf16[1024,1024]{1,0:T(8,128)(2,1)}) custom-call(s32[16]{0:T(128)} %reshape.1496.refs_0_, bf16[1024,768]{1,0:T(8,128)(2,1)} %refs_2_.1, f32[1024,8]{1,0:T(8,128)} %shard_map.239.refs_2_.refs_3_.refs_4_.refs_8_, f32[1024,256]{1,0:T(8,128)} %get-tuple-element.243.refs_3_, f32[1024,256]{1,0:T(8,128)} %get-tuple-element.244.refs_4_, ...), custom_call_target="tpu_custom_call" | custom-call | flops 3221225472 | bytes 18669568 | tf_op jit(solution)/shard_map/pallas_call | solution.py:81
  109.3 6.2 %collective-permute-done.20 = bf16[1,1,1,5,128,256]{5,4,3,2,1,0:T(8,128)(2,1)S(1)} collective-permute-done((bf16[1,1,1,5,128,256]{5,4,3,2,1,0:T(8,128)(2,1)S(1)}, bf16[1,1,1,5,128,256]{5,4,3,2,1,0:T(8,128)(2,1)S(1)}, u32[]{:S(2)}, u32[]{:S(2)}) %collective-permute-start.20) | collective-permute-done | bytes 327712 | tf_op jit(solution)/shard_map/ppermute | solution.py:743
  118.5 6.6 %shard_map.242 = (bf16[1024,512]{1,0:T(8,128)(2,1)}, bf16[1024,512]{1,0:T(8,128)(2,1)}, bf16[1024,512]{1,0:T(8,128)(2,1)}) custom-call(bf16[1024,1024]{1,0:T(8,128)(2,1)} %get-tuple-element.283.refs_0_, f32[2,512]{1,0:T(2,128)} %get-tuple-element.520.refs_1_, bf16[4,1,3,128,256]{4,3,2,1,0:T(8,128)(2,1)} %bitcast.185, bf16[4,1,3,128,256]{4,3,2,1,0:T(8,128)(2,1)} %bitcast.182, ...), custom_call_target="tpu_custom_call" | custom-call | flops 3221225472 | bytes 8392704 | tf_op jit(solution)/shard_map/pallas_call | solution.py:81
  125.1 11.5 %shard_map.243 = (bf16[1024,256]{1,0:T(8,128)(2,1)}, f32[1024,128]{1,0:T(8,128)}) custom-call(bf16[1024,512]{1,0:T(8,128)(2,1)} %get-tuple-element.267.refs_0_, bf16[1024,512]{1,0:T(8,128)(2,1)} %get-tuple-element.268.refs_1_, bf16[1024,512]{1,0:T(8,128)(2,1)} %get-tuple-element.269.refs_2_, f32[1024,8]{1,0:T(8,128)} %shard_map.239.refs_2_.refs_3_.refs_4_.refs_8_, ...), custom_call_target="tpu_custom_call" | custom-call | flops 4294967296 | bytes 4259840 | tf_op jit(solution)/shard_map/pallas_call | solution.py:81
  144.7 11.1 %shard_map.244 = (bf16[1024,256]{1,0:T(8,128)(2,1)}, f32[1024,128]{1,0:T(8,128)}) custom-call(bf16[1024,512]{1,0:T(8,128)(2,1)} %get-tuple-element.267.refs_0_, bf16[1024,512]{1,0:T(8,128)(2,1)} %get-tuple-element.268.refs_1_, bf16[1024,512]{1,0:T(8,128)(2,1)} %get-tuple-element.269.refs_2_, f32[1024,8]{1,0:T(8,128)} %shard_map.239.refs_2_.refs_3_.refs_4_.refs_8_, ...), custom_call_target="tpu_custom_call" | custom-call | flops 4294967296 | bytes 4259840 | tf_op jit(solution)/shard_map/pallas_call | solution.py:81
  162.3 7.3 %shard_map.245 = (bf16[1024,512]{1,0:T(8,128)(2,1)}, bf16[1024,512]{1,0:T(8,128)(2,1)}, bf16[1024,512]{1,0:T(8,128)(2,1)}) custom-call(bf16[1024,1024]{1,0:T(8,128)(2,1)} %get-tuple-element.283.refs_0_, f32[2,512]{1,0:T(2,128)} %get-tuple-element.519.refs_1_, bf16[4,1,5,128,256]{4,3,2,1,0:T(8,128)(2,1)} %bitcast.168, bf16[4,1,5,128,256]{4,3,2,1,0:T(8,128)(2,1)} %bitcast.163, ...), custom_call_target="tpu_custom_call" | custom-call | flops 3221225472 | bytes 10489856 | tf_op jit(solution)/shard_map/pallas_call | solution.py:81
  169.6 19.6 %shard_map.246 = (bf16[1024,512]{1,0:T(8,128)(2,1)}, f32[1024,128]{1,0:T(8,128)}) custom-call(bf16[1024,512]{1,0:T(8,128)(2,1)} %get-tuple-element.288.refs_0_, bf16[1024,512]{1,0:T(8,128)(2,1)} %get-tuple-element.289.refs_1_, bf16[1024,512]{1,0:T(8,128)(2,1)} %get-tuple-element.290.refs_2_, f32[1024,8]{1,0:T(8,128)} %shard_map.239.refs_2_.refs_3_.refs_4_.refs_8_, ...), custom_call_target="tpu_custom_call" | custom-call | flops 8589934592 | bytes 4784128 | tf_op jit(solution)/shard_map/pallas_call | solution.py:81
  193.9 9.5 %shard_map.247 = (f32[1024,1024]{1,0:T(8,128)}, bf16[1024,1024]{1,0:T(8,128)(2,1)}, f32[128,1024]{1,0:T(8,128)}) custom-call(bf16[1024,256]{1,0:T(8,128)(2,1)} %get-tuple-element.274.refs_5_.refs_0_, bf16[1024,256]{1,0:T(8,128)(2,1)} %get-tuple-element.280.refs_1_.refs_6_, bf16[1024,512]{1,0:T(8,128)(2,1)} %get-tuple-element.292.refs_2_.refs_5_, ...), custom_call_target="tpu_custom_call" | custom-call | flops 2147483648 | bytes 19935232 | tf_op jit(solution)/shard_map/pallas_call | solution.py:81
  204.7 36.7 %shard_map.248 = (bf16[1024,1024]{1,0:T(8,128)(2,1)}, bf16[1024,1024]{1,0:T(8,128)(2,1)}, bf16[4,4,128,512]{3,2,1,0:T(8,128)(2,1)}, bf16[4,4,128,512]{3,2,1,0:T(...) custom-call(s32[1]{0:T(128)} %bitcast.refs_0_, ...), custom_call_target="tpu_custom_call" | custom-call | flops 25769803776 | bytes 25182208 | tf_op jit(solution)/shard_map/pallas_call | solution.py:81
  242.0 11.7 %shard_map.249 = (bf16[1024,1024]{1,0:T(8,128)(2,1)}, bf16[1024,1024]{1,0:T(8,128)(2,1)}, bf16[4,4,128,512]{3,2,1,0:T(8,128)(2,1)}, bf16[4,4,128,512]{3,2,1,0:T(...) custom-call(s32[1]{0:T(128)} %bitcast.refs_0_, ...), custom_call_target="tpu_custom_call" | custom-call | flops 6442450944 | bytes 50348032 | tf_op jit(solution)/shard_map/pallas_call | solution.py:81
  258.5 29.3 %shard_map.250 = (bf16[1024,1024]{1,0:T(8,128)(2,1)}, bf16[1024,1024]{1,0:T(8,128)(2,1)}, bf16[4,4,128,512]{3,2,1,0:T(8,128)(2,1)}, bf16[4,4,128,512]{3,2,1,0:T(...) custom-call(s32[1]{0:T(128)} %bitcast.refs_0_, ...), custom_call_target="tpu_custom_call", output_to_operand_aliasing={{2}: (11, {}), {3}: (12, {}), {4}: (13, {}), {5}: (14, {}),... | custom-call | flops 19327352832 | bytes 50348032 | tf_op jit(solution)/shard_map/pallas_call | solution.py:81
  296.2 13.3 %shard_map.251 = (f32[1024,1024]{1,0:T(8,128)}, bf16[1024,1024]{1,0:T(8,128)(2,1)}, bf16[1024,1024]{1,0:T(8,128)(2,1)}, f32[16,1024]{1,0:T(8,128)}, f32[8,1024]{1,0:T(8,128)}) custom-call(bf16[1024,256]{1,0:T(8,128)(2,1)} %get-tuple-element.274.refs_5_.refs_0_, bf16[1024,256]{1,0:T(8,128)(2,1)} %get-tuple-element.280.refs_1_.refs_6_, ...), custom_call_target="tpu_custom_call" | custom-call | flops 2147483648 | bytes 28446720 | tf_op jit(solution)/shard_map/pallas_call | solution.py:81
  311.0 3.4 add_convert_fusion
  316.8 26.8 %shard_map.252 = (bf16[1024,512]{1,0:T(8,128)(2,1)}, bf16[1024,512]{1,0:T(8,128)(2,1)}, bf16[1024,512]{1,0:T(8,128)(2,1)}, f32[2,512]{1,0:T(2,128)}) custom-call(bf16[1024,512]{1,0:T(8,128)(2,1)} %get-tuple-element.267.refs_0_, bf16[1024,512]{1,0:T(8,128)(2,1)} %get-tuple-element.268.refs_1_, bf16[1024,512]{1,0:T(8,128)(2,1)} %get-tuple-element.269.refs_2_, ...), custom_call_target="tpu_custom_call" | custom-call | flops 21474836480 | bytes 9048064 | tf_op jit(solution)/shard_map/pallas_call | solution.py:81
  346.4 8.9 %shard_map.253 = (bf16[4,2,2,128,256]{4,3,2,1,0:T(8,128)(2,1)}, bf16[4,2,2,128,256]{4,3,2,1,0:T(8,128)(2,1)}, bf16[4,2,2,128,256]{4,3,2,1,0:T(8,128)(2,1)}, bf16[4,2,2,128,256]{4,3,2,1,0:T(8,128)(2,1)}) custom-call(bf16[1024,1024]{1,0:T(8,128)(2,1)} %get-tuple-element.283.refs_0_, bf16[1024,1024]{1,0:T(8,128)(2,1)} %get-tuple-element.341.refs_1_, ...), custom_call_target="tpu_custom_call" | custom-call | flops 4294967296 | bytes 12582912 | tf_op jit(solution)/shard_map/pallas_call | solution.py:81
  360.6 26.7 %shard_map.254 = (bf16[1024,512]{1,0:T(8,128)(2,1)}, bf16[1024,512]{1,0:T(8,128)(2,1)}, bf16[1024,512]{1,0:T(8,128)(2,1)}, f32[2,512]{1,0:T(2,128)}) custom-call(bf16[1024,512]{1,0:T(8,128)(2,1)} %get-tuple-element.288.refs_0_, bf16[1024,512]{1,0:T(8,128)(2,1)} %get-tuple-element.289.refs_1_, bf16[1024,512]{1,0:T(8,128)(2,1)} %get-tuple-element.290.refs_2_, ...), custom_call_target="tpu_custom_call" | custom-call | flops 21474836480 | bytes 9048064 | tf_op jit(solution)/shard_map/pallas_call | solution.py:81
  391.8 8.9 %shard_map.255 = (bf16[4,2,2,128,256]{4,3,2,1,0:T(8,128)(2,1)}, bf16[4,2,2,128,256]{4,3,2,1,0:T(8,128)(2,1)}, bf16[4,2,2,128,256]{4,3,2,1,0:T(8,128)(2,1)}, bf16[4,2,2,128,256]{4,3,2,1,0:T(8,128)(2,1)}) custom-call(bf16[1024,1024]{1,0:T(8,128)(2,1)} %get-tuple-element.283.refs_0_, bf16[1024,1024]{1,0:T(8,128)(2,1)} %get-tuple-element.341.refs_1_, ...), custom_call_target="tpu_custom_call" | custom-call | flops 4294967296 | bytes 12582912 | tf_op jit(solution)/shard_map/pallas_call | solution.py:81
  406.3 16.8 %shard_map.256 = (bf16[1024,1024]{1,0:T(8,128)(2,1)}, f32[8,1024]{1,0:T(8,128)}) custom-call(bf16[1024,512]{1,0:T(8,128)(2,1)} %get-tuple-element.345.refs_2_.refs_0_, bf16[1024,512]{1,0:T(8,128)(2,1)} %get-tuple-element.366.refs_2_.refs_1_, bf16[1024,512]{1,0:T(8,128)(2,1)} %get-tuple-element.346.refs_3_.refs_2_, ...), custom_call_target="tpu_custom_call" | custom-call | flops 6442450944 | bytes 25235456 | tf_op jit(solution)/shard_map/pallas_call | solution.py:81
  429.5 11.1 %shard_map.257 = (bf16[512,1536]{1,0:T(8,128)(2,1)}, bf16[512,1536]{1,0:T(8,128)(2,1)}, bf16[512,1536]{1,0:T(8,128)(2,1)}, bf16[512,1536]{1,0:T(8,128)(2,1)}) custom-call(s32[16]{0:T(128)} %reshape.1496.refs_0_, bf16[1024,1024]{1,0:T(8,128)(2,1)} %get-tuple-element.385.refs_1_, bf16[1024,768]{1,0:T(8,128)(2,1)} %refs_2_.1, ...), custom_call_target="tpu_custom_call" | custom-call | flops 3221225472 | bytes 9994240 | tf_op jit(solution)/shard_map/pallas_call | solution.py:81
  456.9 6.4 %shard_map.258.refs_7_ = f32[1024,1024]{1,0:T(8,128)} custom-call(s32[1]{0:T(128)} %bitcast.refs_0_, f32[1024,1024]{1,0:T(8,128)} %get-tuple-element.297.refs_7_.refs_1_, bf16[1024,1024]{1,0:T(8,128)(2,1)} %get-tuple-element.308.refs_8_.refs_2_, bf16[1024,1024]{1,0:T(8,128)(2,1)} %get-tuple-element.313.refs_8_.refs_3_, ...), custom_call_target="tpu_custom_call" | custom-call | bytes 14684160 | tf_op jit(solution)/shard_map/pallas_call | solution.py:81
  465.5 9.2 %shard_map.259 = f32[1024,768]{1,0:T(8,128)} custom-call(s32[16]{0:T(128)} %reshape.1496.refs_0_, bf16[1024,1024]{1,0:T(8,128)(2,1)} %get-tuple-element.385.refs_1_, f32[1024,8]{1,0:T(8,128)} %shard_map.239.refs_2_.refs_3_.refs_4_.refs_8_, bf16[4,128,1536]{2,1,0:T(8,128)(2,1)} %bitcast.178, bf16[4,128,1536]{2,1,0:T(8,128)(2,1)} %collective-permute-done.11.refs_11_.refs_4_, ...), custom_call_target="tpu_custom_call" | custom-call | flops 3221225472 | bytes 11829248 | tf_op jit(solution)/shard_map/pallas_call | solution.py:81
  474.8 3.7 collective-permute-done.60
  487.2 5.9 %collective-permute-done.67 = f32[1,1,1,1,1,512]{5,4,3,2,1,0:T(1,128)S(1)} collective-permute-done((f32[1,1,1,1,1,512]{5,4,3,2,1,0:T(1,128)S(1)}, f32[1,1,1,1,1,512]{5,4,3,2,1,0:T(1,128)S(1)}, u32[]{:S(2)}, u32[]{:S(2)}) %collective-permute-start.67) | collective-permute-done | bytes 2080 | tf_op jit(solution)/shard_map/ppermute | solution.py:743
  498.9 3.4 collective-permute-start.69
  507.1 9.3 %collective-permute-done.68 = bf16[32,3072]{1,0:T(8,128)(2,1)S(1)} collective-permute-done((bf16[32,3072]{1,0:T(8,128)(2,1)S(1)}, bf16[32,3072]{1,0:T(8,128)(2,1)S(1)}, u32[]{:S(2)}, u32[]{:S(2)}) %collective-permute-start.68) | collective-permute-done | bytes 196640 | tf_op jit(solution)/shard_map/ppermute | solution.py:782
  516.4 11.1 %collective-permute-done.69 = bf16[32,3072]{1,0:T(8,128)(2,1)S(1)} collective-permute-done((bf16[32,3072]{1,0:T(8,128)(2,1)S(1)}, bf16[32,3072]{1,0:T(8,128)(2,1)S(1)}, u32[]{:S(2)}, u32[]{:S(2)}) %collective-permute-start.69) | collective-permute-done | bytes 196640 | tf_op jit(solution)/shard_map/ppermute | solution.py:782
  (486 shorter events, 163.8 us)
Async XLA Ops:
  7.2 234.8 %all-gather.3.cloned.1.call-start = ((), (), s32[]{:S(2)}) async-start(), calls=%async_computation.6 | async-start | bytes 8650752 | tf_op jit(solution)/shard_map/all_gather | solution.py:980
  46.3 24.4 %collective-permute-start.7 = (bf16[2,1,128,1664]{3,2,1,0:T(8,128)(2,1)S(1)}, bf16[2,1,128,1664]{3,2,1,0:T(8,128)(2,1)S(1)}, u32[]{:S(2)}, u32[]{:S(2)}) collective-permute-start(bf16[2,1,128,1664]{3,2,1,0:T(8,128)(2,1)S(1)} %maximum_select_fusion.9), channel_id=1, source_target_pairs={{0,8},{4,12},{8,0},{12,4},{16,24},{20,28},{24,16},{28,20},{1,9},{5... | collective-permute-start | bytes 2555912 | tf_op jit(solution)/shard_map/ppermute | solution.py:743
  48.0 22.7 %collective-permute-start.6 = (bf16[1,2,128,1536]{3,2,1,0:T(8,128)(2,1)S(1)}, bf16[1,2,128,1536]{3,2,1,0:T(8,128)(2,1)S(1)}, u32[]{:S(2)}, u32[]{:S(2)}) collective-permute-start(bf16[1,2,128,1536]{3,2,1,0:T(8,128)(2,1)S(1)} %maximum_select_fusion.10), channel_id=1, source_target_pairs={{0,16},{4,20},{8,24},{12,28},{16,0},{20,4},{24,8},{28,12},{1,17},{... | collective-permute-start | bytes 2359304 | tf_op jit(solution)/shard_map/ppermute | solution.py:743
  49.1 21.5 %collective-permute-start.8 = (bf16[2,4,128,256]{3,2,1,0:T(8,128)(2,1)S(1)}, bf16[2,4,128,256]{3,2,1,0:T(8,128)(2,1)S(1)}, u32[]{:S(2)}, u32[]{:S(2)}) collective-permute-start(bf16[2,4,128,256]{3,2,1,0:T(8,128)(2,1)S(1)} %maximum_select_fusion.15), channel_id=1, source_target_pairs={{0,2},{1,3},{2,0},{3,1},{4,6},{5,7},{6,4},{7,5},{8,10},{9,11},{10,... | collective-permute-start | bytes 1572872 | tf_op jit(solution)/shard_map/ppermute | solution.py:743
  83.9 21.0 %collective-permute-start.16 = (bf16[2,1,1,3,128,256]{5,4,3,2,1,0:T(8,128)(2,1)S(1)}, bf16[2,1,1,3,128,256]{5,4,3,2,1,0:T(8,128)(2,1)S(1)}, u32[]{:S(2)}, u32[]{:S(2)}) collective-permute-start(bf16[2,1,1,3,128,256]{5,4,3,2,1,0:T(8,128)(2,1)S(1)} %maximum_select_fusion.21), channel_id=1, source_target_pairs={{0,8},{4,12},{8,0},{12,4},{16,24},{20,28},{24,16},{28,20},{1,9},{5... | collective-permute-start | bytes 1179656 | tf_op jit(solution)/shard_map/ppermute | solution.py:743
  116.1 20.5 %collective-permute-start.23 = (bf16[2,1,1,5,128,256]{5,4,3,2,1,0:T(8,128)(2,1)S(1)}, bf16[2,1,1,5,128,256]{5,4,3,2,1,0:T(8,128)(2,1)S(1)}, u32[]{:S(2)}, u32[]{:S(2)}) collective-permute-start(bf16[2,1,1,5,128,256]{5,4,3,2,1,0:T(8,128)(2,1)S(1)} %maximum_select_fusion.14), channel_id=1, source_target_pairs={{0,8},{4,12},{8,0},{12,4},{16,24},{20,28},{24,16},{28,20},{1,9},{5... | collective-permute-start | bytes 1966088 | tf_op jit(solution)/shard_map/ppermute | solution.py:743
  117.6 19.0 %collective-permute-start.22 = (bf16[1,2,1,5,128,256]{5,4,3,2,1,0:T(8,128)(2,1)S(1)}, bf16[1,2,1,5,128,256]{5,4,3,2,1,0:T(8,128)(2,1)S(1)}, u32[]{:S(2)}, u32[]{:S(2)}) collective-permute-start(bf16[1,2,1,5,128,256]{5,4,3,2,1,0:T(8,128)(2,1)S(1)} %maximum_select_fusion.13), channel_id=1, source_target_pairs={{0,16},{4,20},{8,24},{12,28},{16,0},{20,4},{24,8},{28,12},{1,17},{... | collective-permute-start | bytes 1966088 | tf_op jit(solution)/shard_map/ppermute | solution.py:743
  138.3 366.7 %reduce-scatter.6.cloned.1.call-start = ((), (), s32[]{:S(2)}) async-start(), calls=%async_computation.4 | async-start | bytes 1310720 | tf_op jit(solution)/shard_map/reduce_scatter | solution.py:848
  140.0 20.2 %collective-permute-start.26 = (bf16[4,1,5,128,256]{4,3,2,1,0:T(8,128)(2,1)S(1)}, bf16[4,1,5,128,256]{4,3,2,1,0:T(8,128)(2,1)S(1)}, u32[]{:S(2)}, u32[]{:S(2)}) collective-permute-start(bf16[4,1,5,128,256]{4,3,2,1,0:T(8,128)(2,1)S(1)} %bitcast.162), channel_id=1, source_target_pairs={{0,4},{4,0},{8,12},{12,8},{16,20},{20,16},{24,28},{28,24},{1,5},{5... | collective-permute-start | bytes 3932168 | tf_op jit(solution)/shard_map/ppermute | solution.py:743
  140.3 19.9 %collective-permute-start.25 = (bf16[4,1,5,128,256]{4,3,2,1,0:T(8,128)(2,1)S(1)}, bf16[4,1,5,128,256]{4,3,2,1,0:T(8,128)(2,1)S(1)}, u32[]{:S(2)}, u32[]{:S(2)}) collective-permute-start(bf16[4,1,5,128,256]{4,3,2,1,0:T(8,128)(2,1)S(1)} %bitcast.167), channel_id=1, source_target_pairs={{0,4},{4,0},{8,12},{12,8},{16,20},{20,16},{24,28},{28,24},{1,5},{5... | collective-permute-start | bytes 3932168 | tf_op jit(solution)/shard_map/ppermute | solution.py:743
  160.4 31.7 %collective-permute-start.30 = (bf16[2,1,4,128,512]{4,3,2,1,0:T(8,128)(2,1)S(1)}, bf16[2,1,4,128,512]{4,3,2,1,0:T(8,128)(2,1)S(1)}, u32[]{:S(2)}, u32[]{:S(2)}) collective-permute-start(bf16[2,1,4,128,512]{4,3,2,1,0:T(8,128)(2,1)S(1)} %maximum_select_fusion.8), channel_id=1, source_target_pairs={{0,8},{4,12},{8,0},{12,4},{16,24},{20,28},{24,16},{28,20},{1,9},{5... | collective-permute-start | bytes 3145736 | tf_op jit(solution)/shard_map/ppermute | solution.py:743
  161.8 30.3 %collective-permute-start.29 = (bf16[1,2,4,128,512]{4,3,2,1,0:T(8,128)(2,1)S(1)}, bf16[1,2,4,128,512]{4,3,2,1,0:T(8,128)(2,1)S(1)}, u32[]{:S(2)}, u32[]{:S(2)}) collective-permute-start(bf16[1,2,4,128,512]{4,3,2,1,0:T(8,128)(2,1)S(1)} %maximum_select_fusion.7), channel_id=1, source_target_pairs={{0,16},{4,20},{8,24},{12,28},{16,0},{20,4},{24,8},{28,12},{1,17},{... | collective-permute-start | bytes 3145736 | tf_op jit(solution)/shard_map/ppermute | solution.py:743
  256.1 31.8 %collective-permute-start.36 = (bf16[2,1,4,128,512]{4,3,2,1,0:T(8,128)(2,1)S(1)}, bf16[2,1,4,128,512]{4,3,2,1,0:T(8,128)(2,1)S(1)}, u32[]{:S(2)}, u32[]{:S(2)}) collective-permute-start(bf16[2,1,4,128,512]{4,3,2,1,0:T(8,128)(2,1)S(1)} %get-tuple-element.479.refs_10_), channel_id=1, source_target_pairs={{0,8},{4,12},{8,0},{12,4},{16,24},{20,28},{24,16},{28,20},{1,9},{5... | collective-permute-start | bytes 3145736 | tf_op jit(solution)/shard_map/ppermute | solution.py:743
  257.9 30.0 %collective-permute-start.35 = (bf16[1,2,4,128,512]{4,3,2,1,0:T(8,128)(2,1)}, bf16[1,2,4,128,512]{4,3,2,1,0:T(8,128)(2,1)S(1)}, u32[]{:S(2)}, u32[]{:S(2)}) collective-permute-start(bf16[1,2,4,128,512]{4,3,2,1,0:T(8,128)(2,1)} %get-tuple-element.481.refs_9_), channel_id=1, source_target_pairs={{0,16},{4,20},{8,24},{12,28},{16,0},{20,4},{24,8},{28,12},{1,17},{... | collective-permute-start | bytes 3145736 | tf_op jit(solution)/shard_map/ppermute | solution.py:743
  289.2 20.4 %collective-permute-start.39 = (bf16[4,4,128,512]{3,2,1,0:T(8,128)(2,1)}, bf16[4,4,128,512]{3,2,1,0:T(8,128)(2,1)S(1)}, u32[]{:S(2)}, u32[]{:S(2)}) collective-permute-start(bf16[4,4,128,512]{3,2,1,0:T(8,128)(2,1)} %get-tuple-element.332), channel_id=1, source_target_pairs={{0,4},{4,0},{8,12},{12,8},{16,20},{20,16},{24,28},{28,24},{1,5},{5... | collective-permute-start | bytes 6291464 | tf_op jit(solution)/shard_map/ppermute | solution.py:743
  289.2 20.4 %collective-permute-start.40 = (bf16[4,4,128,512]{3,2,1,0:T(8,128)(2,1)}, bf16[4,4,128,512]{3,2,1,0:T(8,128)(2,1)S(1)}, u32[]{:S(2)}, u32[]{:S(2)}) collective-permute-start(bf16[4,4,128,512]{3,2,1,0:T(8,128)(2,1)} %get-tuple-element.333), channel_id=1, source_target_pairs={{0,4},{4,0},{8,12},{12,8},{16,20},{20,16},{24,28},{28,24},{1,5},{5... | collective-permute-start | bytes 6291464 | tf_op jit(solution)/shard_map/ppermute | solution.py:743
  314.4 40.9 %collective-permute-start.42 = (bf16[2,1,4,128,512]{4,3,2,1,0:T(8,128)(2,1)}, bf16[2,1,4,128,512]{4,3,2,1,0:T(8,128)(2,1)S(1)}, u32[]{:S(2)}, u32[]{:S(2)}) collective-permute-start(bf16[2,1,4,128,512]{4,3,2,1,0:T(8,128)(2,1)} %get-tuple-element.475.refs_9_), channel_id=1, source_target_pairs={{0,8},{4,12},{8,0},{12,4},{16,24},{20,28},{24,16},{28,20},{1,9},{5... | collective-permute-start | bytes 3145736 | tf_op jit(solution)/shard_map/ppermute | solution.py:743
  316.2 39.1 %collective-permute-start.41 = (bf16[1,2,4,128,512]{4,3,2,1,0:T(8,128)(2,1)}, bf16[1,2,4,128,512]{4,3,2,1,0:T(8,128)(2,1)}, u32[]{:S(2)}, u32[]{:S(2)}) collective-permute-start(bf16[1,2,4,128,512]{4,3,2,1,0:T(8,128)(2,1)} %get-tuple-element.477.refs_8_), channel_id=1, source_target_pairs={{0,16},{4,20},{8,24},{12,28},{16,0},{20,4},{24,8},{28,12},{1,17},{... | collective-permute-start | bytes 3145736 | tf_op jit(solution)/shard_map/ppermute | solution.py:743
  355.4 31.9 %collective-permute-start.44 = (bf16[1,1,4,128,512]{4,3,2,1,0:T(8,128)(2,1)S(1)}, bf16[1,1,4,128,512]{4,3,2,1,0:T(8,128)(2,1)S(1)}, u32[]{:S(2)}, u32[]{:S(2)}) collective-permute-start(bf16[1,1,4,128,512]{4,3,2,1,0:T(8,128)(2,1)S(1)} %add_convert_fusion.24.refs_9_), channel_id=1, source_target_pairs={{0,16},{4,20},{8,24},{12,28},{16,0},{20,4},{24,8},{28,12},{1,17},{... | collective-permute-start | bytes 1572872 | tf_op jit(solution)/shard_map/ppermute | solution.py:743
  356.9 30.4 %collective-permute-start.45 = (bf16[4,2,2,128,256]{4,3,2,1,0:T(8,128)(2,1)}, bf16[4,2,2,128,256]{4,3,2,1,0:T(8,128)(2,1)S(1)}, u32[]{:S(2)}, u32[]{:S(2)}) collective-permute-start(bf16[4,2,2,128,256]{4,3,2,1,0:T(8,128)(2,1)} %get-tuple-element.357), channel_id=1, source_target_pairs={{0,4},{4,0},{8,12},{12,8},{16,20},{20,16},{24,28},{28,24},{1,5},{5... | collective-permute-start | bytes 3145736 | tf_op jit(solution)/shard_map/ppermute | solution.py:743
  356.9 30.4 %collective-permute-start.46 = (bf16[4,2,2,128,256]{4,3,2,1,0:T(8,128)(2,1)}, bf16[4,2,2,128,256]{4,3,2,1,0:T(8,128)(2,1)S(1)}, u32[]{:S(2)}, u32[]{:S(2)}) collective-permute-start(bf16[4,2,2,128,256]{4,3,2,1,0:T(8,128)(2,1)} %get-tuple-element.358), channel_id=1, source_target_pairs={{0,4},{4,0},{8,12},{12,8},{16,20},{20,16},{24,28},{28,24},{1,5},{5... | collective-permute-start | bytes 3145736 | tf_op jit(solution)/shard_map/ppermute | solution.py:743
  358.6 28.7 %collective-permute-start.43 = (bf16[1,1,4,128,512]{4,3,2,1,0:T(8,128)(2,1)S(1)}, bf16[1,1,4,128,512]{4,3,2,1,0:T(8,128)(2,1)S(1)}, u32[]{:S(2)}, u32[]{:S(2)}) collective-permute-start(bf16[1,1,4,128,512]{4,3,2,1,0:T(8,128)(2,1)S(1)} %add_convert_fusion.25.refs_8_), channel_id=1, source_target_pairs={{0,8},{4,12},{8,0},{12,4},{16,24},{20,28},{24,16},{28,20},{1,9},{5... | collective-permute-start | bytes 1572872 | tf_op jit(solution)/shard_map/ppermute | solution.py:743
  404.1 19.1 %collective-permute-start.51 = (bf16[4,2,2,128,256]{4,3,2,1,0:T(8,128)(2,1)}, bf16[4,2,2,128,256]{4,3,2,1,0:T(8,128)(2,1)S(1)}, u32[]{:S(2)}, u32[]{:S(2)}) collective-permute-start(bf16[4,2,2,128,256]{4,3,2,1,0:T(8,128)(2,1)} %get-tuple-element.378), channel_id=1, source_target_pairs={{0,4},{4,0},{8,12},{12,8},{16,20},{20,16},{24,28},{28,24},{1,5},{5... | collective-permute-start | bytes 3145736 | tf_op jit(solution)/shard_map/ppermute | solution.py:743
  404.1 19.1 %collective-permute-start.52 = (bf16[4,2,2,128,256]{4,3,2,1,0:T(8,128)(2,1)}, bf16[4,2,2,128,256]{4,3,2,1,0:T(8,128)(2,1)}, u32[]{:S(2)}, u32[]{:S(2)}) collective-permute-start(bf16[4,2,2,128,256]{4,3,2,1,0:T(8,128)(2,1)} %get-tuple-element.379), channel_id=1, source_target_pairs={{0,4},{4,0},{8,12},{12,8},{16,20},{20,16},{24,28},{28,24},{1,5},{5... | collective-permute-start | bytes 3145736 | tf_op jit(solution)/shard_map/ppermute | solution.py:743
  404.7 100.3 %reduce-scatter.8.cloned.1.call-start = ((), (), s32[]{:S(2)}) async-start(), calls=%async_computation.5 | async-start | bytes 1310720 | tf_op jit(solution)/shard_map/reduce_scatter | solution.py:848
  442.6 87.8 %reduce-scatter.4.cloned.1.call-start = ((), (), s32[]{:S(2)}) async-start(), calls=%async_computation.3 | async-start | bytes 1310720 | tf_op jit(solution)/shard_map/reduce_scatter | solution.py:848
  446.0 28.8 %collective-permute-start.61 = (bf16[1,1,2,2,128,256]{5,4,3,2,1,0:T(8,128)(2,1)S(1)}, bf16[1,1,2,2,128,256]{5,4,3,2,1,0:T(8,128)(2,1)S(1)}, u32[]{:S(2)}, u32[]{:S(2)}) collective-permute-start(bf16[1,1,2,2,128,256]{5,4,3,2,1,0:T(8,128)(2,1)S(1)} %add_convert_fusion.46.refs_7_), channel_id=1, source_target_pairs={{0,16},{4,20},{8,24},{12,28},{16,0},{20,4},{24,8},{28,12},{1,17},{... | collective-permute-start | bytes 786440 | tf_op jit(solution)/shard_map/ppermute | solution.py:743
  451.5 27.0 %collective-permute-start.59 = (bf16[1,2,4,32,1536]{4,3,2,1,0:T(8,128)(2,1)S(1)}, bf16[1,2,4,32,1536]{4,3,2,1,0:T(8,128)(2,1)}, u32[]{:S(2)}, u32[]{:S(2)}) collective-permute-start(bf16[1,2,4,32,1536]{4,3,2,1,0:T(8,128)(2,1)S(1)} %get-tuple-element.487.refs_9_), channel_id=1, source_target_pairs={{0,16},{4,20},{8,24},{12,28},{16,0},{20,4},{24,8},{28,12},{1,17},{... | collective-permute-start | bytes 2359304 | tf_op jit(solution)/shard_map/ppermute | solution.py:743
  453.5 25.0 %collective-permute-start.58 = (bf16[2,1,4,32,1536]{4,3,2,1,0:T(8,128)(2,1)S(1)}, bf16[2,1,4,32,1536]{4,3,2,1,0:T(8,128)(2,1)S(1)}, u32[]{:S(2)}, u32[]{:S(2)}) collective-permute-start(bf16[2,1,4,32,1536]{4,3,2,1,0:T(8,128)(2,1)S(1)} %get-tuple-element.489.refs_8_), channel_id=1, source_target_pairs={{0,8},{4,12},{8,0},{12,4},{16,24},{20,28},{24,16},{28,20},{1,9},{5... | collective-permute-start | bytes 2359304 | tf_op jit(solution)/shard_map/ppermute | solution.py:743
  456.2 22.3 %collective-permute-start.60 = (bf16[1,1,2,2,128,256]{5,4,3,2,1,0:T(8,128)(2,1)S(1)}, bf16[1,1,2,2,128,256]{5,4,3,2,1,0:T(8,128)(2,1)S(1)}, u32[]{:S(2)}, u32[]{:S(2)}) collective-permute-start(bf16[1,1,2,2,128,256]{5,4,3,2,1,0:T(8,128)(2,1)S(1)} %add_convert_fusion.47.refs_6_), channel_id=1, source_target_pairs={{0,8},{4,12},{8,0},{12,4},{16,24},{20,28},{24,16},{28,20},{1,9},{5... | collective-permute-start | bytes 786440 | tf_op jit(solution)/shard_map/ppermute | solution.py:743
  498.9 28.6 %collective-permute-start.69 = (bf16[32,3072]{1,0:T(8,128)(2,1)S(1)}, bf16[32,3072]{1,0:T(8,128)(2,1)S(1)}, u32[]{:S(2)}, u32[]{:S(2)}) collective-permute-start(bf16[32,3072]{1,0:T(8,128)(2,1)S(1)} %get-tuple-element.505), channel_id=1, source_target_pairs={{0,2},{1,3},{2,0},{3,1},{4,6},{5,7},{6,4},{7,5},{8,10},{9,11},{10,... | collective-permute-start | bytes 589832 | tf_op jit(solution)/shard_map/ppermute | solution.py:782
  502.3 27.2 %collective-permute-start.70 = (bf16[32,3072]{1,0:T(8,128)(2,1)S(1)}, bf16[32,3072]{1,0:T(8,128)(2,1)S(1)}, u32[]{:S(2)}, u32[]{:S(2)}) collective-permute-start(bf16[32,3072]{1,0:T(8,128)(2,1)S(1)} %get-tuple-element.506), channel_id=1, source_target_pairs={{0,3},{1,0},{2,1},{3,2},{4,7},{5,4},{6,5},{7,6},{8,11},{9,8},{10,9... | collective-permute-start | bytes 589832 | tf_op jit(solution)/shard_map/ppermute | solution.py:782
  (141 other events, 1060.9 us)
Sparse Core Ops, SparseCore 0:
  138.4 87.3 all-gather.2
  404.8 25.2 reduce-scatter.5
  442.7 26.8 reduce-scatter.7
  487.3 40.1 reduce-scatter.3
